TPU v7x, 256 devices: a whole 4x4x8 slice. The times are simulated.
256 devices in a mesh: ty: 16 (over y, z_hi), tx: 16 (over z_lo, x, core).
Axes of the slice: x: 4, y: 4, z: 8 (z_hi: 4, z_lo: 2; z = z_hi * 2 + z_lo), core: 2. Of those that a mesh axis runs over, the one named last changes fastest.
Arguments:
- specimen: float32 [2, 8192, 8192], P(None, 'ty', 'tx'), may hold values from -5 to 5
- illumination: float32 [2, 256, 256], replicated, may hold values from -6 to 6
- scan_offsets: int32 [16, 16, 2, 16], P('ty', 'tx'), may hold values from 0 to 7936, as said below
- slot_counts: int32 [16, 16], P('ty', 'tx'), may hold values from 1 to 16, as said below
- measured: float32 [16, 16, 16, 256, 256], P('ty', 'tx'), may hold values from 0.2 to 3
Outputs:
- new_specimen: float32 [2, 8192, 8192], P(None, 'ty', 'tx')
- new_illumination: float32 [2, 256, 256], replicated
Inputs may be any that keep to these rules, and one draw needn't show every extreme that they name: `scan_offsets`: the row of slot s of tile (a, b) lies in [a * 512 - 256 / 2, a * 512 + 512 - 256 / 2) and in [0, 7936]; the column lies in [b * 512 - 256 / 2, b * 512 + 512 - 256 / 2) and in [0, 7936]. Dead slots hold valid offsets too. Only the first slot_counts[a, b] slots of tile (a, b) are live. Some tile has all 16 slots live in every draw.
All inputs are finite; a program needn't handle non-finite values.
Results may differ from a plain program's by a relative error of at most 0.00016.
Values sent between devices are 32-bit elements; how exact they have to be, the bound alone decides.
A program may use at most 128 MiB of HBM per device.

v0:
```python
import math

import jax
import jax.numpy as jnp
from jax import lax
from jax.sharding import PartitionSpec as P

FLOOR = 0.5


def padded(cells, sides, width):
    for axis, dim in sides:
        count = lax.axis_size(axis)
        ends = count - 1
        head = lax.slice_in_dim(cells, 0, width, axis=dim)
        tail = lax.slice_in_dim(cells, cells.shape[dim] - width, cells.shape[dim], axis=dim)
        cells = jnp.concatenate(
            [
                lax.ppermute(tail, axis, [(i, (i + 1) % count) for i in range(ends)]),
                cells,
                lax.ppermute(head, axis, [((i + 1) % count, i) for i in range(ends)]),
            ],
            axis=dim,
        )
    return cells


def tables(length):
    counter = jnp.arange(length, dtype=jnp.int32)
    phase = counter[:, None] * counter[None, :] % length
    angle = phase.astype(jnp.float32) * (2.0 * math.pi / length)
    factor = 1.0 / math.sqrt(length)
    return (jnp.cos(angle) * factor, -jnp.sin(angle) * factor)


def matmul(left, right):
    return jnp.dot(left, right, precision=lax.Precision.HIGHEST, preferred_element_type=jnp.float32)


def transform(real_part, imag_part, cosines, sines):
    mid_real = matmul(real_part, cosines) - matmul(imag_part, sines)
    mid_imag = matmul(real_part, sines) + matmul(imag_part, cosines)
    out_real = matmul(cosines, mid_real) - matmul(sines, mid_imag)
    out_imag = matmul(sines, mid_real) + matmul(cosines, mid_imag)
    return (out_real, out_imag)


def conj_times(left, right):
    return jnp.stack(
        [left[0] * right[0] + left[1] * right[1], left[0] * right[1] - left[1] * right[0]]
    )


def exit_update(patch_field, modulus, illumination, cosines, sines):
    wave_real = illumination[0] * patch_field[0] - illumination[1] * patch_field[1]
    wave_imag = illumination[0] * patch_field[1] + illumination[1] * patch_field[0]
    far_real, far_imag = transform(wave_real, wave_imag, cosines, sines)
    magnitude = jnp.sqrt(far_real * far_real + far_imag * far_imag)
    factor = modulus / jnp.maximum(magnitude, FLOOR)
    back_real, back_imag = transform(far_real * factor, far_imag * factor, cosines, -sines)
    return jnp.stack([back_real - wave_real, back_imag - wave_imag])


def shards(specimen, illumination, scan_offsets, slot_counts, measured):
    tile_rows = specimen.shape[1]
    tile_cols = specimen.shape[2]
    window = illumination.shape[1]
    margin = window // 2
    slot_count = measured.shape[2]
    cosines, sines = tables(window)
    anchor_row = lax.axis_index("ty") * tile_rows - margin
    anchor_col = lax.axis_index("tx") * tile_cols - margin
    local_row = scan_offsets[0, 0, 0] - anchor_row
    local_col = scan_offsets[0, 0, 1] - anchor_col
    moduli = measured[0, 0]
    live_count = slot_counts[0, 0]
    extended = padded(specimen, (("ty", 1), ("tx", 2)), margin)

    def extract(slot_number):
        corner_start = (jnp.int32(0), local_row[slot_number], local_col[slot_number])
        return lax.dynamic_slice(extended, corner_start, (2, window, window))

    def deposit(gradient, slot_number, correction):
        corner_start = (jnp.int32(0), local_row[slot_number], local_col[slot_number])
        existing = lax.dynamic_slice(gradient, corner_start, (2, window, window))
        return lax.dynamic_update_slice(
            gradient, existing + conj_times(illumination, correction), corner_start
        )

    def own_step(slot_number, carry):
        gradient, probe_term = carry
        patch_field = extract(slot_number)
        correction = exit_update(patch_field, moduli[slot_number], illumination, cosines, sines)
        return (
            deposit(gradient, slot_number, correction),
            probe_term + conj_times(patch_field, correction),
        )

    empty_gradient = jnp.zeros_like(extended)
    empty_probe = jnp.zeros_like(illumination)
    gradient, probe_term = lax.fori_loop(0, live_count, own_step, (empty_gradient, empty_probe))
    folded = padded(gradient, (("ty", 1), ("tx", 2)), margin)
    row_folded = folded[:, 2 * margin : 2 * margin + tile_rows, :]
    row_folded = row_folded.at[:, :margin, :].add(folded[:, :margin, :])
    row_folded = row_folded.at[:, tile_rows - margin :, :].add(
        folded[:, tile_rows + 3 * margin :, :]
    )
    update_field = row_folded[:, :, 2 * margin : 2 * margin + tile_cols]
    update_field = update_field.at[:, :, :margin].add(row_folded[:, :, :margin])
    update_field = update_field.at[:, :, tile_cols - margin :].add(
        row_folded[:, :, tile_cols + 3 * margin :]
    )
    probe_power = (
        jnp.mean(illumination[0] * illumination[0] + illumination[1] * illumination[1]) + 1e-05
    )
    new_specimen = specimen + update_field / probe_power
    summed_term = lax.psum(probe_term, ("ty", "tx"))
    total_slots = slot_count * lax.axis_size("ty") * lax.axis_size("tx")
    new_illumination = illumination + summed_term / math.sqrt(total_slots)
    return (new_specimen, new_illumination)


def solution(mesh):
    in_specs = (
        P(None, "ty", "tx"),
        P(),
        P("ty", "tx", None, None),
        P("ty", "tx"),
        P("ty", "tx", None, None, None),
    )
    out_specs = (P(None, "ty", "tx"), P())
    return jax.shard_map(shards, mesh=mesh, in_specs=in_specs, out_specs=out_specs, check_vma=False)
```

profile of v0, /device:TPU:1, one launch (start us, length us, event | category | flops | bytes accessed | tf_op | source)
XLA Modules:
  0.0 1032.7 jit_solution(5685249720574959318)
XLA Ops:
  7.2 1.9 copy.7
  9.2 5.8 collective-permute-start
  16.3 12.6 %collective-permute-done = f32[2,128,512]{1,2,0:T(8,128)S(1)} collective-permute-done((f32[2,128,512]{1,2,0:T(8,128)S(1)}, f32[2,128,512]{1,2,0:T(8,128)S(1)}, u32[]{:S(2)}, u32[]{:S(2)}) %collective-permute-start) | collective-permute-done | bytes 524320 | tf_op jit(solution)/shard_map/ppermute | solution.py:19
  28.9 15.3 %collective-permute-done.1 = f32[2,128,512]{1,2,0:T(8,128)S(1)} collective-permute-done((f32[2,128,512]{1,2,0:T(8,128)S(1)}, f32[2,128,512]{1,2,0:T(8,128)S(1)}, u32[]{:S(2)}, u32[]{:S(2)}) %collective-permute-start.1) | collective-permute-done | bytes 524320 | tf_op jit(solution)/shard_map/ppermute | solution.py:21
  45.5 4.1 collective-permute-start.2
  49.6 1.9 collective-permute-start.3
  51.6 5.4 copy.10
  57.2 1.6 collective-permute-done.2
  58.9 4.4 collective-permute-done.3
  63.3 3.6 pad_maximum_fusion.1
  66.8 2.5 broadcast_in_dim.8.clone
  69.4 376.9 %while.19 = (s32[]{:T(128)}, f32[2,768,768]{2,1,0:T(8,128)}, f32[2,256,256]{1,2,0:T(8,128)S(1)}, s32[]{:T(128)}, s32[16]{0:T(128)S(1)}, /*index=5*/s32[16]{0:T(1...) while((s32[]{:T(128)}, f32[2,768,768]{2,1,0:T(8,128)}, ...), condition=%wide.region_1.2_spmd.clone.clone, body=%wide.region_0.1_spmd.clone.clone.sunk | while | flops 3240558592 | bytes 22806840 | solution.py:101
  84.0 1.5 fusion.199
  85.5 1.5 fusion.200
  87.0 2.5 fusion.201
  94.0 1.5 convolution_subtract_fusion.7
  99.9 2.7 add_bitcast_fusion.2
  104.6 6.8 dynamic_update_slice.7
  125.9 1.5 fusion.199
  128.8 2.5 fusion.201
  135.8 1.5 convolution_subtract_fusion.7
  141.7 2.7 add_bitcast_fusion.2
  146.5 6.7 dynamic_update_slice.7
  167.6 1.5 fusion.199
  169.1 1.5 fusion.200
  170.6 2.5 fusion.201
  177.6 1.5 convolution_subtract_fusion.7
  183.5 2.7 add_bitcast_fusion.2
  188.2 6.8 dynamic_update_slice.7
  209.5 1.5 fusion.199
  212.4 2.5 fusion.201
  225.3 2.7 add_bitcast_fusion.2
  230.1 6.5 dynamic_update_slice.7
  251.1 1.5 fusion.199
  254.0 2.5 fusion.201
  266.9 2.7 add_bitcast_fusion.2
  271.7 6.8 dynamic_update_slice.7
  292.9 1.5 fusion.199
  294.4 1.5 fusion.200
  295.9 2.5 fusion.201
  302.9 1.5 convolution_subtract_fusion.7
  308.8 2.7 add_bitcast_fusion.2
  313.5 6.7 dynamic_update_slice.7
  334.7 1.5 fusion.199
  337.6 2.5 fusion.201
  350.5 2.7 add_bitcast_fusion.2
  355.3 6.8 dynamic_update_slice.7
  376.5 1.5 fusion.199
  379.5 2.5 fusion.201
  392.4 2.7 add_bitcast_fusion.2
  397.2 6.5 dynamic_update_slice.7
  418.2 1.5 fusion.199
  421.1 2.5 fusion.201
  434.0 2.7 add_bitcast_fusion.2
  438.8 6.7 dynamic_update_slice.7
  446.3 1.6 fusion.123
  450.8 22.3 %collective-permute-done.4 = f32[2,128,768]{2,1,0:T(8,128)S(1)} collective-permute-done((f32[2,128,768]{2,1,0:T(8,128)S(1)}, f32[2,128,768]{2,1,0:T(8,128)S(1)}, u32[]{:S(2)}, u32[]{:S(2)}) %collective-permute-start.4) | collective-permute-done | bytes 786464 | tf_op jit(solution)/shard_map/ppermute | solution.py:19
  473.5 2.6 copy-done
  477.6 1.9 collective-permute-start.6
  479.5 2.5 collective-permute-start.7
  484.3 531.5 %all-reduce.2.cloned.1.call-done = f32[2,256,256]{2,1,0:T(8,128)} async-done(((f32[2,256,256]{2,1,0:T(8,128)}), f32[2,256,256]{2,1,0:T(8,128)}) %all-reduce.2.cloned.1.call-update) | async-done | bytes 524304 | tf_op jit(solution)/shard_map/psum | solution.py:117
  1015.8 2.1 multiply_add_fusion
  1017.9 3.5 pad_maximum_fusion
  1024.0 1.8 divide_add_fusion
  (218 shorter events, 214.8 us)
Async XLA Ops:
  7.2 1008.6 %all-reduce.2.cloned.1.call-start = ((), (), s32[]{:S(2)}) async-start(), calls=%async_computation | async-start | bytes 1048576 | tf_op jit(solution)/shard_map/psum | solution.py:117
  9.2 19.7 %collective-permute-start = (f32[2,128,512]{1,2,0:T(8,128)S(1)}, f32[2,128,512]{1,2,0:T(8,128)S(1)}, u32[]{:S(2)}, u32[]{:S(2)}) collective-permute-start(f32[2,128,512]{1,2,0:T(8,128)S(1)} %get-tuple-element.313), channel_id=1, source_target_pairs={{0,16},{16,32},{32,48},{48,64},{64,80},{80,96},{96,112},{112,128},... | collective-permute-start | bytes 1572872 | tf_op jit(solution)/shard_map/ppermute | solution.py:19
  15.0 29.2 %collective-permute-start.1 = (f32[2,128,512]{1,2,0:T(8,128)S(1)}, f32[2,128,512]{1,2,0:T(8,128)S(1)}, u32[]{:S(2)}, u32[]{:S(2)}) collective-permute-start(f32[2,128,512]{1,2,0:T(8,128)S(1)} %get-tuple-element.314), channel_id=1, source_target_pairs={{16,0},{32,16},{48,32},{64,48},{80,64},{96,80},{112,96},{128,112},... | collective-permute-start | bytes 1572872 | tf_op jit(solution)/shard_map/ppermute | solution.py:21
  28.9 15.3 %copy-start.5 = (f32[2,128,512]{1,2,0:T(8,128)}, f32[2,128,512]{1,2,0:T(8,128)S(1)}, u32[]{:S(2)}) copy-start(f32[2,128,512]{1,2,0:T(8,128)S(1)} %collective-permute-done) | copy-start | bytes 1572868
  44.2 1.3 copy-start.6
  45.5 11.5 %copy-start.3 = (f32[2,256,256]{2,1,0:T(8,128)S(1)}, f32[2,256,256]{2,1,0:T(8,128)}, u32[]{:S(2)}) copy-start(f32[2,256,256]{2,1,0:T(8,128)} %param.16) | copy-start | bytes 1572868
  45.5 13.3 %collective-permute-start.2 = (f32[2,768,128]{1,2,0:T(8,128)}, f32[2,768,128]{1,2,0:T(8,128)}, u32[]{:S(2)}, u32[]{:S(2)}) collective-permute-start(f32[2,768,128]{1,2,0:T(8,128)} %get-tuple-element.311), channel_id=1, source_target_pairs={{0,1},{1,2},{2,3},{3,4},{4,5},{5,6},{6,7},{7,8},{8,9},{9,10},{10,1... | collective-permute-start | bytes 2359304 | tf_op jit(solution)/shard_map/ppermute | solution.py:19
  49.6 13.6 %collective-permute-start.3 = (f32[2,768,128]{1,2,0:T(8,128)}, f32[2,768,128]{1,2,0:T(8,128)}, u32[]{:S(2)}, u32[]{:S(2)}) collective-permute-start(f32[2,768,128]{1,2,0:T(8,128)} %get-tuple-element.312), channel_id=1, source_target_pairs={{1,0},{2,1},{3,2},{4,3},{5,4},{6,5},{7,6},{8,7},{9,8},{10,9},{11,1... | collective-permute-start | bytes 2359304 | tf_op jit(solution)/shard_map/ppermute | solution.py:21
  51.6 5.6 copy-start.7
  446.3 26.8 %copy-start.1 = (f32[2,768,768]{2,1,0:T(8,128)S(1)}, f32[2,768,768]{2,1,0:T(8,128)}, u32[]{:S(2)}) copy-start(f32[2,768,768]{2,1,0:T(8,128)} %get-tuple-element.198) | copy-start | bytes 14155780
  448.0 25.0 %collective-permute-start.4 = (f32[2,128,768]{2,1,0:T(8,128)S(1)}, f32[2,128,768]{2,1,0:T(8,128)S(1)}, u32[]{:S(2)}, u32[]{:S(2)}) collective-permute-start(f32[2,128,768]{2,1,0:T(8,128)S(1)} %get-tuple-element.310), channel_id=1, source_target_pairs={{0,16},{16,32},{32,48},{48,64},{64,80},{80,96},{96,112},{112,128},... | collective-permute-start | bytes 2359304 | tf_op jit(solution)/shard_map/ppermute | solution.py:19
  449.5 24.0 %collective-permute-start.5 = (f32[2,128,768]{2,1,0:T(8,128)S(1)}, f32[2,128,768]{2,1,0:T(8,128)S(1)}, u32[]{:S(2)}, u32[]{:S(2)}) collective-permute-start(f32[2,128,768]{2,1,0:T(8,128)S(1)} %get-tuple-element.309), channel_id=1, source_target_pairs={{16,0},{32,16},{48,32},{64,48},{80,64},{96,80},{112,96},{128,112},... | collective-permute-start | bytes 2359304 | tf_op jit(solution)/shard_map/ppermute | solution.py:21
  473.4 9.6 copy-start.4
  473.5 2.6 copy-start
  477.6 540.3 %collective-permute-start.6 = (f32[2,1024,128]{2,1,0:T(8,128)}, f32[2,1024,128]{2,1,0:T(8,128)S(1)}, u32[]{:S(2)}, u32[]{:S(2)}) collective-permute-start(f32[2,1024,128]{2,1,0:T(8,128)} %get-tuple-element.307), channel_id=1, source_target_pairs={{0,1},{1,2},{2,3},{3,4},{4,5},{5,6},{6,7},{7,8},{8,9},{9,10},{10,1... | collective-permute-start | bytes 3145736 | tf_op jit(solution)/shard_map/ppermute | solution.py:19
  479.5 538.3 %collective-permute-start.7 = (f32[2,1024,128]{2,1,0:T(8,128)}, f32[2,1024,128]{2,1,0:T(8,128)S(1)}, u32[]{:S(2)}, u32[]{:S(2)}) collective-permute-start(f32[2,1024,128]{2,1,0:T(8,128)} %get-tuple-element.308), channel_id=1, source_target_pairs={{1,0},{2,1},{3,2},{4,3},{5,4},{6,5},{7,6},{8,7},{9,8},{10,9},{11,1... | collective-permute-start | bytes 3145736 | tf_op jit(solution)/shard_map/ppermute | solution.py:21
  1015.8 6.2 slice-start
  1017.8 4.1 slice-start.1
  1022.4 1.6 copy-start.2
Sparse Core Ops, SparseCore 0:
  483.1 532.6 all-reduce.1
where the time goes:
time: 1040 us; the launch traced here: 1030 us
  waiting for transfers between devices  588 us (57%)
  matrix products  232 us (22%)
  local copies, waits for them, and re-layouts  106 us (10%)
  loops' own time  43.4 us (4%)
  other arithmetic  28.1 us (3%)
  starting transfers between devices  20.2 us (2%)
  between operations  14.9 us (1%)
    psum x1, waiting for transfers between devices, shards(): summed_term = lax.psum(probe_term, ('ty', 'tx'))  532 us
    dot_general x144, matrix products, matmul(): jnp.dot(left, right, precision=lax.Precision.HIGHEST, preferred_element_t...  232 us
    dynamic_update_slice x18, local copies, waits for them, and re-layouts, deposit(): lax.dynamic_update_slice(gradient, existing + conj_times(illumination, co...  61.9 us
    another operation x1, loops' own time, shards(): lax.fori_loop(0, live_count, own_step, (empty_gradient, empty_probe))  43.4 us
    ppermute x4, waiting for transfers between devices, padded(): lax.ppermute(tail, axis, [(i, (i + 1) % count) for i in range(ends)])  36.5 us
  transfers between devices with their start and end apart: 9, of which 6 were waited for; matrix products, arithmetic and copies ran while one was open for 1% of the time, Pallas kernels for 0%

commit v1 on v0

v1 whole, which is shorter than its diff:
```python
import math

import numpy as np
import jax, jax.numpy as jnp
from jax import lax
from jax.experimental import pallas as pl
from jax.experimental.pallas import tpu as pltpu
import ml_dtypes
from jax.sharding import PartitionSpec as P

F32=jnp.float32; BF=jnp.bfloat16

def consts():
    k=np.arange(128)
    ang=2*np.pi*np.outer(k,k)%(2*np.pi*128)/128
    ang=2*np.pi*((np.outer(k,k))%128)/128
    C=np.cos(ang)/16; S=np.sin(ang)/16
    A=np.block([[C,-S],[S,C]]); B=A.T.copy()
    def split(x):
        x=x.astype(np.float32)
        h=x.astype(ml_dtypes.bfloat16); l=(x-h.astype(np.float32)).astype(ml_dtypes.bfloat16)
        return h,l
    ah,al=split(A); bh,bl=split(B)
    mats=np.stack([ah,al,bh,bl])
    t=2*np.pi*np.arange(128)/256
    c=np.cos(t).astype(np.float32); s=np.sin(t).astype(np.float32)
    twr=np.stack([np.broadcast_to(c[:,None],(128,128)),np.broadcast_to(s[:,None],(128,128))])
    twl=np.stack([np.broadcast_to(c[None],(16,128)),np.broadcast_to(s[None],(16,128))])
    k=np.arange(256)
    perm=np.zeros((256,256));
    perm[k, (k%2)*128+k//2]=1
    return mats, twr.astype(np.float32).copy(), twl.astype(np.float32).copy(), perm.astype(ml_dtypes.bfloat16)

def split(x):
    h=x.astype(BF)
    return h,(x-h.astype(F32)).astype(BF)

def dot(a,b): return jnp.dot(a,b,preferred_element_type=F32)

RC=16
def wkernel(offs, cnt, ext, ill, mats, twr, twl, perm, meas, grad, pterm,
            mbuf, patch, wave, hi, lo, mid, msem):
    n=cnt[0]
    def cp(s,t): return pltpu.make_async_copy(meas.at[s,:,pl.ds(128*t,128)], mbuf.at[s,t], msem.at[s,t])
    @pl.loop(0,n)
    def _(s):
        cp(s,0).start(); cp(s,1).start()
    @pl.loop(0,96)
    def _(i):
        for p in range(2):
            for t in range(6):
                grad[p,t,pl.ds(pl.multiple_of(8*i,8),8),:]=jnp.zeros((8,128),F32)
    pterm[...]=jnp.zeros_like(pterm)
    lane=lax.broadcasted_iota(jnp.int32,(RC,128),1)
    @pl.loop(0,n)
    def _(s):
        r=offs[0,s]; c=offs[1,s]
        ct=c//128; sh=c%128
        ush=(128-sh)%128
        lmask=lane<128-sh
        for j in range(128//RC):
            half=[]
            for h in range(2):
                row=h*128+j*RC
                rr=pl.ds(row,RC)
                x=[[pltpu.roll(ext[p,ct+t,pl.ds(r+row,RC),:],ush,1) for t in range(3)] for p in range(2)]
                pt=[[jnp.where(lmask,x[p][t],x[p][t+1]) for t in range(2)] for p in range(2)]
                ws=[]
                for t in range(2):
                    ls=pl.ds(128*t,128)
                    pr,pi=ill[0,rr,ls],ill[1,rr,ls]
                    a,b=pt[0][t],pt[1][t]
                    patch[0,rr,ls]=a; patch[1,rr,ls]=b
                    wr=pr*a-pi*b; wi=pr*b+pi*a
                    wave[0,rr,ls]=wr; wave[1,rr,ls]=wi
                    ws.append((wr,wi))
                half.append(ws)
            tc=twr[0,pl.ds(j*RC,RC),:]; ts=twr[1,pl.ds(j*RC,RC),:]
            for t in range(2):
                ls=pl.ds(128*t,128)
                (ar,ai),(br,bi)=half[0][t],half[1][t]
                er,ei=ar+br,ai+bi
                dr,di=ar-br,ai-bi
                vr=dr*tc+di*ts; vi=di*tc-dr*ts
                for q,(xr,xi) in enumerate(((er,ei),(vr,vi))):
                    for z,val in enumerate((xr,xi)):
                        hh,ll=split(val)
                        rs=pl.ds(z*128+j*RC,RC)
                        hi[q,rs,ls]=hh; lo[q,rs,ls]=ll
        bh=mats[2]; bl=mats[3]
        for q in range(2):
            mid[q]=dot(bh,hi[q])+dot(bh,lo[q])+dot(bl,hi[q])
        lc=twl[0]; lsn=twl[1]
        for q in range(2):
            for j in range(128//RC):
                ar=mid[q,pl.ds(j*RC,RC),pl.ds(0,128)]; br=mid[q,pl.ds(j*RC,RC),pl.ds(128,128)]
                ai=mid[q,pl.ds(128+j*RC,RC),pl.ds(0,128)]; bi=mid[q,pl.ds(128+j*RC,RC),pl.ds(128,128)]
                er,ei=ar+br,ai+bi
                dr,di=ar-br,ai-bi
                vr=dr*lc+di*lsn; vi=di*lc-dr*lsn
                rs=pl.ds(q*128+j*RC,RC)
                for e,(xr,xi) in enumerate(((er,ei),(vr,vi))):
                    for z,val in enumerate((xr,xi)):
                        hh,ll=split(val)
                        hi[e,rs,pl.ds(128*z,128)]=hh; lo[e,rs,pl.ds(128*z,128)]=ll
        ah=mats[0]; al=mats[1]
        for e in range(2):
            mid[e]=dot(hi[e],ah)+dot(lo[e],ah)+dot(hi[e],al)
        cp(s,0).wait(); cp(s,1).wait()
        pm=perm[...]
        for q in range(2):
            mv=jnp.concatenate([mbuf[s,t,pl.ds(q,128,stride=2),:] for t in range(2)],axis=1)
            mh,ml=split(mv)
            mp=dot(mh,pm)+dot(ml,pm)
            for e in range(2):
                for j in range(128//RC):
                    rs=pl.ds(q*128+j*RC,RC)
                    fr=mid[e,rs,pl.ds(0,128)]; fi=mid[e,rs,pl.ds(128,128)]
                    m=mp[j*RC:(j+1)*RC,e*128:(e+1)*128]
                    f=m*lax.rsqrt(jnp.maximum(fr*fr+fi*fi,0.25))
                    for z,val in enumerate((fr*f,fi*f)):
                        hh,ll=split(val)
                        hi[e,rs,pl.ds(128*z,128)]=hh; lo[e,rs,pl.ds(128*z,128)]=ll
        for e in range(2):
            mid[e]=dot(hi[e],bh)+dot(lo[e],bh)+dot(hi[e],bl)
        for q in range(2):
            for j in range(128//RC):
                rs=pl.ds(q*128+j*RC,RC)
                er=mid[0,rs,pl.ds(0,128)]; ei=mid[0,rs,pl.ds(128,128)]
                orr=mid[1,rs,pl.ds(0,128)]; oi=mid[1,rs,pl.ds(128,128)]
                vr=orr*lc-oi*lsn; vi=oi*lc+orr*lsn
                for t,(xr,xi) in enumerate(((er+vr,ei+vi),(er-vr,ei-vi))):
                    for z,val in enumerate((xr,xi)):
                        hh,ll=split(val)
                        hi[q,pl.ds(z*128+j*RC,RC),pl.ds(128*t,128)]=hh
                        lo[q,pl.ds(z*128+j*RC,RC),pl.ds(128*t,128)]=ll
        for q in range(2):
            mid[q]=dot(ah,hi[q])+dot(ah,lo[q])+dot(al,hi[q])
        for j in range(128//RC):
            tc=twr[0,pl.ds(j*RC,RC),:]; ts=twr[1,pl.ds(j*RC,RC),:]
            g=[[[None]*2 for _ in range(2)] for _ in range(2)]
            for t in range(2):
                ls=pl.ds(128*t,128)
                er=mid[0,pl.ds(j*RC,RC),ls]; ei=mid[0,pl.ds(128+j*RC,RC),ls]
                orr=mid[1,pl.ds(j*RC,RC),ls]; oi=mid[1,pl.ds(128+j*RC,RC),ls]
                vr=orr*tc-oi*ts; vi=oi*tc+orr*ts
                for h,(xr,xi) in enumerate(((er+vr,ei+vi),(er-vr,ei-vi))):
                    rr=pl.ds(h*128+j*RC,RC)
                    cr=xr-wave[0,rr,ls]; ci=xi-wave[1,rr,ls]
                    a,b=patch[0,rr,ls],patch[1,rr,ls]
                    pterm[0,rr,ls]+=a*cr+b*ci
                    pterm[1,rr,ls]+=a*ci-b*cr
                    pr,pi=ill[0,rr,ls],ill[1,rr,ls]
                    g[h][0][t]=pr*cr+pi*ci
                    g[h][1][t]=pr*ci-pi*cr
            for h in range(2):
                for z in range(2):
                    rg=[pltpu.roll(g[h][z][t],sh,1) for t in range(2)]
                    low=lane<sh
                    rows=pl.ds(r+h*128+j*RC,RC)
                    grad[z,ct,rows,:]+=jnp.where(low,0.0,rg[0])
                    grad[z,ct+1,rows,:]+=jnp.where(low,rg[0],rg[1])
                    grad[z,ct+2,rows,:]+=jnp.where(low,rg[1],0.0)

def windows(offs,cnt,ext,ill,meas):
    mats,twr,twl,perm=consts()
    V=pl.BlockSpec(memory_space=pltpu.VMEM); Sm=pl.BlockSpec(memory_space=pltpu.SMEM)
    return pl.pallas_call(wkernel,
        out_shape=(jax.ShapeDtypeStruct((2,6,768,128),F32),jax.ShapeDtypeStruct((2,256,256),F32)),
        in_specs=[Sm,Sm,V,V,V,V,V,V,pl.BlockSpec(memory_space=pl.ANY)],
        out_specs=(V,V),
        scratch_shapes=[pltpu.VMEM((16,2,256,128),F32),pltpu.VMEM((2,256,256),F32),pltpu.VMEM((2,256,256),F32),
            pltpu.VMEM((2,256,256),BF),pltpu.VMEM((2,256,256),BF),pltpu.VMEM((2,256,256),F32),pltpu.SemaphoreType.DMA((16,2))],
        compiler_params=pltpu.CompilerParams(vmem_limit_bytes=48*2**20),
    )(offs,cnt,ext,ill,jnp.asarray(mats),jnp.asarray(twr),jnp.asarray(twl),jnp.asarray(perm),meas)


def padded(cells, sides, width):
    for axis, dim in sides:
        count = lax.axis_size(axis)
        ends = count - 1
        head = lax.slice_in_dim(cells, 0, width, axis=dim)
        tail = lax.slice_in_dim(cells, cells.shape[dim] - width, cells.shape[dim], axis=dim)
        cells = jnp.concatenate(
            [
                lax.ppermute(tail, axis, [(i, (i + 1) % count) for i in range(ends)]),
                cells,
                lax.ppermute(head, axis, [((i + 1) % count, i) for i in range(ends)]),
            ],
            axis=dim,
        )
    return cells


def shards(specimen, illumination, scan_offsets, slot_counts, measured):
    tile_rows = specimen.shape[1]
    tile_cols = specimen.shape[2]
    margin = 128
    slot_count = measured.shape[2]
    anchor = jnp.stack([lax.axis_index("ty") * tile_rows, lax.axis_index("tx") * tile_cols]) - margin
    local = scan_offsets[0, 0] - anchor[:, None]
    extended = padded(specimen, (("ty", 1), ("tx", 2)), margin)
    ext = extended.reshape(2, 768, 6, 128).transpose(0, 2, 1, 3)
    grad, probe_term = windows(local, slot_counts[0], ext, illumination, measured[0, 0])
    gradient = grad.transpose(0, 2, 1, 3).reshape(2, 768, 768)
    folded = padded(gradient, (("ty", 1), ("tx", 2)), margin)
    row_folded = folded[:, 2 * margin : 2 * margin + tile_rows, :]
    row_folded = row_folded.at[:, :margin, :].add(folded[:, :margin, :])
    row_folded = row_folded.at[:, tile_rows - margin :, :].add(
        folded[:, tile_rows + 3 * margin :, :]
    )
    update_field = row_folded[:, :, 2 * margin : 2 * margin + tile_cols]
    update_field = update_field.at[:, :, :margin].add(row_folded[:, :, :margin])
    update_field = update_field.at[:, :, tile_cols - margin :].add(
        row_folded[:, :, tile_cols + 3 * margin :]
    )
    probe_power = (
        jnp.mean(illumination[0] * illumination[0] + illumination[1] * illumination[1]) + 1e-05
    )
    new_specimen = specimen + update_field / probe_power
    summed_term = lax.psum(probe_term, ("ty", "tx"))
    total_slots = slot_count * lax.axis_size("ty") * lax.axis_size("tx")
    new_illumination = illumination + summed_term / math.sqrt(total_slots)
    return (new_specimen, new_illumination)

def solution(mesh):
    in_specs = (
        P(None, "ty", "tx"),
        P(),
        P("ty", "tx", None, None),
        P("ty", "tx"),
        P("ty", "tx", None, None, None),
    )
    out_specs = (P(None, "ty", "tx"), P())
    return jax.shard_map(shards, mesh=mesh, in_specs=in_specs, out_specs=out_specs, check_vma=False)
```

time: 1040 us -> 432 us (0.42)
  waiting for transfers between devices: 588 us -> 330 us
  matrix products: 232 us -> 0 us
  local copies, waits for them, and re-layouts: 106 us -> 22.2 us
  loops' own time: 43.4 us -> 0 us
  Pallas kernels: 0 us -> 18 us
    psum x1, waiting for transfers between devices: 532 us -> 272 us  [shards(): summed_term = lax.psum(probe_term, ('ty', 'tx'))]
    dot_general x144 -> x0, matrix products: 232 us -> none  [matmul(): jnp.dot(left, right, precision=lax.Precision.HIGHEST, preferred_element_t...]
    dynamic_update_slice x18 -> x0, local copies, waits for them, and re-layouts: 61.9 us -> none  [deposit(): lax.dynamic_update_slice(gradient, existing + conj_times(illumination, co...]
    another operation x1 -> x0, loops' own time: 43.4 us -> none  [shards(): lax.fori_loop(0, live_count, own_step, (empty_gradient, empty_probe))]
    dynamic_slice x36 -> x0, local copies, waits for them, and re-layouts: 24.7 us -> none  [the longest x18 14.1 us: deposit(): existing = lax.dynamic_slice(gradient, corner_start, (2, window, window))]
    pallas_call x0 -> x1, Pallas kernels: none -> 18 us  [windows(): pl.pallas_call(wkernel, out_shape=(jax.ShapeDtypeStruct((2, 6, 768, 128),...]
    add x18 -> x0, other arithmetic: 14.5 us -> none  [the longest x9 12.1 us: exit_update(): illumination[0] * patch_field[1] + illumination[1] * patch_field[0]]
    ppermute x4, waiting for transfers between devices: 19.7 us -> 30.6 us  [padded(): lax.ppermute(head, axis, [((i + 1) % count, i) for i in range(ends)])]
  transfers between devices with their start and end apart: 9 -> 9, of which waited for: 6 -> 7; matrix products, arithmetic and copies ran while one was open for 1% -> 1% of each run, Pallas kernels for 0% -> 0%
where the time goes in v1:
time: 432 us; the launch traced here: 431 us
  waiting for transfers between devices  330 us (76%)
  starting transfers between devices  26.3 us (6%)
  local copies, waits for them, and re-layouts  22.2 us (5%)
  other arithmetic  19.2 us (4%)
  Pallas kernels  18 us (4%)
  between operations  15.6 us (4%)
    psum x1, waiting for transfers between devices, shards(): summed_term = lax.psum(probe_term, ('ty', 'tx'))  272 us
    ppermute x4, waiting for transfers between devices, padded(): lax.ppermute(head, axis, [((i + 1) % count, i) for i in range(ends)])  30.6 us
    ppermute x4, waiting for transfers between devices, padded(): lax.ppermute(tail, axis, [(i, (i + 1) % count) for i in range(ends)])  26.8 us
    ppermute x4, starting transfers between devices, padded(): lax.ppermute(tail, axis, [(i, (i + 1) % count) for i in range(ends)])  19.8 us
    pallas_call x1, Pallas kernels, windows(): pl.pallas_call(wkernel, out_shape=(jax.ShapeDtypeStruct((2, 6, 768, 128),...  18 us
  transfers between devices with their start and end apart: 9, of which 7 were waited for; matrix products, arithmetic and copies ran while one was open for 1% of the time, Pallas kernels for 0%

profile of v1, /device:TPU:1, one launch (start us, length us, event | category | flops | bytes accessed | tf_op | source)
XLA Modules:
  0.0 430.9 jit_solution(8916161855953649204)
XLA Ops:
  7.2 0.0 all-reduce.2.cloned.1.call-start
  7.2 1.9 copy.16
  9.1 0.0 copy-start.8
  9.2 0.1 fusion.5
  9.2 5.8 %collective-permute-start = (f32[2,128,512]{1,2,0:T(8,128)S(1)}, f32[2,128,512]{1,2,0:T(8,128)S(1)}, u32[]{:S(2)}, u32[]{:S(2)}) collective-permute-start(f32[2,128,512]{1,2,0:T(8,128)S(1)} %get-tuple-element.62), channel_id=1, source_target_pairs={{0,16},{16,32},{32,48},{48,64},{64,80},{80,96},{96,112},{112,128},... | collective-permute-start | bytes 1572872 | tf_op jit(solution)/shard_map/ppermute | solution.py:186
  15.0 1.3 collective-permute-start.1
  16.3 12.6 %collective-permute-done = f32[2,128,512]{1,2,0:T(8,128)S(1)} collective-permute-done((f32[2,128,512]{1,2,0:T(8,128)S(1)}, f32[2,128,512]{1,2,0:T(8,128)S(1)}, u32[]{:S(2)}, u32[]{:S(2)}) %collective-permute-start) | collective-permute-done | bytes 524320 | tf_op jit(solution)/shard_map/ppermute | solution.py:186
  28.9 15.3 %collective-permute-done.1 = f32[2,128,512]{1,2,0:T(8,128)S(1)} collective-permute-done((f32[2,128,512]{1,2,0:T(8,128)S(1)}, f32[2,128,512]{1,2,0:T(8,128)S(1)}, u32[]{:S(2)}, u32[]{:S(2)}) %collective-permute-start.1) | collective-permute-done | bytes 524320 | tf_op jit(solution)/shard_map/ppermute | solution.py:188
  44.2 1.3 pad_maximum_fusion.7
  45.5 4.0 collective-permute-start.2
  49.5 1.9 collective-permute-start.3
  52.0 0.1 add_add_fusion
  52.1 0.0 copy-done.8
  52.1 0.1 bitcast_subtract_fusion.offs
  52.2 6.5 %collective-permute-done.2 = f32[2,768,128]{1,2,0:T(8,128)} collective-permute-done((f32[2,768,128]{1,2,0:T(8,128)}, f32[2,768,128]{1,2,0:T(8,128)}, u32[]{:S(2)}, u32[]{:S(2)}) %collective-permute-start.2) | collective-permute-done | bytes 786464 | tf_op jit(solution)/shard_map/ppermute | solution.py:186
  58.7 4.4 %collective-permute-done.3 = f32[2,768,128]{1,2,0:T(8,128)} collective-permute-done((f32[2,768,128]{1,2,0:T(8,128)}, f32[2,768,128]{1,2,0:T(8,128)}, u32[]{:S(2)}, u32[]{:S(2)}) %collective-permute-start.3) | collective-permute-done | bytes 786464 | tf_op jit(solution)/shard_map/ppermute | solution.py:188
  63.1 3.5 pad_maximum_fusion.1
  66.5 0.0 copy-start
  66.6 0.0 copy-start.2
  66.6 0.0 copy-start.3
  66.6 0.0 copy-start.4
  66.6 0.0 copy-start.5
  66.6 6.2 %copy.14 = f32[2,768,6,128]{3,1,2,0:T(8,128)} copy(f32[2,768,6,128]{1,3,2,0:T(8,128)} %bitcast.19) | data formatting | bytes 9437184 | tf_op jit(solution)/shard_map/reshape | solution.py:203
  72.8 0.0 copy-done
  72.8 0.0 copy-done.2
  72.8 0.0 copy-done.3
  72.8 0.0 copy-done.4
  72.8 0.0 copy-done.5
  72.8 0.0 copy-start.1
  72.8 2.2 copy-done.1
  75.0 18.0 %shard_map.104 = (f32[2,6,768,128]{3,2,1,0:T(8,128)}, f32[2,256,256]{2,1,0:T(8,128)}) custom-call(s32[2,16]{1,0:T(2,128)S(1)} %bitcast_subtract_fusion.offs, s32[1]{0:T(128)} %bitcast.10.cnt, f32[2,6,768,128]{3,2,1,0:T(8,128)} %bitcast.20, f32[2,256,256]{2,1,0:T(8,128)S(1)} %copy-done, bf16[4,256,256]{2,1,0:T(8,128)(2,1)S(1)} %copy-done.2, ...), custom_call_target="tpu_custom_call" | custom-call | tf_op jit(solution)/shard_map/pallas_call | solution.py:168
  93.0 6.1 %copy.15 = f32[2,768,6,128]{1,3,2,0:T(8,128)} copy(f32[2,768,6,128]{3,1,2,0:T(8,128)} %bitcast.21) | data formatting | bytes 9437184 | tf_op jit(solution)/shard_map/transpose | solution.py:205
  99.1 1.5 fusion.4
  100.6 1.3 collective-permute-start.4
  101.9 1.3 collective-permute-start.5
  103.2 7.7 %collective-permute-done.4 = f32[2,128,768]{1,2,0:T(8,128)S(1)} collective-permute-done((f32[2,128,768]{1,2,0:T(8,128)S(1)}, f32[2,128,768]{1,2,0:T(8,128)S(1)}, u32[]{:S(2)}, u32[]{:S(2)}) %collective-permute-start.4) | collective-permute-done | bytes 786464 | tf_op jit(solution)/shard_map/ppermute | solution.py:186
  110.9 10.9 %collective-permute-done.5 = f32[2,128,768]{1,2,0:T(8,128)S(1)} collective-permute-done((f32[2,128,768]{1,2,0:T(8,128)S(1)}, f32[2,128,768]{1,2,0:T(8,128)S(1)}, u32[]{:S(2)}, u32[]{:S(2)}) %collective-permute-start.5) | collective-permute-done | bytes 786464 | tf_op jit(solution)/shard_map/ppermute | solution.py:188
  121.8 0.0 copy-start.6
  121.8 3.2 pad_maximum_fusion.4
  125.0 0.0 copy-done.6
  125.0 8.8 %collective-permute-start.6 = (f32[2,1024,128]{1,2,0:T(8,128)}, f32[2,1024,128]{1,2,0:T(8,128)}, u32[]{:S(2)}, u32[]{:S(2)}) collective-permute-start(f32[2,1024,128]{1,2,0:T(8,128)} %get-tuple-element.56), channel_id=1, source_target_pairs={{0,1},{1,2},{2,3},{3,4},{4,5},{5,6},{6,7},{7,8},{8,9},{9,10},{10,1... | collective-permute-start | bytes 3145736 | tf_op jit(solution)/shard_map/ppermute | solution.py:186
  133.8 1.9 collective-permute-start.7
  135.7 0.0 all-reduce.2.cloned.1.call-update
  135.7 0.7 add_reduce_fusion
  137.2 272.2 %all-reduce.2.cloned.1.call-done = f32[2,256,256]{2,1,0:T(8,128)} async-done(((f32[2,256,256]{2,1,0:T(8,128)}), f32[2,256,256]{2,1,0:T(8,128)}) %all-reduce.2.cloned.1.call-update) | async-done | bytes 524304 | tf_op jit(solution)/shard_map/psum | solution.py:221
  409.4 0.0 slice-start
  409.4 2.1 multiply_add_fusion
  411.5 0.0 slice-start.1
  411.5 0.0 collective-permute-done.6
  411.5 0.0 collective-permute-done.7
  411.5 3.8 pad_maximum_fusion
  415.3 0.0 copy-start.7
  415.3 0.5 slice.172
  415.8 0.0 slice-done
  415.8 0.0 slice-done.1
  415.8 0.6 copy-done.7
  416.4 1.3 fusion.1
  417.7 1.2 fusion
  418.9 0.2 slice.174
  419.1 0.1 fusion.3
  419.2 0.1 fusion.2
  419.3 1.8 divide_add_fusion
  421.2 2.9 copy.17
  (1 shorter events, 0.0 us)
Async XLA Ops:
  7.2 402.3 %all-reduce.2.cloned.1.call-start = ((), (), s32[]{:S(2)}) async-start(), calls=%async_computation | async-start | bytes 1048576 | tf_op jit(solution)/shard_map/psum | solution.py:221
  9.1 43.0 %copy-start.8 = (s32[1,1,2,16]{3,2,1,0:T(2,128)S(1)}, s32[1,1,2,16]{3,2,1,0:T(2,128)}, u32[]{:S(2)}) copy-start(s32[1,1,2,16]{3,2,1,0:T(2,128)} %param.19) | copy-start | bytes 388
  9.2 19.7 %collective-permute-start = (f32[2,128,512]{1,2,0:T(8,128)S(1)}, f32[2,128,512]{1,2,0:T(8,128)S(1)}, u32[]{:S(2)}, u32[]{:S(2)}) collective-permute-start(f32[2,128,512]{1,2,0:T(8,128)S(1)} %get-tuple-element.62), channel_id=1, source_target_pairs={{0,16},{16,32},{32,48},{48,64},{64,80},{80,96},{96,112},{112,128},... | collective-permute-start | bytes 1572872 | tf_op jit(solution)/shard_map/ppermute | solution.py:186
  15.0 29.2 %collective-permute-start.1 = (f32[2,128,512]{1,2,0:T(8,128)S(1)}, f32[2,128,512]{1,2,0:T(8,128)S(1)}, u32[]{:S(2)}, u32[]{:S(2)}) collective-permute-start(f32[2,128,512]{1,2,0:T(8,128)S(1)} %get-tuple-element.63), channel_id=1, source_target_pairs={{16,0},{32,16},{48,32},{64,48},{80,64},{96,80},{112,96},{128,112},... | collective-permute-start | bytes 1572872 | tf_op jit(solution)/shard_map/ppermute | solution.py:188
  45.5 13.2 %collective-permute-start.2 = (f32[2,768,128]{1,2,0:T(8,128)}, f32[2,768,128]{1,2,0:T(8,128)}, u32[]{:S(2)}, u32[]{:S(2)}) collective-permute-start(f32[2,768,128]{1,2,0:T(8,128)} %get-tuple-element.60), channel_id=1, source_target_pairs={{0,1},{1,2},{2,3},{3,4},{4,5},{5,6},{6,7},{7,8},{8,9},{9,10},{10,1... | collective-permute-start | bytes 2359304 | tf_op jit(solution)/shard_map/ppermute | solution.py:186
  49.5 13.6 %collective-permute-start.3 = (f32[2,768,128]{1,2,0:T(8,128)}, f32[2,768,128]{1,2,0:T(8,128)}, u32[]{:S(2)}, u32[]{:S(2)}) collective-permute-start(f32[2,768,128]{1,2,0:T(8,128)} %get-tuple-element.61), channel_id=1, source_target_pairs={{1,0},{2,1},{3,2},{4,3},{5,4},{6,5},{7,6},{8,7},{9,8},{10,9},{11,1... | collective-permute-start | bytes 2359304 | tf_op jit(solution)/shard_map/ppermute | solution.py:188
  66.5 6.2 %copy-start = (f32[2,256,256]{2,1,0:T(8,128)S(1)}, f32[2,256,256]{2,1,0:T(8,128)}, u32[]{:S(2)}) copy-start(f32[2,256,256]{2,1,0:T(8,128)} %ill.1) | copy-start | bytes 1572868
  66.6 6.2 %copy-start.2 = (bf16[4,256,256]{2,1,0:T(8,128)(2,1)S(1)}, bf16[4,256,256]{2,1,0:T(8,128)(2,1)}, u32[]{:S(2)}) copy-start(bf16[4,256,256]{2,1,0:T(8,128)(2,1)} %constant.136.clone.mats) | copy-start | bytes 1572868
  66.6 6.2 %copy-start.3 = (f32[2,128,128]{2,1,0:T(8,128)S(1)}, f32[2,128,128]{2,1,0:T(8,128)}, u32[]{:S(2)}) copy-start(f32[2,128,128]{2,1,0:T(8,128)} %constant.137.clone.twr) | copy-start | bytes 393220
  66.6 6.2 %copy-start.4 = (bf16[256,256]{1,0:T(8,128)(2,1)S(1)}, bf16[256,256]{1,0:T(8,128)(2,1)}, u32[]{:S(2)}) copy-start(bf16[256,256]{1,0:T(8,128)(2,1)} %constant.139.clone.perm) | copy-start | bytes 393220
  66.6 6.2 %copy-start.5 = (f32[2,16,128]{2,1,0:T(8,128)S(1)}, f32[2,16,128]{2,1,0:T(8,128)}, u32[]{:S(2)}) copy-start(f32[2,16,128]{2,1,0:T(8,128)} %constant.138.clone.twl) | copy-start | bytes 49156
  72.8 2.2 copy-start.1
  100.6 10.3 %collective-permute-start.4 = (f32[2,128,768]{1,2,0:T(8,128)S(1)}, f32[2,128,768]{1,2,0:T(8,128)S(1)}, u32[]{:S(2)}, u32[]{:S(2)}) collective-permute-start(f32[2,128,768]{1,2,0:T(8,128)S(1)} %get-tuple-element.58), channel_id=1, source_target_pairs={{0,16},{16,32},{32,48},{48,64},{64,80},{80,96},{96,112},{112,128},... | collective-permute-start | bytes 2359304 | tf_op jit(solution)/shard_map/ppermute | solution.py:186
  101.9 19.8 %collective-permute-start.5 = (f32[2,128,768]{1,2,0:T(8,128)S(1)}, f32[2,128,768]{1,2,0:T(8,128)S(1)}, u32[]{:S(2)}, u32[]{:S(2)}) collective-permute-start(f32[2,128,768]{1,2,0:T(8,128)S(1)} %get-tuple-element.59), channel_id=1, source_target_pairs={{16,0},{32,16},{48,32},{64,48},{80,64},{96,80},{112,96},{128,112},... | collective-permute-start | bytes 2359304 | tf_op jit(solution)/shard_map/ppermute | solution.py:188
  121.8 3.2 copy-start.6
  125.0 286.5 %collective-permute-start.6 = (f32[2,1024,128]{1,2,0:T(8,128)}, f32[2,1024,128]{1,2,0:T(8,128)}, u32[]{:S(2)}, u32[]{:S(2)}) collective-permute-start(f32[2,1024,128]{1,2,0:T(8,128)} %get-tuple-element.56), channel_id=1, source_target_pairs={{0,1},{1,2},{2,3},{3,4},{4,5},{5,6},{6,7},{7,8},{8,9},{9,10},{10,1... | collective-permute-start | bytes 3145736 | tf_op jit(solution)/shard_map/ppermute | solution.py:186
  133.8 277.7 %collective-permute-start.7 = (f32[2,1024,128]{1,2,0:T(8,128)}, f32[2,1024,128]{1,2,0:T(8,128)}, u32[]{:S(2)}, u32[]{:S(2)}) collective-permute-start(f32[2,1024,128]{1,2,0:T(8,128)} %get-tuple-element.57), channel_id=1, source_target_pairs={{1,0},{2,1},{3,2},{4,3},{5,4},{6,5},{7,6},{8,7},{9,8},{10,9},{11,1... | collective-permute-start | bytes 3145736 | tf_op jit(solution)/shard_map/ppermute | solution.py:188
  409.4 6.4 %slice-start = ((s8[4718592]{0:T(1024)(128)(4,1)}), s8[4194304]{0:T(1024)(128)(4,1)S(1)}, s32[]{:S(2)}) async-start(s8[4718592]{0:T(1024)(128)(4,1)} %bitcast.15), calls=%async_computation.1 | async-start | bytes 8388608
  411.5 4.3 %slice-start.1 = ((s8[4718592]{0:T(1024)(128)(4,1)}), s8[524288]{0:T(1024)(128)(4,1)S(1)}, s32[]{:S(2)}) async-start(s8[4718592]{0:T(1024)(128)(4,1)} %bitcast.15), calls=%async_computation.2 | async-start | bytes 1048576
  415.3 1.1 copy-start.7
Sparse Core Ops, SparseCore 0:
  135.9 273.5 all-reduce.1

commit v2 on v1

--- a/solution.py
+++ b/solution.py
@@ -148,8 +148,8 @@
                     rr=pl.ds(h*128+j*RC,RC)
                     cr=xr-wave[0,rr,ls]; ci=xi-wave[1,rr,ls]
                     a,b=patch[0,rr,ls],patch[1,rr,ls]
-                    pterm[0,rr,ls]+=a*cr+b*ci
-                    pterm[1,rr,ls]+=a*ci-b*cr
+                    pterm[0,t,rr,:]+=a*cr+b*ci
+                    pterm[1,t,rr,:]+=a*ci-b*cr
                     pr,pi=ill[0,rr,ls],ill[1,rr,ls]
                     g[h][0][t]=pr*cr+pi*ci
                     g[h][1][t]=pr*ci-pi*cr
@@ -166,7 +166,7 @@
     mats,twr,twl,perm=consts()
     V=pl.BlockSpec(memory_space=pltpu.VMEM); Sm=pl.BlockSpec(memory_space=pltpu.SMEM)
     return pl.pallas_call(wkernel,
-        out_shape=(jax.ShapeDtypeStruct((2,6,768,128),F32),jax.ShapeDtypeStruct((2,256,256),F32)),
+        out_shape=(jax.ShapeDtypeStruct((2,6,768,128),F32),jax.ShapeDtypeStruct((2,2,256,128),F32)),
         in_specs=[Sm,Sm,V,V,V,V,V,V,pl.BlockSpec(memory_space=pl.ANY)],
         out_specs=(V,V),
         scratch_shapes=[pltpu.VMEM((16,2,256,128),F32),pltpu.VMEM((2,256,256),F32),pltpu.VMEM((2,256,256),F32),
@@ -175,52 +175,285 @@
     )(offs,cnt,ext,ill,jnp.asarray(mats),jnp.asarray(twr),jnp.asarray(twl),jnp.asarray(perm),meas)
 
 
-def padded(cells, sides, width):
-    for axis, dim in sides:
-        count = lax.axis_size(axis)
-        ends = count - 1
-        head = lax.slice_in_dim(cells, 0, width, axis=dim)
-        tail = lax.slice_in_dim(cells, cells.shape[dim] - width, cells.shape[dim], axis=dim)
-        cells = jnp.concatenate(
-            [
-                lax.ppermute(tail, axis, [(i, (i + 1) % count) for i in range(ends)]),
-                cells,
-                lax.ppermute(head, axis, [((i + 1) % count, i) for i in range(ends)]),
-            ],
-            axis=dim,
-        )
-    return cells
+MESH = pl.DeviceIdType.MESH
+
+
+def remote(src, dst, send_sem, recv_sem, device):
+    return pltpu.make_async_remote_copy(
+        src_ref=src, dst_ref=dst, send_sem=send_sem, recv_sem=recv_sem,
+        device_id=device, device_id_type=MESH,
+    )
+
+
+def greet(devices):
+    barrier = pltpu.get_barrier_semaphore()
+    expected = 0
+    for condition, device in devices:
+        if condition is None:
+            pl.semaphore_signal(barrier, inc=1, device_id=device, device_id_type=MESH)
+            expected = expected + 1
+        else:
+            @pl.when(condition)
+            def _(device=device):
+                pl.semaphore_signal(barrier, inc=1, device_id=device, device_id_type=MESH)
+            expected = expected + condition.astype(jnp.int32)
+    return barrier, expected
+
+
+def neighbours():
+    a = lax.axis_index("ty")
+    b = lax.axis_index("tx")
+    has = {"up": a > 0, "down": a < 15, "left": b > 0, "right": b < 15}
+    ids = {"up": (jnp.maximum(a - 1, 0), b), "down": (jnp.minimum(a + 1, 15), b),
+           "left": (a, jnp.maximum(b - 1, 0)), "right": (a, jnp.minimum(b + 1, 15))}
+    return a, b, has, ids
+
+
+OPPOSITE = {"up": "down", "down": "up", "left": "right", "right": "left"}
+
+
+def halo_kernel(tile, ext, own_sem, row_send, row_recv, col_send, col_recv, cor_send, cor_recv):
+    a, b, has, ids = neighbours()
+    barrier, expected = greet([(has[k], ids[k]) for k in ids])
+    own = [pltpu.make_async_copy(tile.at[:, :, pl.ds(128 * t, 128)], ext.at[:, 1 + t, pl.ds(128, 512), :], own_sem.at[t]) for t in range(4)]
+    for copy in own:
+        copy.start()
+    pl.semaphore_wait(barrier, expected)
+    rows, cols, corners = {}, {}, {}
+    for i, way in enumerate(("down", "up")):
+        src_row, dst_row = (384, 0) if way == "down" else (0, 640)
+        for t in (0, 3, 1, 2):
+            rows[way, t] = remote(
+                tile.at[:, pl.ds(src_row, 128), pl.ds(128 * t, 128)],
+                ext.at[:, 1 + t, pl.ds(dst_row, 128), :],
+                row_send.at[i, t], row_recv.at[i, t], ids[way])
+    for i, way in enumerate(("right", "left")):
+        src_t, dst_t = (3, 0) if way == "right" else (0, 5)
+        cols[way] = remote(
+            tile.at[:, :, pl.ds(128 * src_t, 128)], ext.at[:, dst_t, pl.ds(128, 512), :],
+            col_send.at[i], col_recv.at[i], ids[way])
+        for j, row in enumerate((0, 640)):
+            corners[way, j] = remote(
+                ext.at[:, 1 + src_t, pl.ds(row, 128), :], ext.at[:, dst_t, pl.ds(row, 128), :],
+                cor_send.at[i, j], cor_recv.at[i, j], ids[way])
+    for t in (0, 3, 1, 2):
+        for way in ("down", "up"):
+            pl.when(has[way])(rows[way, t].start)
+    for way in ("right", "left"):
+        pl.when(has[way])(cols[way].start)
+    for j, way in enumerate(("down", "up")):
+        @pl.when(has[OPPOSITE[way]])
+        def _(way=way):
+            rows[way, 0].wait_recv()
+            rows[way, 3].wait_recv()
+        for side in ("right", "left"):
+            pl.when(jnp.logical_and(has[side], has[OPPOSITE[way]]))(corners[side, j].start)
+    for copy in own:
+        copy.wait()
+    for way in ("down", "up"):
+        for t in (1, 2):
+            pl.when(has[OPPOSITE[way]])(rows[way, t].wait_recv)
+        for t in range(4):
+            pl.when(has[way])(rows[way, t].wait_send)
+    for side in ("right", "left"):
+        pl.when(has[OPPOSITE[side]])(cols[side].wait_recv)
+        pl.when(has[side])(cols[side].wait_send)
+        for j, way in enumerate(("down", "up")):
+            pl.when(jnp.logical_and(has[OPPOSITE[side]], has[OPPOSITE[way]]))(corners[side, j].wait_recv)
+            pl.when(jnp.logical_and(has[side], has[OPPOSITE[way]]))(corners[side, j].wait_send)
+
+
+def halo(tile):
+    D = pltpu.SemaphoreType.DMA
+    A = pl.BlockSpec(memory_space=pl.ANY)
+    return pl.pallas_call(
+        halo_kernel,
+        out_shape=jax.ShapeDtypeStruct((2, 6, 768, 128), F32),
+        in_specs=[A], out_specs=A,
+        scratch_shapes=[D((4,)), D((2, 4)), D((2, 4)), D((2,)), D((2,)), D((2, 2)), D((2, 2))],
+        compiler_params=pltpu.CompilerParams(collective_id=1, has_side_effects=True, vmem_limit_bytes=60 * 2**20),
+    )(tile)
+
+
+def partners(b):
+    core = b % 2
+    x = (b // 2) % 4
+    zlo = b // 8
+    return core, x, zlo
+
+
+def fold_kernel(grad, pterm, upd, part, rxc, rxm, rz, edge, rcore, rx, sumc,
+                core_s, core_r, xs, xr, cs, cr, ms, mr, zs, zr):
+    a, b, has, ids = neighbours()
+    core, x, zlo = partners(b)
+    mates = [(a, zlo * 8 + ((x + d) % 4) * 2 + core) for d in (1, 2, 3)]
+    other = (a, zlo * 8 + x * 2 + (1 - core))
+    barrier, expected = greet([(has[k], ids[k]) for k in ids] + [(None, m) for m in mates])
+    pl.semaphore_wait(barrier, expected)
+    first = remote(pterm.at[1 - core], rcore, core_s, core_r, other)
+    first.start()
+    corner, middle, zmid, zedge = {}, {}, {}, {}
+    for i, side in enumerate(("right", "left")):
+        src_t = 5 if side == "right" else 0
+        for j, row in enumerate((0, 640)):
+            corner[side, j] = remote(grad.at[:, src_t, pl.ds(row, 128), :], rxc.at[i, j],
+                                     cs.at[i, j], cr.at[i, j], ids[side])
+        middle[side] = remote(grad.at[:, src_t, pl.ds(128, 512), :], rxm.at[i], ms.at[i], mr.at[i], ids[side])
+    for j, way in enumerate(("up", "down")):
+        row = 0 if way == "up" else 640
+        zmid[way] = remote(grad.at[:, pl.ds(2, 2), pl.ds(row, 128), :], rz.at[j, :, pl.ds(1, 2)],
+                           zs.at[j, 1], zr.at[j, 1], ids[way])
+        for k, t in ((0, 0), (2, 3)):
+            zedge[way, k] = remote(edge.at[j, k // 2], rz.at[j, :, t], zs.at[j, k], zr.at[j, k], ids[way])
+    for side in ("right", "left"):
+        for j in range(2):
+            pl.when(has[side])(corner[side, j].start)
+    for way in ("up", "down"):
+        pl.when(has[way])(zmid[way].start)
+    for side in ("right", "left"):
+        pl.when(has[side])(middle[side].start)
+    for j, row in enumerate((0, 640)):
+        for k, (t, side) in enumerate(((1, "right"), (4, "left"))):
+            i = k
+            edge[j, k] = grad[:, t, row:row + 128, :]
+            @pl.when(has[OPPOSITE[side]])
+            def _(i=i, j=j, k=k, side=side):
+                corner[side, j].wait_recv()
+                edge[j, k] += rxc[i, j]
+            way = "up" if j == 0 else "down"
+            pl.when(has[way])(zedge[way, 2 * k].start)
+    first.wait_recv()
+    sumc[...] = pterm[core] + rcore[...]
+    xsend = [remote(sumc.at[(x + d) % 4], rx.at[d - 1], xs.at[d - 1], xr.at[d - 1], mates[d - 1]) for d in (1, 2, 3)]
+    for copy in xsend:
+        copy.start()
+    for t in range(4):
+        upd[:, t] = grad[:, 1 + t, 128:640, :]
+    for copy in xsend:
+        copy.wait_recv()
+    part[...] = sumc[x] + rx[0] + rx[1] + rx[2]
+    for i, (side, t) in enumerate((("right", 0), ("left", 3))):
+        @pl.when(has[OPPOSITE[side]])
+        def _(i=i, side=side, t=t):
+            middle[side].wait_recv()
+            upd[:, t] += rxm[i]
+    for j, (way, row) in enumerate((("up", 384), ("down", 0))):
+        @pl.when(has[OPPOSITE[way]])
+        def _(j=j, way=way, row=row):
+            zmid[way].wait_recv()
+            zedge[way, 0].wait_recv()
+            zedge[way, 2].wait_recv()
+            upd[:, :, row:row + 128, :] += rz[j]
+    first.wait_send()
+    for copy in xsend:
+        copy.wait_send()
+    for side in ("right", "left"):
+        for j in range(2):
+            pl.when(has[side])(corner[side, j].wait_send)
+        pl.when(has[side])(middle[side].wait_send)
+    for way in ("up", "down"):
+        pl.when(has[way])(zmid[way].wait_send)
+        for k in (0, 2):
+            pl.when(has[way])(zedge[way, k].wait_send)
+
+
+def fold(grad, pterm):
+    D = pltpu.SemaphoreType.DMA
+    V = pl.BlockSpec(memory_space=pltpu.VMEM)
+    return pl.pallas_call(
+        fold_kernel,
+        out_shape=(jax.ShapeDtypeStruct((2, 4, 512, 128), F32), jax.ShapeDtypeStruct((16, 8, 128), F32)),
+        in_specs=[V, V], out_specs=(V, V),
+        scratch_shapes=[
+            pltpu.VMEM((2, 2, 2, 128, 128), F32), pltpu.VMEM((2, 2, 512, 128), F32),
+            pltpu.VMEM((2, 2, 4, 128, 128), F32), pltpu.VMEM((2, 2, 2, 128, 128), F32),
+            pltpu.VMEM((4, 16, 8, 128), F32), pltpu.VMEM((3, 16, 8, 128), F32), pltpu.VMEM((4, 16, 8, 128), F32),
+            D, D, D((3,)), D((3,)), D((2, 2)), D((2, 2)), D((2,)), D((2,)), D((2, 3)), D((2, 3)),
+        ],
+        compiler_params=pltpu.CompilerParams(collective_id=2, has_side_effects=True, vmem_limit_bytes=60 * 2**20),
+    )(grad, pterm)
+
+
+def spread_kernel(part, total, rc, cs, cr, ds, dr, es, er, fs, fr):
+    a = lax.axis_index("ty")
+    b = lax.axis_index("tx")
+    core, x, zlo = partners(b)
+    low = x * 2 + core
+    unit = zlo * 16 + a
+
+    def member(d):
+        u = (unit + d) % 32
+        return (u % 16, (u // 16) * 8 + low)
+
+    mates = [(a, zlo * 8 + ((x + d) % 4) * 2 + core) for d in (1, 2, 3)]
+    other = (a, zlo * 8 + x * 2 + (1 - core))
+    barrier, expected = greet([(None, m) for m in mates] + [(None, other)])
+
+    @pl.loop(1, 32)
+    def _(d):
+        pl.semaphore_signal(barrier, inc=1, device_id=member(d), device_id_type=MESH)
+
+    pl.semaphore_wait(barrier, expected + 31)
+
+    @pl.loop(1, 32)
+    def _(d):
+        device = member(d)
+        remote(part.at[device[0]], rc.at[d - 1], cs, cr, device).start()
+
+    whole = remote(rc, rc, cs, cr, other)
+    whole.wait_recv()
+    acc = part[a]
+    for i in range(31):
+        acc = acc + rc[i]
+    total[core, x, a] = acc
+
+    @pl.loop(1, 16)
+    def _(d):
+        remote(total.at[core, x, a], total.at[core, x, a], ds, dr, ((a + d) % 16, b)).start()
+
+    some = remote(rc.at[pl.ds(0, 15)], rc.at[pl.ds(0, 15)], ds, dr, other)
+    some.wait_recv()
+    gather = [remote(total.at[core, x], total.at[core, x], es.at[d - 1], er.at[d - 1], mates[d - 1]) for d in (1, 2, 3)]
+    for copy in gather:
+        copy.start()
+    for copy in gather:
+        copy.wait_recv()
+    last = remote(total.at[core], total.at[core], fs, fr, other)
+    last.start()
+    whole.wait_send()
+    some.wait_send()
+    for copy in gather:
+        copy.wait_send()
+    last.wait()
+
+
+def spread(part):
+    D = pltpu.SemaphoreType.DMA
+    V = pl.BlockSpec(memory_space=pltpu.VMEM)
+    return pl.pallas_call(
+        spread_kernel,
+        out_shape=jax.ShapeDtypeStruct((2, 4, 16, 8, 128), F32),
+        in_specs=[V], out_specs=V,
+        scratch_shapes=[pltpu.VMEM((31, 8, 128), F32), D, D, D, D, D((3,)), D((3,)), D, D],
+        compiler_params=pltpu.CompilerParams(collective_id=3, has_side_effects=True, vmem_limit_bytes=60 * 2**20),
+    )(part)
 
 
 def shards(specimen, illumination, scan_offsets, slot_counts, measured):
-    tile_rows = specimen.shape[1]
-    tile_cols = specimen.shape[2]
-    margin = 128
-    slot_count = measured.shape[2]
-    anchor = jnp.stack([lax.axis_index("ty") * tile_rows, lax.axis_index("tx") * tile_cols]) - margin
+    anchor = jnp.stack([lax.axis_index("ty") * 512, lax.axis_index("tx") * 512]) - 128
     local = scan_offsets[0, 0] - anchor[:, None]
-    extended = padded(specimen, (("ty", 1), ("tx", 2)), margin)
-    ext = extended.reshape(2, 768, 6, 128).transpose(0, 2, 1, 3)
+    ext = halo(specimen)
     grad, probe_term = windows(local, slot_counts[0], ext, illumination, measured[0, 0])
-    gradient = grad.transpose(0, 2, 1, 3).reshape(2, 768, 768)
-    folded = padded(gradient, (("ty", 1), ("tx", 2)), margin)
-    row_folded = folded[:, 2 * margin : 2 * margin + tile_rows, :]
-    row_folded = row_folded.at[:, :margin, :].add(folded[:, :margin, :])
-    row_folded = row_folded.at[:, tile_rows - margin :, :].add(
-        folded[:, tile_rows + 3 * margin :, :]
-    )
-    update_field = row_folded[:, :, 2 * margin : 2 * margin + tile_cols]
-    update_field = update_field.at[:, :, :margin].add(row_folded[:, :, :margin])
-    update_field = update_field.at[:, :, tile_cols - margin :].add(
-        row_folded[:, :, tile_cols + 3 * margin :]
-    )
+    update, part = fold(grad, probe_term.reshape(2, 4, 16, 8, 128))
+    total = spread(part)
     probe_power = (
         jnp.mean(illumination[0] * illumination[0] + illumination[1] * illumination[1]) + 1e-05
     )
-    new_specimen = specimen + update_field / probe_power
-    summed_term = lax.psum(probe_term, ("ty", "tx"))
-    total_slots = slot_count * lax.axis_size("ty") * lax.axis_size("tx")
-    new_illumination = illumination + summed_term / math.sqrt(total_slots)
+    field = update.transpose(0, 2, 1, 3).reshape(2, 512, 512)
+    new_specimen = specimen + field / probe_power
+    summed = total.reshape(2, 2, 256, 128).transpose(0, 2, 1, 3).reshape(2, 256, 256)
+    total_slots = measured.shape[2] * lax.axis_size("ty") * lax.axis_size("tx")
+    new_illumination = illumination + summed / math.sqrt(total_slots)
     return (new_specimen, new_illumination)
 
 def solution(mesh):

time: 432 us -> 196 us (0.45)
  waiting for transfers between devices: 330 us -> 0 us
  Pallas kernels: 18 us -> 173 us
  starting transfers between devices: 26.3 us -> 0 us
  between operations: 15.6 us -> 2.05 us
  local copies, waits for them, and re-layouts: 22.2 us -> 10.7 us
  other arithmetic: 19.2 us -> 9.73 us
    psum x1 -> x0, waiting for transfers between devices: 272 us -> none  [shards(): summed_term = lax.psum(probe_term, ('ty', 'tx'))]
    pallas_call x0 -> x3, Pallas kernels: none -> 163 us  [the longest x1 65.1 us: halo(): pl.pallas_call(halo_kernel, out_shape=jax.ShapeDtypeStruct((2, 6, 768, 12...]
    ppermute x8 -> x0, waiting for transfers between devices: 57.4 us -> none  [the longest x4 30.6 us: padded(): lax.ppermute(head, axis, [((i + 1) % count, i) for i in range(ends)])]
    ppermute x8 -> x0, starting transfers between devices: 26.2 us -> none  [the longest x4 19.8 us: padded(): lax.ppermute(tail, axis, [(i, (i + 1) % count) for i in range(ends)])]
    pallas_call x1, Pallas kernels: 18 us -> 10.3 us  [windows(): pl.pallas_call(wkernel, out_shape=(jax.ShapeDtypeStruct((2, 6, 768, 128),...]
    concatenate x2 -> x0, other arithmetic: 7.25 us -> none  [padded(): jnp.concatenate([lax.ppermute(tail, axis, [(i, (i + 1) % count) for i in...]
    reshape x1 -> x0, local copies, waits for them, and re-layouts: 6.2 us -> none  [shards(): ext = extended.reshape(2, 768, 6, 128).transpose(0, 2, 1, 3)]
    transpose x1 -> x0, local copies, waits for them, and re-layouts: 6.1 us -> none  [shards(): gradient = grad.transpose(0, 2, 1, 3).reshape(2, 768, 768)]
  transfers between devices with their start and end apart: 9 -> 0, of which waited for: 7 -> 0; matrix products, arithmetic and copies ran while one was open for 1% -> 0% of each run, Pallas kernels for 0% -> 0%
where the time goes in v2:
time: 196 us; the launch traced here: 195 us
  Pallas kernels  173 us (88%)
  local copies, waits for them, and re-layouts  10.7 us (5%)
  other arithmetic  9.73 us (5%)
  between operations  2.05 us (1%)
    pallas_call x1, Pallas kernels, halo(): pl.pallas_call(halo_kernel, out_shape=jax.ShapeDtypeStruct((2, 6, 768, 12...  65.1 us
    pallas_call x1, Pallas kernels, spread(): pl.pallas_call(spread_kernel, out_shape=jax.ShapeDtypeStruct((2, 4, 16, 8...  56.4 us
    pallas_call x1, Pallas kernels, fold(): pl.pallas_call(fold_kernel, out_shape=(jax.ShapeDtypeStruct((2, 4, 512, 1...  41.1 us
    pallas_call x1, Pallas kernels, windows(): pl.pallas_call(wkernel, out_shape=(jax.ShapeDtypeStruct((2, 6, 768, 128),...  10.3 us
    unnamed x16, local copies, waits for them, and re-layouts  8.76 us

profile of v2, /device:TPU:1, one launch (start us, length us, event | category | flops | bytes accessed | tf_op | source)
XLA Modules:
  0.0 195.3 jit_solution(14330408260692405591)
XLA Ops:
  0.6 0.1 add_add_fusion
  0.7 0.7 bitcast_subtract_fusion.offs
  1.5 0.0 copy-start
  1.5 0.0 copy-start.3
  1.5 0.0 copy-start.4
  1.5 0.0 copy-start.5
  1.5 0.0 copy-start.6
  1.5 65.1 %shard_map.104.ext = f32[2,6,768,128]{3,2,1,0:T(8,128)} custom-call(f32[2,512,512]{2,1,0:T(8,128)} %tile.1), custom_call_target="tpu_custom_call" | custom-call | tf_op jit(solution)/shard_map/pallas_call | solution.py:269
  67.3 0.0 copy-done
  67.3 0.0 copy-done.3
  67.3 0.0 copy-done.4
  67.3 0.0 copy-done.5
  67.3 0.0 copy-done.6
  67.3 0.0 copy-start.1
  67.3 2.2 %copy-done.1 = f32[1,1,16,256,256]{4,3,2,1,0:T(8,128)S(1)} copy-done((f32[1,1,16,256,256]{4,3,2,1,0:T(8,128)S(1)}, f32[1,1,16,256,256]{4,3,2,1,0:T(8,128)}, u32[]{:S(2)}) %copy-start.1) | copy-done | bytes 4194328
  69.5 10.3 %shard_map.105 = (f32[2,6,768,128]{3,2,1,0:T(8,128)}, f32[2,2,256,128]{3,2,1,0:T(8,128)S(1)}) custom-call(s32[2,16]{1,0:T(2,128)S(1)} %bitcast_subtract_fusion.offs, s32[1]{0:T(128)} %bitcast.21.cnt, f32[2,6,768,128]{3,2,1,0:T(8,128)} %shard_map.104.ext, f32[2,256,256]{2,1,0:T(8,128)S(1)} %copy-done, bf16[4,256,256]{2,1,0:T(8,128)(2,1)S(1)} %copy-done.3, ...), custom_call_target="tpu_custom_call" | custom-call | tf_op jit(solution)/shard_map/pallas_call | solution.py:168
  79.8 0.0 copy-start.2
  79.8 0.8 copy-done.2
  80.6 41.1 %shard_map.106 = (f32[2,4,512,128]{3,2,1,0:T(8,128)}, f32[16,8,128]{2,1,0:T(8,128)}) custom-call(f32[2,6,768,128]{3,2,1,0:T(8,128)} %get-tuple-element.6.grad, f32[2,4,16,8,128]{4,3,2,1,0:T(8,128)} %bitcast.23), custom_call_target="tpu_custom_call" | custom-call | tf_op jit(solution)/shard_map/pallas_call | solution.py:363
  121.7 0.7 add_reduce_fusion
  123.0 3.1 %divide_bitcast_fusion = f32[2,512,4,128]{3,1,2,0:T(8,128)} fusion(f32[2,4,512,128]{3,2,1,0:T(8,128)} %get-tuple-element.8, f32[]{:T(128)S(6)} %add.19), kind=kLoop, calls=%fused_computation.1 | loop fusion | flops 524288 | bytes 4194308 | tf_op jit(solution)/shard_map/div | solution.py:453
  126.0 1.9 copy.12
  128.0 2.9 %copy.13 = f32[2,512,512]{1,2,0:T(8,128)} copy(f32[2,512,512]{2,1,0:T(8,128)} %tile.1) | data formatting | bytes 4194304 | tf_op args[0]
  130.9 3.2 %bitcast_add_fusion = f32[2,512,512]{1,2,0:T(8,128)} fusion(f32[2,512,512]{1,2,0:T(8,128)} %copy.13, f32[2,512,4,128]{1,3,2,0:T(8,128)S(1)} %copy.12), kind=kLoop, calls=%fused_computation | loop fusion | flops 524288 | bytes 6291456 | tf_op jit(solution)/shard_map/add | solution.py:453
  134.1 2.9 %copy.15 = f32[2,512,512]{2,1,0:T(8,128)} copy(f32[2,512,512]{1,2,0:T(8,128)} %bitcast_add_fusion) | data formatting | bytes 4194304
  137.0 56.4 %shard_map.107 = f32[2,4,16,8,128]{4,3,2,1,0:T(8,128)} custom-call(f32[16,8,128]{2,1,0:T(8,128)} %get-tuple-element.9.part), custom_call_target="tpu_custom_call" | custom-call | tf_op jit(solution)/shard_map/pallas_call | solution.py:433
  193.3 1.1 broadcast_multiply_fusion
  194.4 0.9 bitcast_add_fusion.1
Async XLA Ops:
  1.5 65.8 %copy-start = (f32[2,256,256]{2,1,0:T(8,128)S(1)}, f32[2,256,256]{2,1,0:T(8,128)}, u32[]{:S(2)}) copy-start(f32[2,256,256]{2,1,0:T(8,128)} %ill.1) | copy-start | bytes 1572868
  1.5 65.8 %copy-start.3 = (bf16[4,256,256]{2,1,0:T(8,128)(2,1)S(1)}, bf16[4,256,256]{2,1,0:T(8,128)(2,1)}, u32[]{:S(2)}) copy-start(bf16[4,256,256]{2,1,0:T(8,128)(2,1)} %constant.30.clone.mats) | copy-start | bytes 1572868
  1.5 65.8 %copy-start.4 = (f32[2,128,128]{2,1,0:T(8,128)S(1)}, f32[2,128,128]{2,1,0:T(8,128)}, u32[]{:S(2)}) copy-start(f32[2,128,128]{2,1,0:T(8,128)} %constant.31.clone.twr) | copy-start | bytes 393220
  1.5 65.8 %copy-start.5 = (bf16[256,256]{1,0:T(8,128)(2,1)S(1)}, bf16[256,256]{1,0:T(8,128)(2,1)}, u32[]{:S(2)}) copy-start(bf16[256,256]{1,0:T(8,128)(2,1)} %constant.33.clone.perm) | copy-start | bytes 393220
  1.5 65.8 %copy-start.6 = (f32[2,16,128]{2,1,0:T(8,128)S(1)}, f32[2,16,128]{2,1,0:T(8,128)}, u32[]{:S(2)}) copy-start(f32[2,16,128]{2,1,0:T(8,128)} %constant.32.clone.twl) | copy-start | bytes 49156
  67.3 2.2 %copy-start.1 = (f32[1,1,16,256,256]{4,3,2,1,0:T(8,128)S(1)}, f32[1,1,16,256,256]{4,3,2,1,0:T(8,128)}, u32[]{:S(2)}) copy-start(f32[1,1,16,256,256]{4,3,2,1,0:T(8,128)} %param.13) | copy-start | bytes 12582916
  79.8 0.8 copy-start.2

commit v3 on v2

--- a/solution.py
+++ b/solution.py
@@ -171,7 +171,7 @@
         out_specs=(V,V),
         scratch_shapes=[pltpu.VMEM((16,2,256,128),F32),pltpu.VMEM((2,256,256),F32),pltpu.VMEM((2,256,256),F32),
             pltpu.VMEM((2,256,256),BF),pltpu.VMEM((2,256,256),BF),pltpu.VMEM((2,256,256),F32),pltpu.SemaphoreType.DMA((16,2))],
-        compiler_params=pltpu.CompilerParams(vmem_limit_bytes=48*2**20),
+        compiler_params=pltpu.CompilerParams(vmem_limit_bytes=28*2**20),
     )(offs,cnt,ext,ill,jnp.asarray(mats),jnp.asarray(twr),jnp.asarray(twl),jnp.asarray(perm),meas)
 
 
@@ -269,9 +269,9 @@
     return pl.pallas_call(
         halo_kernel,
         out_shape=jax.ShapeDtypeStruct((2, 6, 768, 128), F32),
-        in_specs=[A], out_specs=A,
+        in_specs=[A], out_specs=pl.BlockSpec(memory_space=pltpu.VMEM),
         scratch_shapes=[D((4,)), D((2, 4)), D((2, 4)), D((2,)), D((2,)), D((2, 2)), D((2, 2))],
-        compiler_params=pltpu.CompilerParams(collective_id=1, has_side_effects=True, vmem_limit_bytes=60 * 2**20),
+        compiler_params=pltpu.CompilerParams(collective_id=1, has_side_effects=True, vmem_limit_bytes=24 * 2**20),
     )(tile)
 
 
@@ -282,14 +282,32 @@
     return core, x, zlo
 
 
-def fold_kernel(grad, pterm, upd, part, rxc, rxm, rz, edge, rcore, rx, sumc,
-                core_s, core_r, xs, xr, cs, cr, ms, mr, zs, zr):
+def finish_kernel(spec, ill, grad, pterm, newspec, newill,
+                  rxc, rxm, rz, edge, rcore, rx, sumc, part, rc, total,
+                  core_s, core_r, xs, xr, cs, cr, ms, mr, zs, zr,
+                  us, ur, ds, dr, es, er, fs, fr):
     a, b, has, ids = neighbours()
     core, x, zlo = partners(b)
+    low = x * 2 + core
+    unit = zlo * 16 + a
+
+    def member(d):
+        u = (unit + d) % 32
+        return (u % 16, (u // 16) * 8 + low)
+
     mates = [(a, zlo * 8 + ((x + d) % 4) * 2 + core) for d in (1, 2, 3)]
     other = (a, zlo * 8 + x * 2 + (1 - core))
-    barrier, expected = greet([(has[k], ids[k]) for k in ids] + [(None, m) for m in mates])
-    pl.semaphore_wait(barrier, expected)
+    barrier, expected = greet([(None, m) for m in mates] + [(None, other)]
+                              + [(jnp.logical_and(core == 0, has["left"]), ids["left"]),
+                                 (jnp.logical_and(core == 1, has["right"]), ids["right"])])
+
+    @pl.loop(1, 32)
+    def _(d):
+        pl.semaphore_signal(barrier, inc=1, device_id=member(d), device_id_type=MESH)
+
+    power = jnp.sum(ill[0] * ill[0] + ill[1] * ill[1]) * (1.0 / 65536) + 1e-05
+    inv = 1.0 / power
+    pl.semaphore_wait(barrier, expected + 31)
     first = remote(pterm.at[1 - core], rcore, core_s, core_r, other)
     first.start()
     corner, middle, zmid, zedge = {}, {}, {}, {}
@@ -310,97 +328,41 @@
             pl.when(has[side])(corner[side, j].start)
     for way in ("up", "down"):
         pl.when(has[way])(zmid[way].start)
-    for side in ("right", "left"):
-        pl.when(has[side])(middle[side].start)
-    for j, row in enumerate((0, 640)):
-        for k, (t, side) in enumerate(((1, "right"), (4, "left"))):
-            i = k
-            edge[j, k] = grad[:, t, row:row + 128, :]
-            @pl.when(has[OPPOSITE[side]])
-            def _(i=i, j=j, k=k, side=side):
-                corner[side, j].wait_recv()
-                edge[j, k] += rxc[i, j]
-            way = "up" if j == 0 else "down"
-            pl.when(has[way])(zedge[way, 2 * k].start)
     first.wait_recv()
     sumc[...] = pterm[core] + rcore[...]
     xsend = [remote(sumc.at[(x + d) % 4], rx.at[d - 1], xs.at[d - 1], xr.at[d - 1], mates[d - 1]) for d in (1, 2, 3)]
     for copy in xsend:
         copy.start()
-    for t in range(4):
-        upd[:, t] = grad[:, 1 + t, 128:640, :]
+    for side in ("right", "left"):
+        pl.when(has[side])(middle[side].start)
+    for j, row in enumerate((0, 640)):
+        for k, (t, side) in enumerate(((1, "right"), (4, "left"))):
+            edge[j, k] = grad[:, t, row:row + 128, :]
+            @pl.when(has[OPPOSITE[side]])
+            def _(j=j, k=k, side=side):
+                corner[side, j].wait_recv()
+                edge[j, k] += rxc[k, j]
+            way = "up" if j == 0 else "down"
+            pl.when(has[way])(zedge[way, 2 * k].start)
     for copy in xsend:
         copy.wait_recv()
     part[...] = sumc[x] + rx[0] + rx[1] + rx[2]
-    for i, (side, t) in enumerate((("right", 0), ("left", 3))):
-        @pl.when(has[OPPOSITE[side]])
-        def _(i=i, side=side, t=t):
-            middle[side].wait_recv()
-            upd[:, t] += rxm[i]
-    for j, (way, row) in enumerate((("up", 384), ("down", 0))):
-        @pl.when(has[OPPOSITE[way]])
-        def _(j=j, way=way, row=row):
-            zmid[way].wait_recv()
-            zedge[way, 0].wait_recv()
-            zedge[way, 2].wait_recv()
-            upd[:, :, row:row + 128, :] += rz[j]
-    first.wait_send()
-    for copy in xsend:
-        copy.wait_send()
-    for side in ("right", "left"):
-        for j in range(2):
-            pl.when(has[side])(corner[side, j].wait_send)
-        pl.when(has[side])(middle[side].wait_send)
-    for way in ("up", "down"):
-        pl.when(has[way])(zmid[way].wait_send)
-        for k in (0, 2):
-            pl.when(has[way])(zedge[way, k].wait_send)
-
-
-def fold(grad, pterm):
-    D = pltpu.SemaphoreType.DMA
-    V = pl.BlockSpec(memory_space=pltpu.VMEM)
-    return pl.pallas_call(
-        fold_kernel,
-        out_shape=(jax.ShapeDtypeStruct((2, 4, 512, 128), F32), jax.ShapeDtypeStruct((16, 8, 128), F32)),
-        in_specs=[V, V], out_specs=(V, V),
-        scratch_shapes=[
-            pltpu.VMEM((2, 2, 2, 128, 128), F32), pltpu.VMEM((2, 2, 512, 128), F32),
-            pltpu.VMEM((2, 2, 4, 128, 128), F32), pltpu.VMEM((2, 2, 2, 128, 128), F32),
-            pltpu.VMEM((4, 16, 8, 128), F32), pltpu.VMEM((3, 16, 8, 128), F32), pltpu.VMEM((4, 16, 8, 128), F32),
-            D, D, D((3,)), D((3,)), D((2, 2)), D((2, 2)), D((2,)), D((2,)), D((2, 3)), D((2, 3)),
-        ],
-        compiler_params=pltpu.CompilerParams(collective_id=2, has_side_effects=True, vmem_limit_bytes=60 * 2**20),
-    )(grad, pterm)
-
-
-def spread_kernel(part, total, rc, cs, cr, ds, dr, es, er, fs, fr):
-    a = lax.axis_index("ty")
-    b = lax.axis_index("tx")
-    core, x, zlo = partners(b)
-    low = x * 2 + core
-    unit = zlo * 16 + a
-
-    def member(d):
-        u = (unit + d) % 32
-        return (u % 16, (u // 16) * 8 + low)
-
-    mates = [(a, zlo * 8 + ((x + d) % 4) * 2 + core) for d in (1, 2, 3)]
-    other = (a, zlo * 8 + x * 2 + (1 - core))
-    barrier, expected = greet([(None, m) for m in mates] + [(None, other)])
-
-    @pl.loop(1, 32)
-    def _(d):
-        pl.semaphore_signal(barrier, inc=1, device_id=member(d), device_id_type=MESH)
-
-    pl.semaphore_wait(barrier, expected + 31)
 
     @pl.loop(1, 32)
     def _(d):
         device = member(d)
-        remote(part.at[device[0]], rc.at[d - 1], cs, cr, device).start()
-
-    whole = remote(rc, rc, cs, cr, other)
+        remote(part.at[device[0]], rc.at[d - 1], us, ur, device).start()
+
+    @pl.loop(0, 16)
+    def _(i):
+        rows = pl.ds(pl.multiple_of(32 * i, 32), 32)
+        more = pl.ds(pl.multiple_of(32 * i + 128, 32), 32)
+        for p in range(2):
+            for t in range(4):
+                lanes = pl.ds(128 * t, 128)
+                newspec[p, rows, lanes] = spec[p, rows, lanes] + inv * grad[p, 1 + t, more, :]
+
+    whole = remote(rc, rc, us, ur, other)
     whole.wait_recv()
     acc = part[a]
     for i in range(31):
@@ -411,6 +373,11 @@
     def _(d):
         remote(total.at[core, x, a], total.at[core, x, a], ds, dr, ((a + d) % 16, b)).start()
 
+    for k, (side, t) in enumerate((("right", 0), ("left", 3))):
+        @pl.when(has[OPPOSITE[side]])
+        def _(k=k, side=side, t=t):
+            middle[side].wait_recv()
+            newspec[:, :, 128 * t:128 * t + 128] += inv * rxm[k]
     some = remote(rc.at[pl.ds(0, 15)], rc.at[pl.ds(0, 15)], ds, dr, other)
     some.wait_recv()
     gather = [remote(total.at[core, x], total.at[core, x], es.at[d - 1], er.at[d - 1], mates[d - 1]) for d in (1, 2, 3)]
@@ -420,23 +387,51 @@
         copy.wait_recv()
     last = remote(total.at[core], total.at[core], fs, fr, other)
     last.start()
+    for j, (way, row) in enumerate((("up", 384), ("down", 0))):
+        @pl.when(has[OPPOSITE[way]])
+        def _(j=j, way=way, row=row):
+            zmid[way].wait_recv()
+            zedge[way, 0].wait_recv()
+            zedge[way, 2].wait_recv()
+            for t in range(4):
+                newspec[:, row:row + 128, 128 * t:128 * t + 128] += inv * rz[j, :, t]
+    last.wait()
+    for p in range(2):
+        for s in range(4):
+            rows, lanes = pl.ds((s % 2) * 128, 128), pl.ds((s // 2) * 128, 128)
+            newill[p, rows, lanes] = ill[p, rows, lanes] + total[p, s].reshape(128, 128) * (1.0 / 64)
+    first.wait_send()
+    for copy in xsend + gather:
+        copy.wait_send()
     whole.wait_send()
     some.wait_send()
-    for copy in gather:
-        copy.wait_send()
-    last.wait()
-
-
-def spread(part):
+    for side in ("right", "left"):
+        for j in range(2):
+            pl.when(has[side])(corner[side, j].wait_send)
+        pl.when(has[side])(middle[side].wait_send)
+    for way in ("up", "down"):
+        pl.when(has[way])(zmid[way].wait_send)
+        for k in (0, 2):
+            pl.when(has[way])(zedge[way, k].wait_send)
+
+
+def finish(spec, ill, grad, pterm):
     D = pltpu.SemaphoreType.DMA
     V = pl.BlockSpec(memory_space=pltpu.VMEM)
     return pl.pallas_call(
-        spread_kernel,
-        out_shape=jax.ShapeDtypeStruct((2, 4, 16, 8, 128), F32),
-        in_specs=[V], out_specs=V,
-        scratch_shapes=[pltpu.VMEM((31, 8, 128), F32), D, D, D, D, D((3,)), D((3,)), D, D],
-        compiler_params=pltpu.CompilerParams(collective_id=3, has_side_effects=True, vmem_limit_bytes=60 * 2**20),
-    )(part)
+        finish_kernel,
+        out_shape=(jax.ShapeDtypeStruct((2, 512, 512), F32), jax.ShapeDtypeStruct((2, 256, 256), F32)),
+        in_specs=[V, V, V, V], out_specs=(V, V),
+        scratch_shapes=[
+            pltpu.VMEM((2, 2, 2, 128, 128), F32), pltpu.VMEM((2, 2, 512, 128), F32),
+            pltpu.VMEM((2, 2, 4, 128, 128), F32), pltpu.VMEM((2, 2, 2, 128, 128), F32),
+            pltpu.VMEM((4, 16, 8, 128), F32), pltpu.VMEM((3, 16, 8, 128), F32), pltpu.VMEM((4, 16, 8, 128), F32),
+            pltpu.VMEM((16, 8, 128), F32), pltpu.VMEM((31, 8, 128), F32), pltpu.VMEM((2, 4, 16, 8, 128), F32),
+            D, D, D((3,)), D((3,)), D((2, 2)), D((2, 2)), D((2,)), D((2,)), D((2, 3)), D((2, 3)),
+            D, D, D, D, D((3,)), D((3,)), D, D,
+        ],
+        compiler_params=pltpu.CompilerParams(collective_id=2, has_side_effects=True, vmem_limit_bytes=32 * 2**20),
+    )(spec, ill, grad, pterm)
 
 
 def shards(specimen, illumination, scan_offsets, slot_counts, measured):
@@ -444,17 +439,8 @@
     local = scan_offsets[0, 0] - anchor[:, None]
     ext = halo(specimen)
     grad, probe_term = windows(local, slot_counts[0], ext, illumination, measured[0, 0])
-    update, part = fold(grad, probe_term.reshape(2, 4, 16, 8, 128))
-    total = spread(part)
-    probe_power = (
-        jnp.mean(illumination[0] * illumination[0] + illumination[1] * illumination[1]) + 1e-05
-    )
-    field = update.transpose(0, 2, 1, 3).reshape(2, 512, 512)
-    new_specimen = specimen + field / probe_power
-    summed = total.reshape(2, 2, 256, 128).transpose(0, 2, 1, 3).reshape(2, 256, 256)
-    total_slots = measured.shape[2] * lax.axis_size("ty") * lax.axis_size("tx")
-    new_illumination = illumination + summed / math.sqrt(total_slots)
-    return (new_specimen, new_illumination)
+    return finish(specimen, illumination, grad, probe_term.reshape(2, 4, 16, 8, 128))
+
 
 def solution(mesh):
     in_specs = (

time: 196 us -> 131 us (0.67)
  Pallas kernels: 173 us -> 125 us
  other arithmetic: 9.73 us -> 0.82 us
  local copies, waits for them, and re-layouts: 10.7 us -> 3.74 us
    pallas_call x1, Pallas kernels: 65.1 us -> 31.6 us  [halo(): pl.pallas_call(halo_kernel, out_shape=jax.ShapeDtypeStruct((2, 6, 768, 12...]
    pallas_call x2 -> x1, Pallas kernels: 97.5 us -> 89.2 us  [finish(): pl.pallas_call(finish_kernel, out_shape=(jax.ShapeDtypeStruct((2, 512, 51...]
    pallas_call x1, Pallas kernels: 10.3 us -> 3.91 us  [windows(): pl.pallas_call(wkernel, out_shape=(jax.ShapeDtypeStruct((2, 6, 768, 128),...]
    unnamed x16 -> x18, local copies, waits for them, and re-layouts: 8.76 us -> 3.74 us
    div x2 -> x0, other arithmetic: 4.13 us -> none  [the longest x1 3.05 us: shards(): new_specimen = specimen + field / probe_power]
    add x2 -> x0, other arithmetic: 4.11 us -> none  [the longest x1 3.23 us: shards(): new_specimen = specimen + field / probe_power]
where the time goes in v3:
time: 131 us
  Pallas kernels  125 us (95%)
  local copies, waits for them, and re-layouts  3.74 us (3%)
  between operations  1.4 us (1%)
    pallas_call x1, Pallas kernels, finish(): pl.pallas_call(finish_kernel, out_shape=(jax.ShapeDtypeStruct((2, 512, 51...  89.2 us
    pallas_call x1, Pallas kernels, halo(): pl.pallas_call(halo_kernel, out_shape=jax.ShapeDtypeStruct((2, 6, 768, 12...  31.6 us
    pallas_call x1, Pallas kernels, windows(): pl.pallas_call(wkernel, out_shape=(jax.ShapeDtypeStruct((2, 6, 768, 128),...  3.91 us
    unnamed x18, local copies, waits for them, and re-layouts  3.74 us

profile of v3, /device:TPU:1, one launch (start us, length us, event | category | flops | bytes accessed | tf_op | source)
XLA Modules:
  0.0 130.7 jit_solution(13418820842820271134)
XLA Ops:
  0.6 0.0 copy-start.7
  1.3 0.1 add_add_fusion
  1.4 0.7 bitcast_subtract_fusion.offs
  2.1 0.0 copy-start
  2.1 1.6 %copy-done = f32[2,512,512]{2,1,0:T(8,128)S(1)} copy-done((f32[2,512,512]{2,1,0:T(8,128)S(1)}, f32[2,512,512]{2,1,0:T(8,128)}, u32[]{:S(2)}) %copy-start) | copy-done | bytes 2097176
  3.7 0.0 copy-start.2
  3.7 0.0 copy-start.3
  3.7 0.0 copy-start.4
  3.7 0.0 copy-start.5
  3.7 0.0 copy-start.6
  3.7 31.6 %shard_map.104.ext = f32[2,6,768,128]{3,2,1,0:T(8,128)S(1)} custom-call(f32[2,512,512]{2,1,0:T(8,128)S(1)} %copy-done), custom_call_target="tpu_custom_call" | custom-call | tf_op jit(solution)/shard_map/pallas_call | solution.py:269
  35.4 0.0 copy-done.7
  35.4 0.0 copy-done.2
  35.4 0.0 copy-done.3
  35.4 0.0 copy-done.4
  35.4 0.0 copy-done.5
  35.4 0.0 copy-done.6
  35.4 0.0 copy-start.1
  35.4 3.9 %shard_map.105 = (f32[2,6,768,128]{3,2,1,0:T(8,128)S(1)}, f32[2,2,256,128]{3,2,1,0:T(8,128)S(1)}) custom-call(s32[2,16]{1,0:T(2,128)S(1)} %bitcast_subtract_fusion.offs, s32[1]{0:T(128)} %bitcast.7.cnt, f32[2,6,768,128]{3,2,1,0:T(8,128)S(1)} %shard_map.104.ext, f32[2,256,256]{2,1,0:T(8,128)S(1)} %copy-done.3, bf16[4,256,256]{2,1,0:T(8,128)(2,1)S(1)} %copy-done.4, ...), custom_call_target="tpu_custom_call" | custom-call | tf_op jit(solution)/shard_map/pallas_call | solution.py:168
  39.4 0.0 copy-done.1
  39.4 89.2 %shard_map.106 = (f32[2,512,512]{2,1,0:T(8,128)S(1)}, f32[2,256,256]{2,1,0:T(8,128)S(1)}) custom-call(f32[2,512,512]{2,1,0:T(8,128)S(1)} %copy-done.1, f32[2,256,256]{2,1,0:T(8,128)S(1)} %copy-done.3, f32[2,6,768,128]{3,2,1,0:T(8,128)S(1)} %get-tuple-element.4.grad, f32[2,4,16,8,128]{4,3,2,1,0:T(8,128)S(1)} %bitcast.9), custom_call_target="tpu_custom_call" | custom-call | tf_op jit(solution)/shard_map/pallas_call | solution.py:421
  128.6 1.3 %copy.14 = f32[2,512,512]{2,1,0:T(8,128)} copy(f32[2,512,512]{2,1,0:T(8,128)S(1)} %get-tuple-element.8) | data formatting | bytes 4194304
  129.9 0.8 copy.15
Async XLA Ops:
  0.6 34.7 %copy-start.7 = (f32[2,16,128]{2,1,0:T(8,128)S(1)}, f32[2,16,128]{2,1,0:T(8,128)}, u32[]{:S(2)}) copy-start(f32[2,16,128]{2,1,0:T(8,128)} %constant.22.clone.twl) | copy-start | bytes 49156
  2.1 1.6 %copy-start = (f32[2,512,512]{2,1,0:T(8,128)S(1)}, f32[2,512,512]{2,1,0:T(8,128)}, u32[]{:S(2)}) copy-start(f32[2,512,512]{2,1,0:T(8,128)} %spec.1) | copy-start | bytes 6291460
  3.7 31.7 %copy-start.2 = (f32[1,1,16,256,256]{4,3,2,1,0:T(8,128)S(1)}, f32[1,1,16,256,256]{4,3,2,1,0:T(8,128)}, u32[]{:S(2)}) copy-start(f32[1,1,16,256,256]{4,3,2,1,0:T(8,128)} %param.13) | copy-start | bytes 12582916
  3.7 31.7 %copy-start.3 = (f32[2,256,256]{2,1,0:T(8,128)S(1)}, f32[2,256,256]{2,1,0:T(8,128)}, u32[]{:S(2)}) copy-start(f32[2,256,256]{2,1,0:T(8,128)} %ill.3) | copy-start | bytes 1572868
  3.7 31.7 %copy-start.4 = (bf16[4,256,256]{2,1,0:T(8,128)(2,1)S(1)}, bf16[4,256,256]{2,1,0:T(8,128)(2,1)}, u32[]{:S(2)}) copy-start(bf16[4,256,256]{2,1,0:T(8,128)(2,1)} %constant.20.clone.mats) | copy-start | bytes 1572868
  3.7 31.7 %copy-start.5 = (bf16[256,256]{1,0:T(8,128)(2,1)S(1)}, bf16[256,256]{1,0:T(8,128)(2,1)}, u32[]{:S(2)}) copy-start(bf16[256,256]{1,0:T(8,128)(2,1)} %constant.23.clone.perm) | copy-start | bytes 393220
  3.7 31.7 %copy-start.6 = (f32[2,128,128]{2,1,0:T(8,128)S(1)}, f32[2,128,128]{2,1,0:T(8,128)}, u32[]{:S(2)}) copy-start(f32[2,128,128]{2,1,0:T(8,128)} %constant.21.clone.twr) | copy-start | bytes 393220
  35.4 3.9 %copy-start.1 = (f32[2,512,512]{2,1,0:T(8,128)S(1)}, f32[2,512,512]{2,1,0:T(8,128)}, u32[]{:S(2)}) copy-start(f32[2,512,512]{2,1,0:T(8,128)} %spec.1) | copy-start | bytes 6291460

commit v4 on v3

--- a/solution.py
+++ b/solution.py
@@ -1,5 +1,4 @@
 import math
-
 import numpy as np
 import jax, jax.numpy as jnp
 from jax import lax
@@ -11,25 +10,21 @@
 F32=jnp.float32; BF=jnp.bfloat16
 
 def consts():
-    k=np.arange(128)
-    ang=2*np.pi*np.outer(k,k)%(2*np.pi*128)/128
-    ang=2*np.pi*((np.outer(k,k))%128)/128
-    C=np.cos(ang)/16; S=np.sin(ang)/16
-    A=np.block([[C,-S],[S,C]]); B=A.T.copy()
-    def split(x):
-        x=x.astype(np.float32)
-        h=x.astype(ml_dtypes.bfloat16); l=(x-h.astype(np.float32)).astype(ml_dtypes.bfloat16)
-        return h,l
-    ah,al=split(A); bh,bl=split(B)
-    mats=np.stack([ah,al,bh,bl])
-    t=2*np.pi*np.arange(128)/256
-    c=np.cos(t).astype(np.float32); s=np.sin(t).astype(np.float32)
-    twr=np.stack([np.broadcast_to(c[:,None],(128,128)),np.broadcast_to(s[:,None],(128,128))])
-    twl=np.stack([np.broadcast_to(c[None],(16,128)),np.broadcast_to(s[None],(16,128))])
+    n=np.arange(128)
+    out=[]
+    for odd in (0,1):
+        phase=np.outer(n,2*n+odd)%256
+        ang=2*np.pi*phase/256
+        tr,ti=np.cos(ang)/16,-np.sin(ang)/16
+        r=np.block([[tr,ti],[-ti,tr]])
+        for m in (r,r.T):
+            m=m.astype(np.float32)
+            h=m.astype(ml_dtypes.bfloat16); l=(m-h.astype(np.float32)).astype(ml_dtypes.bfloat16)
+            out.append(np.stack([h,l]))
+    mats=np.stack(out).reshape(2,2,2,256,256)
     k=np.arange(256)
-    perm=np.zeros((256,256));
-    perm[k, (k%2)*128+k//2]=1
-    return mats, twr.astype(np.float32).copy(), twl.astype(np.float32).copy(), perm.astype(ml_dtypes.bfloat16)
+    perm=np.zeros((256,256)); perm[k, (k%2)*128+k//2]=1
+    return mats, perm.astype(ml_dtypes.bfloat16)
 
 def split(x):
     h=x.astype(BF)
@@ -37,14 +32,15 @@
 
 def dot(a,b): return jnp.dot(a,b,preferred_element_type=F32)
 
+
 RC=16
-def wkernel(offs, cnt, ext, ill, mats, twr, twl, perm, meas, grad, pterm,
-            mbuf, patch, wave, hi, lo, mid, msem):
+def left(mh,ml,h,l):
+    return dot(mh,h)+dot(mh,l)+dot(ml,h)
+def right(h,l,mh,ml):
+    return dot(h,mh)+dot(l,mh)+dot(h,ml)
+
+def wkernel(offs, cnt, ext, ill, mats, meas, grad, pterm, *bufs):
     n=cnt[0]
-    def cp(s,t): return pltpu.make_async_copy(meas.at[s,:,pl.ds(128*t,128)], mbuf.at[s,t], msem.at[s,t])
-    @pl.loop(0,n)
-    def _(s):
-        cp(s,0).start(); cp(s,1).start()
     @pl.loop(0,96)
     def _(i):
         for p in range(2):
@@ -52,127 +48,154 @@
                 grad[p,t,pl.ds(pl.multiple_of(8*i,8),8),:]=jnp.zeros((8,128),F32)
     pterm[...]=jnp.zeros_like(pterm)
     lane=lax.broadcasted_iota(jnp.int32,(RC,128),1)
-    @pl.loop(0,n)
-    def _(s):
+
+    def phases(s, live, bset):
+        patch, wave, h1, l1, m1, h2, l2, m2, h3, l3, m3, h4, l4, m4 = bset
         r=offs[0,s]; c=offs[1,s]
         ct=c//128; sh=c%128
         ush=(128-sh)%128
         lmask=lane<128-sh
-        for j in range(128//RC):
-            half=[]
-            for h in range(2):
-                row=h*128+j*RC
-                rr=pl.ds(row,RC)
-                x=[[pltpu.roll(ext[p,ct+t,pl.ds(r+row,RC),:],ush,1) for t in range(3)] for p in range(2)]
-                pt=[[jnp.where(lmask,x[p][t],x[p][t+1]) for t in range(2)] for p in range(2)]
-                ws=[]
+        low=lane<sh
+        def P1():
+            for j in range(128//RC):
+                half=[]
+                for h in range(2):
+                    row=h*128+j*RC
+                    rr=pl.ds(row,RC)
+                    x=[[pltpu.roll(ext[p,ct+t,pl.ds(r+row,RC),:],ush,1) for t in range(3)] for p in range(2)]
+                    pt=[[jnp.where(lmask,x[p][t],x[p][t+1]) for t in range(2)] for p in range(2)]
+                    ws=[]
+                    for t in range(2):
+                        ls=pl.ds(128*t,128)
+                        pr,pi=ill[0,rr,ls],ill[1,rr,ls]
+                        a,b=pt[0][t],pt[1][t]
+                        patch[0,rr,ls]=a; patch[1,rr,ls]=b
+                        wr=pr*a-pi*b; wi=pr*b+pi*a
+                        wave[0,rr,ls]=wr; wave[1,rr,ls]=wi
+                        ws.append((wr,wi))
+                    half.append(ws)
                 for t in range(2):
                     ls=pl.ds(128*t,128)
-                    pr,pi=ill[0,rr,ls],ill[1,rr,ls]
-                    a,b=pt[0][t],pt[1][t]
-                    patch[0,rr,ls]=a; patch[1,rr,ls]=b
-                    wr=pr*a-pi*b; wi=pr*b+pi*a
-                    wave[0,rr,ls]=wr; wave[1,rr,ls]=wi
-                    ws.append((wr,wi))
-                half.append(ws)
-            tc=twr[0,pl.ds(j*RC,RC),:]; ts=twr[1,pl.ds(j*RC,RC),:]
-            for t in range(2):
-                ls=pl.ds(128*t,128)
-                (ar,ai),(br,bi)=half[0][t],half[1][t]
-                er,ei=ar+br,ai+bi
-                dr,di=ar-br,ai-bi
-                vr=dr*tc+di*ts; vi=di*tc-dr*ts
-                for q,(xr,xi) in enumerate(((er,ei),(vr,vi))):
-                    for z,val in enumerate((xr,xi)):
-                        hh,ll=split(val)
-                        rs=pl.ds(z*128+j*RC,RC)
-                        hi[q,rs,ls]=hh; lo[q,rs,ls]=ll
-        bh=mats[2]; bl=mats[3]
-        for q in range(2):
-            mid[q]=dot(bh,hi[q])+dot(bh,lo[q])+dot(bl,hi[q])
-        lc=twl[0]; lsn=twl[1]
-        for q in range(2):
-            for j in range(128//RC):
-                ar=mid[q,pl.ds(j*RC,RC),pl.ds(0,128)]; br=mid[q,pl.ds(j*RC,RC),pl.ds(128,128)]
-                ai=mid[q,pl.ds(128+j*RC,RC),pl.ds(0,128)]; bi=mid[q,pl.ds(128+j*RC,RC),pl.ds(128,128)]
-                er,ei=ar+br,ai+bi
-                dr,di=ar-br,ai-bi
-                vr=dr*lc+di*lsn; vi=di*lc-dr*lsn
-                rs=pl.ds(q*128+j*RC,RC)
-                for e,(xr,xi) in enumerate(((er,ei),(vr,vi))):
-                    for z,val in enumerate((xr,xi)):
-                        hh,ll=split(val)
-                        hi[e,rs,pl.ds(128*z,128)]=hh; lo[e,rs,pl.ds(128*z,128)]=ll
-        ah=mats[0]; al=mats[1]
-        for e in range(2):
-            mid[e]=dot(hi[e],ah)+dot(lo[e],ah)+dot(hi[e],al)
-        cp(s,0).wait(); cp(s,1).wait()
-        pm=perm[...]
-        for q in range(2):
-            mv=jnp.concatenate([mbuf[s,t,pl.ds(q,128,stride=2),:] for t in range(2)],axis=1)
-            mh,ml=split(mv)
-            mp=dot(mh,pm)+dot(ml,pm)
+                    (ar,ai),(br,bi)=half[0][t],half[1][t]
+                    for q,(xr,xi) in enumerate(((ar+br,ai+bi),(ar-br,ai-bi))):
+                        for z,val in enumerate((xr,xi)):
+                            hh,ll=split(val)
+                            rs=pl.ds(z*128+j*RC,RC)
+                            h1[q,rs,ls]=hh; l1[q,rs,ls]=ll
+                yield
+        def M1():
+            for q in range(2):
+                m1[q]=left(mats[q,1,0],mats[q,1,1],h1[q],l1[q]); yield
+        def P2():
+            for q in range(2):
+                for j in range(128//RC):
+                    ar=m1[q,pl.ds(j*RC,RC),pl.ds(0,128)]; br=m1[q,pl.ds(j*RC,RC),pl.ds(128,128)]
+                    ai=m1[q,pl.ds(128+j*RC,RC),pl.ds(0,128)]; bi=m1[q,pl.ds(128+j*RC,RC),pl.ds(128,128)]
+                    rs=pl.ds(q*128+j*RC,RC)
+                    for e,(xr,xi) in enumerate(((ar+br,ai+bi),(ar-br,ai-bi))):
+                        for z,val in enumerate((xr,xi)):
+                            hh,ll=split(val)
+                            h2[e,rs,pl.ds(128*z,128)]=hh; l2[e,rs,pl.ds(128*z,128)]=ll
+                    yield
+        def M2():
             for e in range(2):
+                m2[e]=right(h2[e],l2[e],mats[e,0,0],mats[e,0,1]); yield
+        def P3():
+            for q in range(2):
+                for e in range(2):
+                    for j in range(128//RC):
+                        rs=pl.ds(q*128+j*RC,RC)
+                        fr=m2[e,rs,pl.ds(0,128)]; fi=m2[e,rs,pl.ds(128,128)]
+                        f=meas[s,rs,pl.ds(e*128,128)]*lax.rsqrt(jnp.maximum(fr*fr+fi*fi,0.25))
+                        for z,val in enumerate((fr*f,fi*f)):
+                            hh,ll=split(val)
+                            h3[e,rs,pl.ds(128*z,128)]=hh; l3[e,rs,pl.ds(128*z,128)]=ll
+                        yield
+        def M3():
+            for e in range(2):
+                m3[e]=right(h3[e],l3[e],mats[e,1,0],mats[e,1,1]); yield
+        def P4():
+            for q in range(2):
                 for j in range(128//RC):
                     rs=pl.ds(q*128+j*RC,RC)
-                    fr=mid[e,rs,pl.ds(0,128)]; fi=mid[e,rs,pl.ds(128,128)]
-                    m=mp[j*RC:(j+1)*RC,e*128:(e+1)*128]
-                    f=m*lax.rsqrt(jnp.maximum(fr*fr+fi*fi,0.25))
-                    for z,val in enumerate((fr*f,fi*f)):
-                        hh,ll=split(val)
-                        hi[e,rs,pl.ds(128*z,128)]=hh; lo[e,rs,pl.ds(128*z,128)]=ll
-        for e in range(2):
-            mid[e]=dot(hi[e],bh)+dot(lo[e],bh)+dot(hi[e],bl)
-        for q in range(2):
+                    er=m3[0,rs,pl.ds(0,128)]; ei=m3[0,rs,pl.ds(128,128)]
+                    vr=m3[1,rs,pl.ds(0,128)]; vi=m3[1,rs,pl.ds(128,128)]
+                    for t,(xr,xi) in enumerate(((er+vr,ei+vi),(er-vr,ei-vi))):
+                        for z,val in enumerate((xr,xi)):
+                            hh,ll=split(val)
+                            h4[q,pl.ds(z*128+j*RC,RC),pl.ds(128*t,128)]=hh
+                            l4[q,pl.ds(z*128+j*RC,RC),pl.ds(128*t,128)]=ll
+                    yield
+        def M4():
+            for q in range(2):
+                m4[q]=left(mats[q,0,0],mats[q,0,1],h4[q],l4[q]); yield
+        def P5():
             for j in range(128//RC):
-                rs=pl.ds(q*128+j*RC,RC)
-                er=mid[0,rs,pl.ds(0,128)]; ei=mid[0,rs,pl.ds(128,128)]
-                orr=mid[1,rs,pl.ds(0,128)]; oi=mid[1,rs,pl.ds(128,128)]
-                vr=orr*lc-oi*lsn; vi=oi*lc+orr*lsn
-                for t,(xr,xi) in enumerate(((er+vr,ei+vi),(er-vr,ei-vi))):
-                    for z,val in enumerate((xr,xi)):
-                        hh,ll=split(val)
-                        hi[q,pl.ds(z*128+j*RC,RC),pl.ds(128*t,128)]=hh
-                        lo[q,pl.ds(z*128+j*RC,RC),pl.ds(128*t,128)]=ll
-        for q in range(2):
-            mid[q]=dot(ah,hi[q])+dot(ah,lo[q])+dot(al,hi[q])
-        for j in range(128//RC):
-            tc=twr[0,pl.ds(j*RC,RC),:]; ts=twr[1,pl.ds(j*RC,RC),:]
-            g=[[[None]*2 for _ in range(2)] for _ in range(2)]
-            for t in range(2):
-                ls=pl.ds(128*t,128)
-                er=mid[0,pl.ds(j*RC,RC),ls]; ei=mid[0,pl.ds(128+j*RC,RC),ls]
-                orr=mid[1,pl.ds(j*RC,RC),ls]; oi=mid[1,pl.ds(128+j*RC,RC),ls]
-                vr=orr*tc-oi*ts; vi=oi*tc+orr*ts
-                for h,(xr,xi) in enumerate(((er+vr,ei+vi),(er-vr,ei-vi))):
-                    rr=pl.ds(h*128+j*RC,RC)
-                    cr=xr-wave[0,rr,ls]; ci=xi-wave[1,rr,ls]
-                    a,b=patch[0,rr,ls],patch[1,rr,ls]
-                    pterm[0,t,rr,:]+=a*cr+b*ci
-                    pterm[1,t,rr,:]+=a*ci-b*cr
-                    pr,pi=ill[0,rr,ls],ill[1,rr,ls]
-                    g[h][0][t]=pr*cr+pi*ci
-                    g[h][1][t]=pr*ci-pi*cr
-            for h in range(2):
-                for z in range(2):
-                    rg=[pltpu.roll(g[h][z][t],sh,1) for t in range(2)]
-                    low=lane<sh
-                    rows=pl.ds(r+h*128+j*RC,RC)
-                    grad[z,ct,rows,:]+=jnp.where(low,0.0,rg[0])
-                    grad[z,ct+1,rows,:]+=jnp.where(low,rg[0],rg[1])
-                    grad[z,ct+2,rows,:]+=jnp.where(low,rg[1],0.0)
-
-def windows(offs,cnt,ext,ill,meas):
-    mats,twr,twl,perm=consts()
+                g=[[[None]*2 for _ in range(2)] for _ in range(2)]
+                for t in range(2):
+                    ls=pl.ds(128*t,128)
+                    er=m4[0,pl.ds(j*RC,RC),ls]; ei=m4[0,pl.ds(128+j*RC,RC),ls]
+                    vr=m4[1,pl.ds(j*RC,RC),ls]; vi=m4[1,pl.ds(128+j*RC,RC),ls]
+                    for h,(xr,xi) in enumerate(((er+vr,ei+vi),(er-vr,ei-vi))):
+                        rr=pl.ds(h*128+j*RC,RC)
+                        cr=xr-wave[0,rr,ls]; ci=xi-wave[1,rr,ls]
+                        if live is not None:
+                            cr=cr*live; ci=ci*live
+                        a,b=patch[0,rr,ls],patch[1,rr,ls]
+                        pterm[0,t,rr,:]+=a*cr+b*ci
+                        pterm[1,t,rr,:]+=a*ci-b*cr
+                        pr,pi=ill[0,rr,ls],ill[1,rr,ls]
+                        g[h][0][t]=pr*cr+pi*ci
+                        g[h][1][t]=pr*ci-pi*cr
+                for h in range(2):
+                    for z in range(2):
+                        rg=[pltpu.roll(g[h][z][t],sh,1) for t in range(2)]
+                        rows=pl.ds(r+h*128+j*RC,RC)
+                        grad[z,ct,rows,:]+=jnp.where(low,0.0,rg[0])
+                        grad[z,ct+1,rows,:]+=jnp.where(low,rg[0],rg[1])
+                        grad[z,ct+2,rows,:]+=jnp.where(low,rg[1],0.0)
+                yield
+        return P1,M1,P2,M2,P3,M3,P4,M4,P5
+
+    def together(m, p):
+        m, p = list_len(m), list_len(p)
+        mi, pi_ = iter(m[0]()), iter(p[0]())
+        for k in range(m[1]):
+            next(mi, None)
+            for _ in range(-(-p[1]//m[1])):
+                next(pi_, None)
+        for _ in mi: pass
+        for _ in pi_: pass
+    COUNT={"P1":128//RC,"P2":256//RC,"P3":512//RC,"P4":256//RC,"P5":128//RC,"M1":2,"M2":2,"M3":2,"M4":2}
+    def list_len(f): return f, COUNT[f.__name__]
+    def alone(f):
+        for _ in f(): pass
+    half=len(bufs)//2
+
+    @pl.loop(0,(n+1)//2)
+    def _(k):
+        S=[]
+        for i in range(2):
+            s=jnp.minimum(2*k+i,15)
+            live=None if i==0 else jnp.where(2*k+i<n,1.0,0.0).astype(F32)
+            S.append(phases(s,live,bufs[half*i:half*(i+1)]))
+        A,Bp=S
+        alone(A[0])
+        for i in range(4):
+            together(A[2*i+1],Bp[2*i])
+            together(Bp[2*i+1],A[2*i+2])
+        alone(Bp[8])
+
+def windows(offs,cnt,ext,ill,mats,meas):
     V=pl.BlockSpec(memory_space=pltpu.VMEM); Sm=pl.BlockSpec(memory_space=pltpu.SMEM)
+    W=pltpu.VMEM((2,256,256),F32); Bq=pltpu.VMEM((2,256,256),BF)
     return pl.pallas_call(wkernel,
         out_shape=(jax.ShapeDtypeStruct((2,6,768,128),F32),jax.ShapeDtypeStruct((2,2,256,128),F32)),
-        in_specs=[Sm,Sm,V,V,V,V,V,V,pl.BlockSpec(memory_space=pl.ANY)],
+        in_specs=[Sm,Sm,V,V,V,V],
         out_specs=(V,V),
-        scratch_shapes=[pltpu.VMEM((16,2,256,128),F32),pltpu.VMEM((2,256,256),F32),pltpu.VMEM((2,256,256),F32),
-            pltpu.VMEM((2,256,256),BF),pltpu.VMEM((2,256,256),BF),pltpu.VMEM((2,256,256),F32),pltpu.SemaphoreType.DMA((16,2))],
-        compiler_params=pltpu.CompilerParams(vmem_limit_bytes=28*2**20),
-    )(offs,cnt,ext,ill,jnp.asarray(mats),jnp.asarray(twr),jnp.asarray(twl),jnp.asarray(perm),meas)
+        scratch_shapes=([W,W]+[Bq,Bq,W]*4)*2,
+        compiler_params=pltpu.CompilerParams(vmem_limit_bytes=36*2**20),
+    )(offs,cnt,ext,ill,mats,meas)
 
 
 MESH = pl.DeviceIdType.MESH
@@ -212,12 +235,21 @@
 OPPOSITE = {"up": "down", "down": "up", "left": "right", "right": "left"}
 
 
-def halo_kernel(tile, ext, own_sem, row_send, row_recv, col_send, col_recv, cor_send, cor_recv):
+def halo_kernel(tile, meas, perm, ext, sorted_meas, mbuf, meas_sem, own_sem, row_send, row_recv, col_send, col_recv, cor_send, cor_recv):
     a, b, has, ids = neighbours()
     barrier, expected = greet([(has[k], ids[k]) for k in ids])
     own = [pltpu.make_async_copy(tile.at[:, :, pl.ds(128 * t, 128)], ext.at[:, 1 + t, pl.ds(128, 512), :], own_sem.at[t]) for t in range(4)]
     for copy in own:
         copy.start()
+
+    def fetch(s, t):
+        return pltpu.make_async_copy(meas.at[s, :, pl.ds(128 * t, 128)], mbuf.at[s, t], meas_sem.at[s, t])
+
+    @pl.loop(0, 16)
+    def _(s):
+        for t in range(2):
+            fetch(s, t).start()
+
     pl.semaphore_wait(barrier, expected)
     rows, cols, corners = {}, {}, {}
     for i, way in enumerate(("down", "up")):
@@ -241,6 +273,16 @@
             pl.when(has[way])(rows[way, t].start)
     for way in ("right", "left"):
         pl.when(has[way])(cols[way].start)
+
+    @pl.loop(0, 16)
+    def _(s):
+        for t in range(2):
+            fetch(s, t).wait()
+        for q in range(2):
+            picked = jnp.concatenate([mbuf[s, t, pl.ds(q, 128, stride=2), :] for t in range(2)], axis=1)
+            high, low = split(picked)
+            sorted_meas[s, pl.ds(128 * q, 128), :] = dot(high, perm[...]) + dot(low, perm[...])
+
     for j, way in enumerate(("down", "up")):
         @pl.when(has[OPPOSITE[way]])
         def _(way=way):
@@ -263,16 +305,18 @@
             pl.when(jnp.logical_and(has[side], has[OPPOSITE[way]]))(corners[side, j].wait_send)
 
 
-def halo(tile):
+def halo(tile, meas, perm):
     D = pltpu.SemaphoreType.DMA
-    A = pl.BlockSpec(memory_space=pl.ANY)
+    H = pl.BlockSpec(memory_space=pltpu.HBM)
+    V = pl.BlockSpec(memory_space=pltpu.VMEM)
     return pl.pallas_call(
         halo_kernel,
-        out_shape=jax.ShapeDtypeStruct((2, 6, 768, 128), F32),
-        in_specs=[A], out_specs=pl.BlockSpec(memory_space=pltpu.VMEM),
-        scratch_shapes=[D((4,)), D((2, 4)), D((2, 4)), D((2,)), D((2,)), D((2, 2)), D((2, 2))],
+        out_shape=(jax.ShapeDtypeStruct((2, 6, 768, 128), F32), jax.ShapeDtypeStruct((16, 256, 256), F32)),
+        in_specs=[H, H, V], out_specs=(V, V),
+        scratch_shapes=[pltpu.VMEM((16, 2, 256, 128), F32), D((16, 2)),
+                        D((4,)), D((2, 4)), D((2, 4)), D((2,)), D((2,)), D((2, 2)), D((2, 2))],
         compiler_params=pltpu.CompilerParams(collective_id=1, has_side_effects=True, vmem_limit_bytes=24 * 2**20),
-    )(tile)
+    )(tile, meas, perm)
 
 
 def partners(b):
@@ -437,8 +481,9 @@
 def shards(specimen, illumination, scan_offsets, slot_counts, measured):
     anchor = jnp.stack([lax.axis_index("ty") * 512, lax.axis_index("tx") * 512]) - 128
     local = scan_offsets[0, 0] - anchor[:, None]
-    ext = halo(specimen)
-    grad, probe_term = windows(local, slot_counts[0], ext, illumination, measured[0, 0])
+    mats, perm = consts()
+    ext, moduli = halo(specimen, measured[0, 0], jnp.asarray(perm))
+    grad, probe_term = windows(local, slot_counts[0], ext, illumination, jnp.asarray(mats), moduli)
     return finish(specimen, illumination, grad, probe_term.reshape(2, 4, 16, 8, 128))
 
 

time: 131 us -> 116 us (0.89)
  Pallas kernels: 125 us -> 106 us
  local copies, waits for them, and re-layouts: 3.74 us -> 6.81 us
    pallas_call x1, Pallas kernels: 89.2 us -> 59.4 us  [finish(): pl.pallas_call(finish_kernel, out_shape=(jax.ShapeDtypeStruct((2, 512, 51...]
    pallas_call x1, Pallas kernels: 3.91 us -> 15.2 us  [windows(): pl.pallas_call(wkernel, out_shape=(jax.ShapeDtypeStruct((2, 6, 768, 128),...]
    unnamed x18 -> x14, local copies, waits for them, and re-layouts: 3.74 us -> 6.81 us
where the time goes in v4:
time: 116 us; the launch traced here: 115 us
  Pallas kernels  106 us (91%)
  local copies, waits for them, and re-layouts  6.81 us (6%)
  between operations  1.34 us (1%)
    pallas_call x1, Pallas kernels, finish(): pl.pallas_call(finish_kernel, out_shape=(jax.ShapeDtypeStruct((2, 512, 51...  59.4 us
    pallas_call x1, Pallas kernels, halo(): pl.pallas_call(halo_kernel, out_shape=(jax.ShapeDtypeStruct((2, 6, 768, 1...  31.7 us
    pallas_call x1, Pallas kernels, windows(): pl.pallas_call(wkernel, out_shape=(jax.ShapeDtypeStruct((2, 6, 768, 128),...  15.2 us
    unnamed x14, local copies, waits for them, and re-layouts  6.81 us

profile of v4, /device:TPU:1, one launch (start us, length us, event | category | flops | bytes accessed | tf_op | source)
XLA Modules:
  0.0 115.4 jit_solution(15891079038349219191)
XLA Ops:
  1.3 0.1 add_add_fusion
  1.4 0.7 bitcast_subtract_fusion.offs
  2.1 0.0 copy-start
  2.1 1.6 %copy-done = f32[2,512,512]{2,1,0:T(8,128)S(1)} copy-done((f32[2,512,512]{2,1,0:T(8,128)S(1)}, f32[2,512,512]{2,1,0:T(8,128)}, u32[]{:S(2)}) %copy-start) | copy-done | bytes 2097176
  3.7 0.0 copy-start.2
  3.7 2.2 %copy-done.2 = f32[1,1,16,256,256]{4,3,2,1,0:T(8,128)S(1)} copy-done((f32[1,1,16,256,256]{4,3,2,1,0:T(8,128)S(1)}, f32[1,1,16,256,256]{4,3,2,1,0:T(8,128)}, u32[]{:S(2)}) %copy-start.2) | copy-done | bytes 4194328
  5.9 0.0 copy-start.5
  5.9 0.9 copy-done.5
  6.8 0.0 copy-start.3
  6.8 0.0 copy-start.4
  6.8 31.7 %shard_map.86 = (f32[2,6,768,128]{3,2,1,0:T(8,128)S(1)}, f32[16,256,256]{2,1,0:T(8,128)S(1)}) custom-call(f32[2,512,512]{2,1,0:T(8,128)S(1)} %copy-done, f32[16,256,256]{2,1,0:T(8,128)S(1)} %bitcast.8, bf16[256,256]{1,0:T(8,128)(2,1)S(1)} %copy-done.5), custom_call_target="tpu_custom_call" | custom-call | tf_op jit(solution)/shard_map/pallas_call | solution.py:312
  38.6 0.0 copy-done.3
  38.6 0.0 copy-done.4
  38.6 0.0 copy-start.1
  38.6 15.2 %shard_map.87 = (f32[2,6,768,128]{3,2,1,0:T(8,128)S(1)}, f32[2,2,256,128]{3,2,1,0:T(8,128)S(1)}) custom-call(s32[2,16]{1,0:T(2,128)S(1)} %bitcast_subtract_fusion.offs, s32[1]{0:T(128)} %bitcast.7.cnt, f32[2,6,768,128]{3,2,1,0:T(8,128)S(1)} %get-tuple-element.6.ext, f32[2,256,256]{2,1,0:T(8,128)S(1)} %copy-done.3, ...), custom_call_target="tpu_custom_call" | custom-call | tf_op jit(solution)/shard_map/pallas_call | solution.py:192
  53.8 0.0 copy-done.1
  53.8 59.4 %shard_map.88 = (f32[2,512,512]{2,1,0:T(8,128)S(1)}, f32[2,256,256]{2,1,0:T(8,128)S(1)}) custom-call(f32[2,512,512]{2,1,0:T(8,128)S(1)} %copy-done.1, f32[2,256,256]{2,1,0:T(8,128)S(1)} %copy-done.3, f32[2,6,768,128]{3,2,1,0:T(8,128)S(1)} %get-tuple-element.8.grad, f32[2,4,16,8,128]{4,3,2,1,0:T(8,128)S(1)} %bitcast.9), custom_call_target="tpu_custom_call" | custom-call | tf_op jit(solution)/shard_map/pallas_call | solution.py:465
  113.2 1.3 %copy.12 = f32[2,512,512]{2,1,0:T(8,128)} copy(f32[2,512,512]{2,1,0:T(8,128)S(1)} %get-tuple-element.12) | data formatting | bytes 4194304
  114.6 0.8 copy.13
Async XLA Ops:
  2.1 1.6 %copy-start = (f32[2,512,512]{2,1,0:T(8,128)S(1)}, f32[2,512,512]{2,1,0:T(8,128)}, u32[]{:S(2)}) copy-start(f32[2,512,512]{2,1,0:T(8,128)} %spec.1) | copy-start | bytes 6291460
  3.7 2.2 %copy-start.2 = (f32[1,1,16,256,256]{4,3,2,1,0:T(8,128)S(1)}, f32[1,1,16,256,256]{4,3,2,1,0:T(8,128)}, u32[]{:S(2)}) copy-start(f32[1,1,16,256,256]{4,3,2,1,0:T(8,128)} %param.11) | copy-start | bytes 12582916
  5.9 0.9 copy-start.5
  6.8 31.8 %copy-start.3 = (f32[2,256,256]{2,1,0:T(8,128)S(1)}, f32[2,256,256]{2,1,0:T(8,128)}, u32[]{:S(2)}) copy-start(f32[2,256,256]{2,1,0:T(8,128)} %ill.3) | copy-start | bytes 1572868
  6.8 31.8 %copy-start.4 = (bf16[2,2,2,256,256]{4,3,2,1,0:T(8,128)(2,1)S(1)}, bf16[2,2,2,256,256]{4,3,2,1,0:T(8,128)(2,1)}, u32[]{:S(2)}) copy-start(bf16[2,2,2,256,256]{4,3,2,1,0:T(8,128)(2,1)} %constant.17.clone.mats) | copy-start | bytes 3145732
  38.6 15.2 %copy-start.1 = (f32[2,512,512]{2,1,0:T(8,128)S(1)}, f32[2,512,512]{2,1,0:T(8,128)}, u32[]{:S(2)}) copy-start(f32[2,512,512]{2,1,0:T(8,128)} %spec.1) | copy-start | bytes 6291460

commit v5 on v4

--- a/solution.py
+++ b/solution.py
@@ -353,8 +353,7 @@
     inv = 1.0 / power
     pl.semaphore_wait(barrier, expected + 31)
     first = remote(pterm.at[1 - core], rcore, core_s, core_r, other)
-    first.start()
-    corner, middle, zmid, zedge = {}, {}, {}, {}
+    corner, middle, vert = {}, {}, {}
     for i, side in enumerate(("right", "left")):
         src_t = 5 if side == "right" else 0
         for j, row in enumerate((0, 640)):
@@ -363,31 +362,31 @@
         middle[side] = remote(grad.at[:, src_t, pl.ds(128, 512), :], rxm.at[i], ms.at[i], mr.at[i], ids[side])
     for j, way in enumerate(("up", "down")):
         row = 0 if way == "up" else 640
-        zmid[way] = remote(grad.at[:, pl.ds(2, 2), pl.ds(row, 128), :], rz.at[j, :, pl.ds(1, 2)],
-                           zs.at[j, 1], zr.at[j, 1], ids[way])
-        for k, t in ((0, 0), (2, 3)):
-            zedge[way, k] = remote(edge.at[j, k // 2], rz.at[j, :, t], zs.at[j, k], zr.at[j, k], ids[way])
-    for side in ("right", "left"):
-        for j in range(2):
-            pl.when(has[side])(corner[side, j].start)
-    for way in ("up", "down"):
-        pl.when(has[way])(zmid[way].start)
+        for t in range(4):
+            src = edge.at[j, t // 3] if t in (0, 3) else grad.at[:, 1 + t, pl.ds(row, 128), :]
+            vert[way, t] = remote(src, rz.at[j, :, t], zs.at[j, t], zr.at[j, t], ids[way])
+
+    def send_vert(t):
+        for way in ("up", "down"):
+            pl.when(has[way])(vert[way, t].start)
+
+    def add_vert(t):
+        for j, (way, row) in enumerate((("up", 384), ("down", 0))):
+            @pl.when(has[OPPOSITE[way]])
+            def _(j=j, way=way, row=row):
+                vert[way, t].wait_recv()
+                newspec[:, row:row + 128, 128 * t:128 * t + 128] += inv * rz[j, :, t]
+
+    first.start()
+    send_vert(1)
     first.wait_recv()
     sumc[...] = pterm[core] + rcore[...]
     xsend = [remote(sumc.at[(x + d) % 4], rx.at[d - 1], xs.at[d - 1], xr.at[d - 1], mates[d - 1]) for d in (1, 2, 3)]
     for copy in xsend:
         copy.start()
     for side in ("right", "left"):
-        pl.when(has[side])(middle[side].start)
-    for j, row in enumerate((0, 640)):
-        for k, (t, side) in enumerate(((1, "right"), (4, "left"))):
-            edge[j, k] = grad[:, t, row:row + 128, :]
-            @pl.when(has[OPPOSITE[side]])
-            def _(j=j, k=k, side=side):
-                corner[side, j].wait_recv()
-                edge[j, k] += rxc[k, j]
-            way = "up" if j == 0 else "down"
-            pl.when(has[way])(zedge[way, 2 * k].start)
+        for j in range(2):
+            pl.when(has[side])(corner[side, j].start)
     for copy in xsend:
         copy.wait_recv()
     part[...] = sumc[x] + rx[0] + rx[1] + rx[2]
@@ -396,6 +395,10 @@
     def _(d):
         device = member(d)
         remote(part.at[device[0]], rc.at[d - 1], us, ur, device).start()
+
+    send_vert(2)
+    for side in ("right", "left"):
+        pl.when(has[side])(middle[side].start)
 
     @pl.loop(0, 16)
     def _(i):
@@ -406,6 +409,13 @@
                 lanes = pl.ds(128 * t, 128)
                 newspec[p, rows, lanes] = spec[p, rows, lanes] + inv * grad[p, 1 + t, more, :]
 
+    for j, row in enumerate((0, 640)):
+        for k, (t, side) in enumerate(((1, "right"), (4, "left"))):
+            edge[j, k] = grad[:, t, row:row + 128, :]
+            @pl.when(has[OPPOSITE[side]])
+            def _(j=j, k=k, side=side):
+                corner[side, j].wait_recv()
+                edge[j, k] += rxc[k, j]
     whole = remote(rc, rc, us, ur, other)
     whole.wait_recv()
     acc = part[a]
@@ -417,6 +427,8 @@
     def _(d):
         remote(total.at[core, x, a], total.at[core, x, a], ds, dr, ((a + d) % 16, b)).start()
 
+    send_vert(0)
+    send_vert(3)
     for k, (side, t) in enumerate((("right", 0), ("left", 3))):
         @pl.when(has[OPPOSITE[side]])
         def _(k=k, side=side, t=t):
@@ -427,23 +439,19 @@
     gather = [remote(total.at[core, x], total.at[core, x], es.at[d - 1], er.at[d - 1], mates[d - 1]) for d in (1, 2, 3)]
     for copy in gather:
         copy.start()
+    add_vert(1)
+    add_vert(2)
     for copy in gather:
         copy.wait_recv()
     last = remote(total.at[core], total.at[core], fs, fr, other)
     last.start()
-    for j, (way, row) in enumerate((("up", 384), ("down", 0))):
-        @pl.when(has[OPPOSITE[way]])
-        def _(j=j, way=way, row=row):
-            zmid[way].wait_recv()
-            zedge[way, 0].wait_recv()
-            zedge[way, 2].wait_recv()
-            for t in range(4):
-                newspec[:, row:row + 128, 128 * t:128 * t + 128] += inv * rz[j, :, t]
     last.wait()
     for p in range(2):
         for s in range(4):
             rows, lanes = pl.ds((s % 2) * 128, 128), pl.ds((s // 2) * 128, 128)
             newill[p, rows, lanes] = ill[p, rows, lanes] + total[p, s].reshape(128, 128) * (1.0 / 64)
+    add_vert(0)
+    add_vert(3)
     first.wait_send()
     for copy in xsend + gather:
         copy.wait_send()
@@ -454,9 +462,8 @@
             pl.when(has[side])(corner[side, j].wait_send)
         pl.when(has[side])(middle[side].wait_send)
     for way in ("up", "down"):
-        pl.when(has[way])(zmid[way].wait_send)
-        for k in (0, 2):
-            pl.when(has[way])(zedge[way, k].wait_send)
+        for t in range(4):
+            pl.when(has[way])(vert[way, t].wait_send)
 
 
 def finish(spec, ill, grad, pterm):
@@ -471,7 +478,7 @@
             pltpu.VMEM((2, 2, 4, 128, 128), F32), pltpu.VMEM((2, 2, 2, 128, 128), F32),
             pltpu.VMEM((4, 16, 8, 128), F32), pltpu.VMEM((3, 16, 8, 128), F32), pltpu.VMEM((4, 16, 8, 128), F32),
             pltpu.VMEM((16, 8, 128), F32), pltpu.VMEM((31, 8, 128), F32), pltpu.VMEM((2, 4, 16, 8, 128), F32),
-            D, D, D((3,)), D((3,)), D((2, 2)), D((2, 2)), D((2,)), D((2,)), D((2, 3)), D((2, 3)),
+            D, D, D((3,)), D((3,)), D((2, 2)), D((2, 2)), D((2,)), D((2,)), D((2, 4)), D((2, 4)),
             D, D, D, D, D((3,)), D((3,)), D, D,
         ],
         compiler_params=pltpu.CompilerParams(collective_id=2, has_side_effects=True, vmem_limit_bytes=32 * 2**20),

time: 116 us -> 111 us (0.957)
  Pallas kernels: 106 us -> 102 us
    pallas_call x1, Pallas kernels: 15.2 us -> 3.99 us  [windows(): pl.pallas_call(wkernel, out_shape=(jax.ShapeDtypeStruct((2, 6, 768, 128),...]
    pallas_call x1, Pallas kernels: 59.4 us -> 66.4 us  [finish(): pl.pallas_call(finish_kernel, out_shape=(jax.ShapeDtypeStruct((2, 512, 51...]
where the time goes in v5:
time: 111 us
  Pallas kernels  102 us (92%)
  local copies, waits for them, and re-layouts  6.81 us (6%)
  between operations  1.34 us (1%)
    pallas_call x1, Pallas kernels, finish(): pl.pallas_call(finish_kernel, out_shape=(jax.ShapeDtypeStruct((2, 512, 51...  66.4 us
    pallas_call x1, Pallas kernels, halo(): pl.pallas_call(halo_kernel, out_shape=(jax.ShapeDtypeStruct((2, 6, 768, 1...  31.7 us
    unnamed x14, local copies, waits for them, and re-layouts  6.81 us
    pallas_call x1, Pallas kernels, windows(): pl.pallas_call(wkernel, out_shape=(jax.ShapeDtypeStruct((2, 6, 768, 128),...  3.99 us

profile of v5, /device:TPU:1, one launch (start us, length us, event | category | flops | bytes accessed | tf_op | source)
XLA Modules:
  0.0 111.1 jit_solution(13364550342457102052)
XLA Ops:
  1.3 0.1 add_add_fusion
  1.4 0.7 bitcast_subtract_fusion.offs
  2.1 0.0 copy-start
  2.1 1.6 %copy-done = f32[2,512,512]{2,1,0:T(8,128)S(1)} copy-done((f32[2,512,512]{2,1,0:T(8,128)S(1)}, f32[2,512,512]{2,1,0:T(8,128)}, u32[]{:S(2)}) %copy-start) | copy-done | bytes 2097176
  3.7 0.0 copy-start.2
  3.7 2.2 %copy-done.2 = f32[1,1,16,256,256]{4,3,2,1,0:T(8,128)S(1)} copy-done((f32[1,1,16,256,256]{4,3,2,1,0:T(8,128)S(1)}, f32[1,1,16,256,256]{4,3,2,1,0:T(8,128)}, u32[]{:S(2)}) %copy-start.2) | copy-done | bytes 4194328
  5.9 0.0 copy-start.5
  5.9 0.9 copy-done.5
  6.8 0.0 copy-start.3
  6.8 0.0 copy-start.4
  6.8 31.7 %shard_map.86 = (f32[2,6,768,128]{3,2,1,0:T(8,128)S(1)}, f32[16,256,256]{2,1,0:T(8,128)S(1)}) custom-call(f32[2,512,512]{2,1,0:T(8,128)S(1)} %copy-done, f32[16,256,256]{2,1,0:T(8,128)S(1)} %bitcast.8, bf16[256,256]{1,0:T(8,128)(2,1)S(1)} %copy-done.5), custom_call_target="tpu_custom_call" | custom-call | tf_op jit(solution)/shard_map/pallas_call | solution.py:312
  38.6 0.0 copy-done.3
  38.6 0.0 copy-done.4
  38.6 0.0 copy-start.1
  38.6 4.0 %shard_map.87 = (f32[2,6,768,128]{3,2,1,0:T(8,128)S(1)}, f32[2,2,256,128]{3,2,1,0:T(8,128)S(1)}) custom-call(s32[2,16]{1,0:T(2,128)S(1)} %bitcast_subtract_fusion.offs, s32[1]{0:T(128)} %bitcast.7.cnt, f32[2,6,768,128]{3,2,1,0:T(8,128)S(1)} %get-tuple-element.6.ext, f32[2,256,256]{2,1,0:T(8,128)S(1)} %copy-done.3, ...), custom_call_target="tpu_custom_call" | custom-call | tf_op jit(solution)/shard_map/pallas_call | solution.py:192
  42.6 0.0 copy-done.1
  42.6 66.4 %shard_map.88 = (f32[2,512,512]{2,1,0:T(8,128)S(1)}, f32[2,256,256]{2,1,0:T(8,128)S(1)}) custom-call(f32[2,512,512]{2,1,0:T(8,128)S(1)} %copy-done.1, f32[2,256,256]{2,1,0:T(8,128)S(1)} %copy-done.3, f32[2,6,768,128]{3,2,1,0:T(8,128)S(1)} %get-tuple-element.8.grad, f32[2,4,16,8,128]{4,3,2,1,0:T(8,128)S(1)} %bitcast.9), custom_call_target="tpu_custom_call" | custom-call | tf_op jit(solution)/shard_map/pallas_call | solution.py:472
  109.0 1.3 %copy.12 = f32[2,512,512]{2,1,0:T(8,128)} copy(f32[2,512,512]{2,1,0:T(8,128)S(1)} %get-tuple-element.12) | data formatting | bytes 4194304
  110.3 0.8 copy.13
Async XLA Ops:
  2.1 1.6 %copy-start = (f32[2,512,512]{2,1,0:T(8,128)S(1)}, f32[2,512,512]{2,1,0:T(8,128)}, u32[]{:S(2)}) copy-start(f32[2,512,512]{2,1,0:T(8,128)} %spec.1) | copy-start | bytes 6291460
  3.7 2.2 %copy-start.2 = (f32[1,1,16,256,256]{4,3,2,1,0:T(8,128)S(1)}, f32[1,1,16,256,256]{4,3,2,1,0:T(8,128)}, u32[]{:S(2)}) copy-start(f32[1,1,16,256,256]{4,3,2,1,0:T(8,128)} %param.11) | copy-start | bytes 12582916
  5.9 0.9 copy-start.5
  6.8 31.8 %copy-start.3 = (f32[2,256,256]{2,1,0:T(8,128)S(1)}, f32[2,256,256]{2,1,0:T(8,128)}, u32[]{:S(2)}) copy-start(f32[2,256,256]{2,1,0:T(8,128)} %ill.3) | copy-start | bytes 1572868
  6.8 31.8 %copy-start.4 = (bf16[2,2,2,256,256]{4,3,2,1,0:T(8,128)(2,1)S(1)}, bf16[2,2,2,256,256]{4,3,2,1,0:T(8,128)(2,1)}, u32[]{:S(2)}) copy-start(bf16[2,2,2,256,256]{4,3,2,1,0:T(8,128)(2,1)} %constant.17.clone.mats) | copy-start | bytes 3145732
  38.6 4.0 %copy-start.1 = (f32[2,512,512]{2,1,0:T(8,128)S(1)}, f32[2,512,512]{2,1,0:T(8,128)}, u32[]{:S(2)}) copy-start(f32[2,512,512]{2,1,0:T(8,128)} %spec.1) | copy-start | bytes 6291460

commit v6 on v5

v6 whole, which is shorter than its diff:
```python
import math
import numpy as np
import jax, jax.numpy as jnp
from jax import lax
from jax.experimental import pallas as pl
from jax.experimental.pallas import tpu as pltpu
from jax.sharding import PartitionSpec as P
import ml_dtypes

F32 = jnp.float32
BF = jnp.bfloat16
MESH = pl.DeviceIdType.MESH
NEAR = 10


def consts():
    n = np.arange(128)
    out = []
    for odd in (0, 1):
        angle = 2 * np.pi * (np.outer(n, 2 * n + odd) % 256) / 256
        real, imag = np.cos(angle) / 16, -np.sin(angle) / 16
        block = np.block([[real, imag], [-imag, real]])
        for m in (block, block.T):
            m = m.astype(np.float32)
            high = m.astype(ml_dtypes.bfloat16)
            low = (m - high.astype(np.float32)).astype(ml_dtypes.bfloat16)
            out.append(np.stack([high, low]))
    mats = np.stack(out).reshape(2, 2, 2, 256, 256)
    k = np.arange(256)
    perm = np.zeros((256, 256))
    perm[k, (k % 2) * 128 + k // 2] = 1
    return mats, perm.astype(ml_dtypes.bfloat16)


def split(x):
    high = x.astype(BF)
    return high, (x - high.astype(F32)).astype(BF)


def dot(a, b):
    return jnp.dot(a, b, preferred_element_type=F32)


def left(mats, high, low):
    x = dot(jnp.concatenate([mats[0], mats[1]], axis=0), high)
    return x[:256] + x[256:] + dot(mats[0], low)


def right(high, low, mats):
    x = dot(jnp.concatenate([high, low], axis=0), mats[0])
    return x[:256] + x[256:] + dot(high, mats[1])


BUFFERS = 14


def buffers():
    whole = pltpu.VMEM((2, 256, 256), F32)
    half = pltpu.VMEM((2, 256, 256), BF)
    return [whole, whole] + [half, half, whole] * 4


def stages(slot, row, col, live, source, ill, mats, moduli, pterm, place, bufs):
    patch, wave, h1, l1, m1, h2, l2, m2, h3, l3, m3, h4, l4, m4 = bufs
    tile = col // 128
    shift = col % 128
    back = (128 - shift) % 128
    lane = lax.broadcasted_iota(jnp.int32, (128, 128), 1)

    def cut():
        halves = []
        for h in range(2):
            rows = pl.ds(h * 128, 128)
            x = [[pltpu.roll(source[p, tile + t, pl.ds(row + h * 128, 128), :], back, 1) for t in range(3)]
                 for p in range(2)]
            picked = [[jnp.where(lane < 128 - shift, x[p][t], x[p][t + 1]) for t in range(2)] for p in range(2)]
            waves = []
            for t in range(2):
                lanes = pl.ds(128 * t, 128)
                pr, pi = ill[0, rows, lanes], ill[1, rows, lanes]
                a, b = picked[0][t], picked[1][t]
                patch[0, rows, lanes] = a
                patch[1, rows, lanes] = b
                wr, wi = pr * a - pi * b, pr * b + pi * a
                wave[0, rows, lanes] = wr
                wave[1, rows, lanes] = wi
                waves.append((wr, wi))
            halves.append(waves)
        for t in range(2):
            lanes = pl.ds(128 * t, 128)
            (ar, ai), (br, bi) = halves[0][t], halves[1][t]
            for q, pair in enumerate(((ar + br, ai + bi), (ar - br, ai - bi))):
                for z, value in enumerate(pair):
                    rows = pl.ds(z * 128, 128)
                    h1[q, rows, lanes], l1[q, rows, lanes] = split(value)

    def rows_forward():
        for q in range(2):
            m1[q] = left(mats.at[q, 1], h1[q], l1[q])

    def between_forward():
        for q in range(2):
            ar, br = m1[q, pl.ds(0, 128), pl.ds(0, 128)], m1[q, pl.ds(0, 128), pl.ds(128, 128)]
            ai, bi = m1[q, pl.ds(128, 128), pl.ds(0, 128)], m1[q, pl.ds(128, 128), pl.ds(128, 128)]
            rows = pl.ds(q * 128, 128)
            for e, pair in enumerate(((ar + br, ai + bi), (ar - br, ai - bi))):
                for z, value in enumerate(pair):
                    lanes = pl.ds(z * 128, 128)
                    h2[e, rows, lanes], l2[e, rows, lanes] = split(value)

    def columns_forward():
        for e in range(2):
            m2[e] = right(h2[e], l2[e], mats.at[e, 0])

    def project():
        for q in range(2):
            for e in range(2):
                rows = pl.ds(q * 128, 128)
                fr, fi = m2[e, rows, pl.ds(0, 128)], m2[e, rows, pl.ds(128, 128)]
                f = moduli[slot, rows, pl.ds(e * 128, 128)] * lax.rsqrt(jnp.maximum(fr * fr + fi * fi, 0.25))
                for z, value in enumerate((fr * f, fi * f)):
                    lanes = pl.ds(z * 128, 128)
                    h3[e, rows, lanes], l3[e, rows, lanes] = split(value)

    def columns_back():
        for e in range(2):
            m3[e] = right(h3[e], l3[e], mats.at[e, 1])

    def between_back():
        for q in range(2):
            rows = pl.ds(q * 128, 128)
            er, ei = m3[0, rows, pl.ds(0, 128)], m3[0, rows, pl.ds(128, 128)]
            vr, vi = m3[1, rows, pl.ds(0, 128)], m3[1, rows, pl.ds(128, 128)]
            for t, pair in enumerate(((er + vr, ei + vi), (er - vr, ei - vi))):
                for z, value in enumerate(pair):
                    at, lanes = pl.ds(z * 128, 128), pl.ds(t * 128, 128)
                    h4[q, at, lanes], l4[q, at, lanes] = split(value)

    def rows_back():
        for q in range(2):
            m4[q] = left(mats.at[q, 0], h4[q], l4[q])

    def update():
        out = [[[None] * 2 for _ in range(2)] for _ in range(2)]
        for t in range(2):
            lanes = pl.ds(128 * t, 128)
            er, ei = m4[0, pl.ds(0, 128), lanes], m4[0, pl.ds(128, 128), lanes]
            vr, vi = m4[1, pl.ds(0, 128), lanes], m4[1, pl.ds(128, 128), lanes]
            for h, (xr, xi) in enumerate(((er + vr, ei + vi), (er - vr, ei - vi))):
                rows = pl.ds(h * 128, 128)
                cr, ci = xr - wave[0, rows, lanes], xi - wave[1, rows, lanes]
                if live is not None:
                    cr, ci = cr * live, ci * live
                a, b = patch[0, rows, lanes], patch[1, rows, lanes]
                pterm[0, t, rows, :] += a * cr + b * ci
                pterm[1, t, rows, :] += a * ci - b * cr
                pr, pi = ill[0, rows, lanes], ill[1, rows, lanes]
                out[h][0][t] = pr * cr + pi * ci
                out[h][1][t] = pr * ci - pi * cr
        for h in range(2):
            for z in range(2):
                place(z, h, out[h][z])

    return (cut, rows_forward, between_forward, columns_forward, project,
            columns_back, between_back, rows_back, update)


def together(*windows):
    for steps in zip(*windows):
        for step in steps:
            step()


def deposit(grad, row, col, z, h, values):
    tile = col // 128
    shift = col % 128
    low = lax.broadcasted_iota(jnp.int32, (128, 128), 1) < shift
    first, second = (pltpu.roll(v, shift, 1) for v in values)
    rows = pl.ds(row + h * 128, 128)
    grad[z, tile, rows, :] += jnp.where(low, 0.0, first)
    grad[z, tile + 1, rows, :] += jnp.where(low, first, second)
    grad[z, tile + 2, rows, :] += jnp.where(low, second, 0.0)


def window_kernel(offs, count, ext, ill, mats, moduli, near, near_term, grad, pterm, todo, done, *bufs):
    n = count[0]

    @pl.loop(0, 96)
    def _(i):
        rows = pl.ds(pl.multiple_of(8 * i, 8), 8)
        for p in range(2):
            for t in range(6):
                grad[p, t, rows, :] = jnp.zeros((8, 128), F32)

    pterm[...] = near_term[...]

    def sort(s, counts):
        left_over, taken = counts
        r = offs[0, s]
        inside = jnp.logical_and(jnp.logical_and(r >= 128, r <= 384), s < n)
        inside = jnp.logical_and(inside, taken < NEAR)
        todo[left_over] = s
        done[taken] = s
        return (left_over + jnp.logical_and(s < n, jnp.logical_not(inside)).astype(jnp.int32),
                taken + inside.astype(jnp.int32))

    left_over, taken = lax.fori_loop(0, 16, sort, (jnp.int32(0), jnp.int32(0)))

    @pl.loop(0, taken)
    def _(i):
        s = done[i]
        for h in range(2):
            for z in range(2):
                deposit(grad, offs[0, s], offs[1, s], z, h, [near[i, z, t, pl.ds(h * 128, 128), :] for t in range(2)])

    @pl.loop(0, (left_over + 1) // 2)
    def _(k):
        windows = []
        for i in range(2):
            s = todo[jnp.minimum(2 * k + i, left_over - 1)]
            row, col = offs[0, s], offs[1, s]
            live = None if i == 0 else jnp.where(2 * k + i < left_over, 1.0, 0.0).astype(F32)

            def place(z, h, values, row=row, col=col):
                deposit(grad, row, col, z, h, values)

            windows.append(stages(s, row, col, live, ext, ill, mats, moduli, pterm, place,
                                  bufs[BUFFERS * i:BUFFERS * (i + 1)]))
        together(*windows)


def windows(offs, count, ext, ill, mats, moduli, near, near_term):
    V = pl.BlockSpec(memory_space=pltpu.VMEM)
    S = pl.BlockSpec(memory_space=pltpu.SMEM)
    return pl.pallas_call(
        window_kernel,
        out_shape=(jax.ShapeDtypeStruct((2, 6, 768, 128), F32), jax.ShapeDtypeStruct((2, 2, 256, 128), F32)),
        in_specs=[S, S, V, V, V, V, V, V], out_specs=(V, V),
        scratch_shapes=[pltpu.SMEM((16,), jnp.int32), pltpu.SMEM((16,), jnp.int32)] + buffers() * 2,
        compiler_params=pltpu.CompilerParams(vmem_limit_bytes=28 * 2**20),
    )(offs, count, ext, ill, mats, moduli, near, near_term)


def remote(src, dst, send_sem, recv_sem, device):
    return pltpu.make_async_remote_copy(
        src_ref=src, dst_ref=dst, send_sem=send_sem, recv_sem=recv_sem,
        device_id=device, device_id_type=MESH,
    )


def greet(devices):
    barrier = pltpu.get_barrier_semaphore()
    expected = 0
    for condition, device in devices:
        if condition is None:
            pl.semaphore_signal(barrier, inc=1, device_id=device, device_id_type=MESH)
            expected = expected + 1
        else:
            @pl.when(condition)
            def _(device=device):
                pl.semaphore_signal(barrier, inc=1, device_id=device, device_id_type=MESH)
            expected = expected + condition.astype(jnp.int32)
    return barrier, expected


def neighbours():
    a = lax.axis_index("ty")
    b = lax.axis_index("tx")
    has = {"up": a > 0, "down": a < 15, "left": b > 0, "right": b < 15}
    ids = {"up": (jnp.maximum(a - 1, 0), b), "down": (jnp.minimum(a + 1, 15), b),
           "left": (a, jnp.maximum(b - 1, 0)), "right": (a, jnp.minimum(b + 1, 15))}
    return a, b, has, ids


OPPOSITE = {"up": "down", "down": "up", "left": "right", "right": "left"}


def halo_kernel(offs, count, tile, meas, perm, ill, mats, ext, moduli, near, near_term,
                mid, mbuf, meas_sem, own_sem, mid_sem, row_send, row_recv, col_send, col_recv, cor_send, cor_recv, *bufs):
    a, b, has, ids = neighbours()
    barrier, expected = greet([(has[k], ids[k]) for k in ids])
    own = [pltpu.make_async_copy(tile.at[:, :, pl.ds(128 * t, 128)], mid.at[:, 1 + t], own_sem.at[t]) for t in range(4)]
    for copy in own:
        copy.start()

    def fetch(s, t):
        return pltpu.make_async_copy(meas.at[s, :, pl.ds(128 * t, 128)], mbuf.at[s, t], meas_sem.at[s, t])

    @pl.loop(0, 16)
    def _(s):
        for t in range(2):
            fetch(s, t).start()

    pl.semaphore_wait(barrier, expected)
    rows, cols, corners = {}, {}, {}
    for i, way in enumerate(("down", "up")):
        src_row, dst_row = (384, 0) if way == "down" else (0, 640)
        for t in (0, 3, 1, 2):
            rows[way, t] = remote(
                tile.at[:, pl.ds(src_row, 128), pl.ds(128 * t, 128)],
                ext.at[:, 1 + t, pl.ds(dst_row, 128), :],
                row_send.at[i, t], row_recv.at[i, t], ids[way])
    for i, way in enumerate(("right", "left")):
        src_t, dst_t = (3, 0) if way == "right" else (0, 5)
        cols[way] = remote(
            tile.at[:, :, pl.ds(128 * src_t, 128)], mid.at[:, dst_t],
            col_send.at[i], col_recv.at[i], ids[way])
        for j, row in enumerate((0, 640)):
            corners[way, j] = remote(
                ext.at[:, 1 + src_t, pl.ds(row, 128), :], ext.at[:, dst_t, pl.ds(row, 128), :],
                cor_send.at[i, j], cor_recv.at[i, j], ids[way])
    for t in (0, 3):
        for way in ("down", "up"):
            pl.when(has[way])(rows[way, t].start)
    for way in ("right", "left"):
        pl.when(has[way])(cols[way].start)
    for t in (1, 2):
        for way in ("down", "up"):
            pl.when(has[way])(rows[way, t].start)

    @pl.loop(0, 16)
    def _(s):
        for t in range(2):
            fetch(s, t).wait()
        for q in range(2):
            picked = jnp.concatenate([mbuf[s, t, pl.ds(q, 128, stride=2), :] for t in range(2)], axis=1)
            high, low = split(picked)
            moduli[s, pl.ds(128 * q, 128), :] = dot(high, perm[...]) + dot(low, perm[...])

    near_term[...] = jnp.zeros_like(near_term)
    n = count[0]
    inside, rank, total = [], [], jnp.int32(0)
    for s in range(16):
        r = offs[0, s]
        ok = jnp.logical_and(jnp.logical_and(r >= 128, r <= 384), s < n).astype(jnp.int32)
        inside.append(ok)
        rank.append(total)
        total = total + ok
    for copy in own:
        copy.wait()
    for side in ("right", "left"):
        pl.when(has[OPPOSITE[side]])(cols[side].wait_recv)
    centre = pltpu.make_async_copy(mid, ext.at[:, :, pl.ds(128, 512), :], mid_sem)
    centre.start()

    @pl.loop(0, NEAR // 2)
    def _(k):
        @pl.when(k == 2)
        def _():
            for j, way in enumerate(("down", "up")):
                @pl.when(has[OPPOSITE[way]])
                def _(way=way):
                    rows[way, 0].wait_recv()
                    rows[way, 3].wait_recv()
                for side in ("right", "left"):
                    pl.when(jnp.logical_and(has[side], has[OPPOSITE[way]]))(corners[side, j].start)

        taken = []
        for i in range(2):
            at = 2 * k + i
            slot = jnp.int32(0)
            for s in range(1, 16):
                slot = slot + s * inside[s] * (rank[s] == at).astype(jnp.int32)
            row = jnp.clip(offs[0, slot] - 128, 0, 256)
            live = (at < total).astype(F32)

            def place(z, h, values, at=at):
                for t in range(2):
                    near[at, z, t, pl.ds(h * 128, 128), :] = values[t]

            taken.append(stages(slot, row, offs[1, slot], live, mid, ill, mats, moduli, near_term, place,
                                bufs[BUFFERS * i:BUFFERS * (i + 1)]))
        together(*taken)

    for way in ("down", "up"):
        for t in (1, 2):
            pl.when(has[OPPOSITE[way]])(rows[way, t].wait_recv)
        for t in range(4):
            pl.when(has[way])(rows[way, t].wait_send)
    for side in ("right", "left"):
        pl.when(has[side])(cols[side].wait_send)
        for j, way in enumerate(("down", "up")):
            pl.when(jnp.logical_and(has[OPPOSITE[side]], has[OPPOSITE[way]]))(corners[side, j].wait_recv)
            pl.when(jnp.logical_and(has[side], has[OPPOSITE[way]]))(corners[side, j].wait_send)
    centre.wait()


def halo(offs, count, tile, meas, perm, ill, mats):
    D = pltpu.SemaphoreType.DMA
    A = pl.BlockSpec(memory_space=pl.ANY)
    V = pl.BlockSpec(memory_space=pltpu.VMEM)
    S = pl.BlockSpec(memory_space=pltpu.SMEM)
    return pl.pallas_call(
        halo_kernel,
        out_shape=(jax.ShapeDtypeStruct((2, 6, 768, 128), F32), jax.ShapeDtypeStruct((16, 256, 256), F32),
                   jax.ShapeDtypeStruct((NEAR, 2, 2, 256, 128), F32), jax.ShapeDtypeStruct((2, 2, 256, 128), F32)),
        in_specs=[S, S, A, A, V, V, V], out_specs=(V, V, V, V),
        scratch_shapes=[pltpu.VMEM((2, 6, 512, 128), F32), pltpu.VMEM((16, 2, 256, 128), F32), D((16, 2)),
                        D((4,)), D, D((2, 4)), D((2, 4)), D((2,)), D((2,)), D((2, 2)), D((2, 2))] + buffers() * 2,
        compiler_params=pltpu.CompilerParams(collective_id=1, has_side_effects=True, vmem_limit_bytes=26 * 2**20),
    )(offs, count, tile, meas, perm, ill, mats)


def partners(b):
    core = b % 2
    x = (b // 2) % 4
    zlo = b // 8
    return core, x, zlo


def finish_kernel(spec, ill, grad, pterm, newspec, newill,
                  rxc, rxm, rz, edge, rcore, rx, sumc, part, rc, total,
                  core_s, core_r, xs, xr, cs, cr, ms, mr, zs, zr,
                  us, ur, ds, dr, es, er, fs, fr):
    a, b, has, ids = neighbours()
    core, x, zlo = partners(b)
    low = x * 2 + core
    unit = zlo * 16 + a

    def member(d):
        u = (unit + d) % 32
        return (u % 16, (u // 16) * 8 + low)

    mates = [(a, zlo * 8 + ((x + d) % 4) * 2 + core) for d in (1, 2, 3)]
    other = (a, zlo * 8 + x * 2 + (1 - core))
    barrier, expected = greet([(None, m) for m in mates] + [(None, other)]
                              + [(jnp.logical_and(core == 0, has["left"]), ids["left"]),
                                 (jnp.logical_and(core == 1, has["right"]), ids["right"])])

    @pl.loop(1, 32)
    def _(d):
        pl.semaphore_signal(barrier, inc=1, device_id=member(d), device_id_type=MESH)

    power = jnp.sum(ill[0] * ill[0] + ill[1] * ill[1]) * (1.0 / 65536) + 1e-05
    inv = 1.0 / power
    pl.semaphore_wait(barrier, expected + 31)
    first = remote(pterm.at[1 - core], rcore, core_s, core_r, other)
    corner, middle, vert = {}, {}, {}
    for i, side in enumerate(("right", "left")):
        src_t = 5 if side == "right" else 0
        for j, row in enumerate((0, 640)):
            corner[side, j] = remote(grad.at[:, src_t, pl.ds(row, 128), :], rxc.at[i, j],
                                     cs.at[i, j], cr.at[i, j], ids[side])
        middle[side] = remote(grad.at[:, src_t, pl.ds(128, 512), :], rxm.at[i], ms.at[i], mr.at[i], ids[side])
    for j, way in enumerate(("up", "down")):
        row = 0 if way == "up" else 640
        for t in range(4):
            src = edge.at[j, t // 3] if t in (0, 3) else grad.at[:, 1 + t, pl.ds(row, 128), :]
            vert[way, t] = remote(src, rz.at[j, :, t], zs.at[j, t], zr.at[j, t], ids[way])

    def send_vert(t):
        for way in ("up", "down"):
            pl.when(has[way])(vert[way, t].start)

    def add_vert(t):
        for j, (way, row) in enumerate((("up", 384), ("down", 0))):
            @pl.when(has[OPPOSITE[way]])
            def _(j=j, way=way, row=row):
                vert[way, t].wait_recv()
                newspec[:, row:row + 128, 128 * t:128 * t + 128] += inv * rz[j, :, t]

    first.start()
    send_vert(1)
    first.wait_recv()
    sumc[...] = pterm[core] + rcore[...]
    xsend = [remote(sumc.at[(x + d) % 4], rx.at[d - 1], xs.at[d - 1], xr.at[d - 1], mates[d - 1]) for d in (1, 2, 3)]
    for copy in xsend:
        copy.start()
    for side in ("right", "left"):
        for j in range(2):
            pl.when(has[side])(corner[side, j].start)
    for copy in xsend:
        copy.wait_recv()
    part[...] = sumc[x] + rx[0] + rx[1] + rx[2]

    @pl.loop(1, 32)
    def _(d):
        device = member(d)
        remote(part.at[device[0]], rc.at[d - 1], us, ur, device).start()

    send_vert(2)
    for side in ("right", "left"):
        pl.when(has[side])(middle[side].start)

    @pl.loop(0, 16)
    def _(i):
        rows = pl.ds(pl.multiple_of(32 * i, 32), 32)
        more = pl.ds(pl.multiple_of(32 * i + 128, 32), 32)
        for p in range(2):
            for t in range(4):
                lanes = pl.ds(128 * t, 128)
                newspec[p, rows, lanes] = spec[p, rows, lanes] + inv * grad[p, 1 + t, more, :]

    for j, row in enumerate((0, 640)):
        for k, (t, side) in enumerate(((1, "right"), (4, "left"))):
            edge[j, k] = grad[:, t, row:row + 128, :]
            @pl.when(has[OPPOSITE[side]])
            def _(j=j, k=k, side=side):
                corner[side, j].wait_recv()
                edge[j, k] += rxc[k, j]
    whole = remote(rc, rc, us, ur, other)
    whole.wait_recv()
    acc = part[a]
    for i in range(31):
        acc = acc + rc[i]
    total[core, x, a] = acc

    @pl.loop(1, 16)
    def _(d):
        remote(total.at[core, x, a], total.at[core, x, a], ds, dr, ((a + d) % 16, b)).start()

    send_vert(0)
    send_vert(3)
    for k, (side, t) in enumerate((("right", 0), ("left", 3))):
        @pl.when(has[OPPOSITE[side]])
        def _(k=k, side=side, t=t):
            middle[side].wait_recv()
            newspec[:, :, 128 * t:128 * t + 128] += inv * rxm[k]
    some = remote(rc.at[pl.ds(0, 15)], rc.at[pl.ds(0, 15)], ds, dr, other)
    some.wait_recv()
    gather = [remote(total.at[core, x], total.at[core, x], es.at[d - 1], er.at[d - 1], mates[d - 1]) for d in (1, 2, 3)]
    for copy in gather:
        copy.start()
    add_vert(1)
    add_vert(2)
    for copy in gather:
        copy.wait_recv()
    last = remote(total.at[core], total.at[core], fs, fr, other)
    last.start()
    last.wait()
    for p in range(2):
        for s in range(4):
            rows, lanes = pl.ds((s % 2) * 128, 128), pl.ds((s // 2) * 128, 128)
            newill[p, rows, lanes] = ill[p, rows, lanes] + total[p, s].reshape(128, 128) * (1.0 / 64)
    add_vert(0)
    add_vert(3)
    first.wait_send()
    for copy in xsend + gather:
        copy.wait_send()
    whole.wait_send()
    some.wait_send()
    for side in ("right", "left"):
        for j in range(2):
            pl.when(has[side])(corner[side, j].wait_send)
        pl.when(has[side])(middle[side].wait_send)
    for way in ("up", "down"):
        for t in range(4):
            pl.when(has[way])(vert[way, t].wait_send)


def finish(spec, ill, grad, pterm):
    D = pltpu.SemaphoreType.DMA
    V = pl.BlockSpec(memory_space=pltpu.VMEM)
    return pl.pallas_call(
        finish_kernel,
        out_shape=(jax.ShapeDtypeStruct((2, 512, 512), F32), jax.ShapeDtypeStruct((2, 256, 256), F32)),
        in_specs=[V, V, V, V], out_specs=(V, V),
        scratch_shapes=[
            pltpu.VMEM((2, 2, 2, 128, 128), F32), pltpu.VMEM((2, 2, 512, 128), F32),
            pltpu.VMEM((2, 2, 4, 128, 128), F32), pltpu.VMEM((2, 2, 2, 128, 128), F32),
            pltpu.VMEM((4, 16, 8, 128), F32), pltpu.VMEM((3, 16, 8, 128), F32), pltpu.VMEM((4, 16, 8, 128), F32),
            pltpu.VMEM((16, 8, 128), F32), pltpu.VMEM((31, 8, 128), F32), pltpu.VMEM((2, 4, 16, 8, 128), F32),
            D, D, D((3,)), D((3,)), D((2, 2)), D((2, 2)), D((2,)), D((2,)), D((2, 4)), D((2, 4)),
            D, D, D, D, D((3,)), D((3,)), D, D,
        ],
        compiler_params=pltpu.CompilerParams(collective_id=2, has_side_effects=True, vmem_limit_bytes=32 * 2**20),
    )(spec, ill, grad, pterm)


def shards(specimen, illumination, scan_offsets, slot_counts, measured):
    anchor = jnp.stack([lax.axis_index("ty") * 512, lax.axis_index("tx") * 512]) - 128
    local = scan_offsets[0, 0] - anchor[:, None]
    count = slot_counts[0]
    mats, perm = (jnp.asarray(m) for m in consts())
    ext, moduli, near, near_term = halo(local, count, specimen, measured[0, 0], perm, illumination, mats)
    grad, probe_term = windows(local, count, ext, illumination, mats, moduli, near, near_term)
    return finish(specimen, illumination, grad, probe_term.reshape(2, 4, 16, 8, 128))


def solution(mesh):
    in_specs = (
        P(None, "ty", "tx"),
        P(),
        P("ty", "tx", None, None),
        P("ty", "tx"),
        P("ty", "tx", None, None, None),
    )
    out_specs = (P(None, "ty", "tx"), P())
    return jax.shard_map(shards, mesh=mesh, in_specs=in_specs, out_specs=out_specs, check_vma=False)
```

time: 111 us -> 118 us (1.063)
  Pallas kernels: 102 us -> 107 us
  local copies, waits for them, and re-layouts: 6.81 us -> 9.07 us
    pallas_call x1, Pallas kernels: 66.4 us -> 69.5 us  [finish(): pl.pallas_call(finish_kernel, out_shape=(jax.ShapeDtypeStruct((2, 512, 51...]
    unnamed x14, local copies, waits for them, and re-layouts: 6.81 us -> 9.07 us
    pallas_call x1, Pallas kernels: 3.99 us -> 5.19 us  [windows(): pl.pallas_call(window_kernel, out_shape=(jax.ShapeDtypeStruct((2, 6, 768,...]
where the time goes in v6:
time: 118 us
  Pallas kernels  107 us (91%)
  local copies, waits for them, and re-layouts  9.07 us (8%)
  between operations  1.33 us (1%)
    pallas_call x1, Pallas kernels, finish(): pl.pallas_call(finish_kernel, out_shape=(jax.ShapeDtypeStruct((2, 512, 51...  69.5 us
    pallas_call x1, Pallas kernels, halo(): pl.pallas_call(halo_kernel, out_shape=(jax.ShapeDtypeStruct((2, 6, 768, 1...  32 us
    unnamed x14, local copies, waits for them, and re-layouts  9.07 us
    pallas_call x1, Pallas kernels, windows(): pl.pallas_call(window_kernel, out_shape=(jax.ShapeDtypeStruct((2, 6, 768,...  5.19 us

profile of v6, /device:TPU:1, one launch (start us, length us, event | category | flops | bytes accessed | tf_op | source)
XLA Modules:
  0.0 117.9 jit_solution(13884824370950782892)
XLA Ops:
  1.3 0.1 add_add_fusion
  1.4 0.7 bitcast_subtract_fusion.offs
  2.1 0.0 copy-start
  2.1 1.6 %copy-done = f32[2,512,512]{2,1,0:T(8,128)S(1)} copy-done((f32[2,512,512]{2,1,0:T(8,128)S(1)}, f32[2,512,512]{2,1,0:T(8,128)}, u32[]{:S(2)}) %copy-start) | copy-done | bytes 2097176
  3.7 0.0 copy-start.2
  3.7 1.0 copy-done.2
  4.7 0.0 copy-start.3
  4.7 1.2 %copy-done.3 = bf16[2,2,2,256,256]{4,3,2,1,0:T(8,128)(2,1)S(1)} copy-done((bf16[2,2,2,256,256]{4,3,2,1,0:T(8,128)(2,1)S(1)}, bf16[2,2,2,256,256]{4,3,2,1,0:T(8,128)(2,1)}, u32[]{:S(2)}) %copy-start.3) | copy-done | bytes 1048600
  6.0 0.0 copy-start.4
  6.0 2.2 %copy-done.4 = f32[1,1,16,256,256]{4,3,2,1,0:T(8,128)S(1)} copy-done((f32[1,1,16,256,256]{4,3,2,1,0:T(8,128)S(1)}, f32[1,1,16,256,256]{4,3,2,1,0:T(8,128)}, u32[]{:S(2)}) %copy-start.4) | copy-done | bytes 4194328
  8.2 0.0 copy-start.5
  8.2 0.9 copy-done.5
  9.1 32.0 %shard_map.86 = (f32[2,6,768,128]{3,2,1,0:T(8,128)S(1)}, f32[16,256,256]{2,1,0:T(8,128)S(1)}, f32[10,2,2,256,128]{4,3,2,1,0:T(8,128)S(1)}, f32[2,2,256,128]{3,2,1,0:T(8,128)S(1)}) custom-call(s32[2,16]{1,0:T(2,128)S(1)} %bitcast_subtract_fusion.offs, s32[1]{0:T(128)} %bitcast.7.count, f32[2,512,512]{2,1,0:T(8,128)S(1)} %copy-done, ...), custom_call_target="tpu_custom_call" | custom-call | tf_op jit(solution)/shard_map/pallas_call | solution.py:393
  41.0 0.0 copy-start.1
  41.1 5.2 %shard_map.87 = (f32[2,6,768,128]{3,2,1,0:T(8,128)S(1)}, f32[2,2,256,128]{3,2,1,0:T(8,128)S(1)}) custom-call(s32[2,16]{1,0:T(2,128)S(1)} %bitcast_subtract_fusion.offs, s32[1]{0:T(128)} %bitcast.8.count, f32[2,6,768,128]{3,2,1,0:T(8,128)S(1)} %get-tuple-element.8.ext, f32[2,256,256]{2,1,0:T(8,128)S(1)} %copy-done.2, ...), custom_call_target="tpu_custom_call" | custom-call | tf_op jit(solution)/shard_map/pallas_call | solution.py:235
  46.2 0.0 copy-done.1
  46.3 69.5 %shard_map.88 = (f32[2,512,512]{2,1,0:T(8,128)S(1)}, f32[2,256,256]{2,1,0:T(8,128)S(1)}) custom-call(f32[2,512,512]{2,1,0:T(8,128)S(1)} %copy-done.1, f32[2,256,256]{2,1,0:T(8,128)S(1)} %copy-done.2, f32[2,6,768,128]{3,2,1,0:T(8,128)S(1)} %get-tuple-element.12.grad, f32[2,4,16,8,128]{4,3,2,1,0:T(8,128)S(1)} %bitcast.10), custom_call_target="tpu_custom_call" | custom-call | tf_op jit(solution)/shard_map/pallas_call | solution.py:554
  115.8 1.3 %copy.12 = f32[2,512,512]{2,1,0:T(8,128)} copy(f32[2,512,512]{2,1,0:T(8,128)S(1)} %get-tuple-element.16) | data formatting | bytes 4194304
  117.1 0.8 copy.13
Async XLA Ops:
  2.1 1.6 %copy-start = (f32[2,512,512]{2,1,0:T(8,128)S(1)}, f32[2,512,512]{2,1,0:T(8,128)}, u32[]{:S(2)}) copy-start(f32[2,512,512]{2,1,0:T(8,128)} %spec.1) | copy-start | bytes 6291460
  3.7 1.0 copy-start.2
  4.7 1.2 %copy-start.3 = (bf16[2,2,2,256,256]{4,3,2,1,0:T(8,128)(2,1)S(1)}, bf16[2,2,2,256,256]{4,3,2,1,0:T(8,128)(2,1)}, u32[]{:S(2)}) copy-start(bf16[2,2,2,256,256]{4,3,2,1,0:T(8,128)(2,1)} %constant.16.clone.mats) | copy-start | bytes 3145732
  6.0 2.2 %copy-start.4 = (f32[1,1,16,256,256]{4,3,2,1,0:T(8,128)S(1)}, f32[1,1,16,256,256]{4,3,2,1,0:T(8,128)}, u32[]{:S(2)}) copy-start(f32[1,1,16,256,256]{4,3,2,1,0:T(8,128)} %param.11) | copy-start | bytes 12582916
  8.2 0.9 copy-start.5
  41.0 5.2 %copy-start.1 = (f32[2,512,512]{2,1,0:T(8,128)S(1)}, f32[2,512,512]{2,1,0:T(8,128)}, u32[]{:S(2)}) copy-start(f32[2,512,512]{2,1,0:T(8,128)} %spec.1) | copy-start | bytes 6291460

commit v7 on v6

--- a/solution.py
+++ b/solution.py
@@ -26,10 +26,7 @@
             low = (m - high.astype(np.float32)).astype(ml_dtypes.bfloat16)
             out.append(np.stack([high, low]))
     mats = np.stack(out).reshape(2, 2, 2, 256, 256)
-    k = np.arange(256)
-    perm = np.zeros((256, 256))
-    perm[k, (k % 2) * 128 + k // 2] = 1
-    return mats, perm.astype(ml_dtypes.bfloat16)
+    return mats
 
 
 def split(x):
@@ -165,6 +162,10 @@
             columns_back, between_back, rows_back, update)
 
 
+def places(offs):
+    return lambda s: offs[0, s], lambda s: offs[1, s]
+
+
 def together(*windows):
     for steps in zip(*windows):
         for step in steps:
@@ -184,6 +185,7 @@
 
 def window_kernel(offs, count, ext, ill, mats, moduli, near, near_term, grad, pterm, todo, done, *bufs):
     n = count[0]
+    row_of, col_of = places(offs)
 
     @pl.loop(0, 96)
     def _(i):
@@ -196,7 +198,7 @@
 
     def sort(s, counts):
         left_over, taken = counts
-        r = offs[0, s]
+        r = row_of(s)
         inside = jnp.logical_and(jnp.logical_and(r >= 128, r <= 384), s < n)
         inside = jnp.logical_and(inside, taken < NEAR)
         todo[left_over] = s
@@ -211,14 +213,14 @@
         s = done[i]
         for h in range(2):
             for z in range(2):
-                deposit(grad, offs[0, s], offs[1, s], z, h, [near[i, z, t, pl.ds(h * 128, 128), :] for t in range(2)])
+                deposit(grad, row_of(s), col_of(s), z, h, [near[i, z, t, pl.ds(h * 128, 128), :] for t in range(2)])
 
     @pl.loop(0, (left_over + 1) // 2)
     def _(k):
         windows = []
         for i in range(2):
             s = todo[jnp.minimum(2 * k + i, left_over - 1)]
-            row, col = offs[0, s], offs[1, s]
+            row, col = row_of(s), col_of(s)
             live = None if i == 0 else jnp.where(2 * k + i < left_over, 1.0, 0.0).astype(F32)
 
             def place(z, h, values, row=row, col=col):
@@ -275,7 +277,7 @@
 OPPOSITE = {"up": "down", "down": "up", "left": "right", "right": "left"}
 
 
-def halo_kernel(offs, count, tile, meas, perm, ill, mats, ext, moduli, near, near_term,
+def halo_kernel(offs, count, tile, meas, ill, mats, ext, moduli, near, near_term,
                 mid, mbuf, meas_sem, own_sem, mid_sem, row_send, row_recv, col_send, col_recv, cor_send, cor_recv, *bufs):
     a, b, has, ids = neighbours()
     barrier, expected = greet([(has[k], ids[k]) for k in ids])
@@ -309,14 +311,28 @@
             corners[way, j] = remote(
                 ext.at[:, 1 + src_t, pl.ds(row, 128), :], ext.at[:, dst_t, pl.ds(row, 128), :],
                 cor_send.at[i, j], cor_recv.at[i, j], ids[way])
-    for t in (0, 3):
-        for way in ("down", "up"):
-            pl.when(has[way])(rows[way, t].start)
+    outer = jnp.logical_or((b // 2) % 4 == 0, (b // 2) % 4 == 3)
+
+    def start_rows(mine):
+        for t in (0, 3, 1, 2):
+            for way in ("down", "up"):
+                pl.when(jnp.logical_and(has[way], mine))(rows[way, t].start)
+
     for way in ("right", "left"):
         pl.when(has[way])(cols[way].start)
-    for t in (1, 2):
-        for way in ("down", "up"):
-            pl.when(has[way])(rows[way, t].start)
+    start_rows(jnp.logical_not(outer))
+    near_term[...] = jnp.zeros_like(near_term)
+    for side in ("right", "left"):
+        pl.when(has[side])(cols[side].wait_send)
+        pl.when(has[OPPOSITE[side]])(cols[side].wait_recv)
+    start_rows(outer)
+    for copy in own:
+        copy.wait()
+    centre = pltpu.make_async_copy(mid, ext.at[:, :, pl.ds(128, 512), :], mid_sem)
+    centre.start()
+    to = lax.broadcasted_iota(jnp.int32, (256, 256), 1)
+    source = 2 * (to % 128) + to // 128
+    perm = jnp.where(lax.broadcasted_iota(jnp.int32, (256, 256), 0) == source, 1.0, 0.0).astype(BF)
 
     @pl.loop(0, 16)
     def _(s):
@@ -325,23 +341,17 @@
         for q in range(2):
             picked = jnp.concatenate([mbuf[s, t, pl.ds(q, 128, stride=2), :] for t in range(2)], axis=1)
             high, low = split(picked)
-            moduli[s, pl.ds(128 * q, 128), :] = dot(high, perm[...]) + dot(low, perm[...])
-
-    near_term[...] = jnp.zeros_like(near_term)
+            moduli[s, pl.ds(128 * q, 128), :] = dot(high, perm) + dot(low, perm)
+
     n = count[0]
+    row_of, col_of = places(offs)
     inside, rank, total = [], [], jnp.int32(0)
     for s in range(16):
-        r = offs[0, s]
+        r = row_of(s)
         ok = jnp.logical_and(jnp.logical_and(r >= 128, r <= 384), s < n).astype(jnp.int32)
         inside.append(ok)
         rank.append(total)
         total = total + ok
-    for copy in own:
-        copy.wait()
-    for side in ("right", "left"):
-        pl.when(has[OPPOSITE[side]])(cols[side].wait_recv)
-    centre = pltpu.make_async_copy(mid, ext.at[:, :, pl.ds(128, 512), :], mid_sem)
-    centre.start()
 
     @pl.loop(0, NEAR // 2)
     def _(k):
@@ -361,14 +371,14 @@
             slot = jnp.int32(0)
             for s in range(1, 16):
                 slot = slot + s * inside[s] * (rank[s] == at).astype(jnp.int32)
-            row = jnp.clip(offs[0, slot] - 128, 0, 256)
+            row = jnp.clip(row_of(slot) - 128, 0, 256)
             live = (at < total).astype(F32)
 
             def place(z, h, values, at=at):
                 for t in range(2):
                     near[at, z, t, pl.ds(h * 128, 128), :] = values[t]
 
-            taken.append(stages(slot, row, offs[1, slot], live, mid, ill, mats, moduli, near_term, place,
+            taken.append(stages(slot, row, col_of(slot), live, mid, ill, mats, moduli, near_term, place,
                                 bufs[BUFFERS * i:BUFFERS * (i + 1)]))
         together(*taken)
 
@@ -378,14 +388,13 @@
         for t in range(4):
             pl.when(has[way])(rows[way, t].wait_send)
     for side in ("right", "left"):
-        pl.when(has[side])(cols[side].wait_send)
         for j, way in enumerate(("down", "up")):
             pl.when(jnp.logical_and(has[OPPOSITE[side]], has[OPPOSITE[way]]))(corners[side, j].wait_recv)
             pl.when(jnp.logical_and(has[side], has[OPPOSITE[way]]))(corners[side, j].wait_send)
     centre.wait()
 
 
-def halo(offs, count, tile, meas, perm, ill, mats):
+def halo(offs, count, tile, meas, ill, mats):
     D = pltpu.SemaphoreType.DMA
     A = pl.BlockSpec(memory_space=pl.ANY)
     V = pl.BlockSpec(memory_space=pltpu.VMEM)
@@ -394,11 +403,11 @@
         halo_kernel,
         out_shape=(jax.ShapeDtypeStruct((2, 6, 768, 128), F32), jax.ShapeDtypeStruct((16, 256, 256), F32),
                    jax.ShapeDtypeStruct((NEAR, 2, 2, 256, 128), F32), jax.ShapeDtypeStruct((2, 2, 256, 128), F32)),
-        in_specs=[S, S, A, A, V, V, V], out_specs=(V, V, V, V),
+        in_specs=[S, S, A, A, V, V], out_specs=(V, V, V, V),
         scratch_shapes=[pltpu.VMEM((2, 6, 512, 128), F32), pltpu.VMEM((16, 2, 256, 128), F32), D((16, 2)),
                         D((4,)), D, D((2, 4)), D((2, 4)), D((2,)), D((2,)), D((2, 2)), D((2, 2))] + buffers() * 2,
         compiler_params=pltpu.CompilerParams(collective_id=1, has_side_effects=True, vmem_limit_bytes=26 * 2**20),
-    )(offs, count, tile, meas, perm, ill, mats)
+    )(offs, count, tile, meas, ill, mats)
 
 
 def partners(b):
@@ -448,9 +457,13 @@
             src = edge.at[j, t // 3] if t in (0, 3) else grad.at[:, 1 + t, pl.ds(row, 128), :]
             vert[way, t] = remote(src, rz.at[j, :, t], zs.at[j, t], zr.at[j, t], ids[way])
 
-    def send_vert(t):
+    outer = jnp.logical_or(x == 0, x == 3)
+    inner = jnp.logical_not(outer)
+    crossing = {"right": b == 7, "left": b == 8}
+
+    def send_vert(t, mine):
         for way in ("up", "down"):
-            pl.when(has[way])(vert[way, t].start)
+            pl.when(jnp.logical_and(has[way], mine))(vert[way, t].start)
 
     def add_vert(t):
         for j, (way, row) in enumerate((("up", 384), ("down", 0))):
@@ -460,7 +473,9 @@
                 newspec[:, row:row + 128, 128 * t:128 * t + 128] += inv * rz[j, :, t]
 
     first.start()
-    send_vert(1)
+    for side in ("right", "left"):
+        pl.when(crossing[side])(middle[side].start)
+    send_vert(1, inner)
     first.wait_recv()
     sumc[...] = pterm[core] + rcore[...]
     xsend = [remote(sumc.at[(x + d) % 4], rx.at[d - 1], xs.at[d - 1], xr.at[d - 1], mates[d - 1]) for d in (1, 2, 3)]
@@ -478,9 +493,10 @@
         device = member(d)
         remote(part.at[device[0]], rc.at[d - 1], us, ur, device).start()
 
-    send_vert(2)
+    send_vert(1, outer)
+    send_vert(2, inner)
     for side in ("right", "left"):
-        pl.when(has[side])(middle[side].start)
+        pl.when(jnp.logical_and(has[side], jnp.logical_not(crossing[side])))(middle[side].start)
 
     @pl.loop(0, 16)
     def _(i):
@@ -509,8 +525,9 @@
     def _(d):
         remote(total.at[core, x, a], total.at[core, x, a], ds, dr, ((a + d) % 16, b)).start()
 
-    send_vert(0)
-    send_vert(3)
+    send_vert(2, outer)
+    send_vert(0, has["up"] | has["down"])
+    send_vert(3, has["up"] | has["down"])
     for k, (side, t) in enumerate((("right", 0), ("left", 3))):
         @pl.when(has[OPPOSITE[side]])
         def _(k=k, side=side, t=t):
@@ -571,8 +588,8 @@
     anchor = jnp.stack([lax.axis_index("ty") * 512, lax.axis_index("tx") * 512]) - 128
     local = scan_offsets[0, 0] - anchor[:, None]
     count = slot_counts[0]
-    mats, perm = (jnp.asarray(m) for m in consts())
-    ext, moduli, near, near_term = halo(local, count, specimen, measured[0, 0], perm, illumination, mats)
+    mats = jnp.asarray(consts())
+    ext, moduli, near, near_term = halo(local, count, specimen, measured[0, 0], illumination, mats)
     grad, probe_term = windows(local, count, ext, illumination, mats, moduli, near, near_term)
     return finish(specimen, illumination, grad, probe_term.reshape(2, 4, 16, 8, 128))
 

time: 118 us -> 116 us (0.983)
  the two profiles are of different devices: /device:TPU:1 before, /device:TPU:32 now
where the time goes in v7:
time: 116 us
  Pallas kernels  105 us (91%)
  local copies, waits for them, and re-layouts  8.16 us (7%)
  between operations  1.33 us (1%)
    pallas_call x1, Pallas kernels, finish(): pl.pallas_call(finish_kernel, out_shape=(jax.ShapeDtypeStruct((2, 512, 51...  54.9 us
    pallas_call x1, Pallas kernels, halo(): pl.pallas_call(halo_kernel, out_shape=(jax.ShapeDtypeStruct((2, 6, 768, 1...  45.8 us
    unnamed x12, local copies, waits for them, and re-layouts  8.16 us
    pallas_call x1, Pallas kernels, windows(): pl.pallas_call(window_kernel, out_shape=(jax.ShapeDtypeStruct((2, 6, 768,...  4.54 us

profile of v7, /device:TPU:32, one launch (start us, length us, event | category | flops | bytes accessed | tf_op | source)
XLA Modules:
  0.0 115.5 jit_solution(8741486658365050484)
XLA Ops:
  1.3 0.1 add_add_fusion
  1.4 0.7 bitcast_subtract_fusion.offs
  2.1 0.0 copy-start
  2.1 1.6 %copy-done = f32[2,512,512]{2,1,0:T(8,128)S(1)} copy-done((f32[2,512,512]{2,1,0:T(8,128)S(1)}, f32[2,512,512]{2,1,0:T(8,128)}, u32[]{:S(2)}) %copy-start) | copy-done | bytes 2097176
  3.7 0.0 copy-start.2
  3.7 1.0 copy-done.2
  4.7 0.0 copy-start.3
  4.7 1.2 %copy-done.3 = bf16[2,2,2,256,256]{4,3,2,1,0:T(8,128)(2,1)S(1)} copy-done((bf16[2,2,2,256,256]{4,3,2,1,0:T(8,128)(2,1)S(1)}, bf16[2,2,2,256,256]{4,3,2,1,0:T(8,128)(2,1)}, u32[]{:S(2)}) %copy-start.3) | copy-done | bytes 1048600
  6.0 0.0 copy-start.4
  6.0 2.2 %copy-done.4 = f32[1,1,16,256,256]{4,3,2,1,0:T(8,128)S(1)} copy-done((f32[1,1,16,256,256]{4,3,2,1,0:T(8,128)S(1)}, f32[1,1,16,256,256]{4,3,2,1,0:T(8,128)}, u32[]{:S(2)}) %copy-start.4) | copy-done | bytes 4194328
  8.2 45.8 %shard_map.77 = (f32[2,6,768,128]{3,2,1,0:T(8,128)S(1)}, f32[16,256,256]{2,1,0:T(8,128)S(1)}, f32[10,2,2,256,128]{4,3,2,1,0:T(8,128)S(1)}, f32[2,2,256,128]{3,2,1,0:T(8,128)S(1)}) custom-call(s32[2,16]{1,0:T(2,128)S(1)} %bitcast_subtract_fusion.offs, s32[1]{0:T(128)} %bitcast.7.count, f32[2,512,512]{2,1,0:T(8,128)S(1)} %copy-done, ...), custom_call_target="tpu_custom_call" | custom-call | tf_op jit(solution)/shard_map/pallas_call | solution.py:402
  53.9 0.0 copy-start.1
  53.9 4.5 %shard_map.78 = (f32[2,6,768,128]{3,2,1,0:T(8,128)S(1)}, f32[2,2,256,128]{3,2,1,0:T(8,128)S(1)}) custom-call(s32[2,16]{1,0:T(2,128)S(1)} %bitcast_subtract_fusion.offs, s32[1]{0:T(128)} %bitcast.8.count, f32[2,6,768,128]{3,2,1,0:T(8,128)S(1)} %get-tuple-element.8.ext, f32[2,256,256]{2,1,0:T(8,128)S(1)} %copy-done.2, ...), custom_call_target="tpu_custom_call" | custom-call | tf_op jit(solution)/shard_map/pallas_call | solution.py:237
  58.5 0.0 copy-done.1
  58.5 54.9 %shard_map.79 = (f32[2,512,512]{2,1,0:T(8,128)S(1)}, f32[2,256,256]{2,1,0:T(8,128)S(1)}) custom-call(f32[2,512,512]{2,1,0:T(8,128)S(1)} %copy-done.1, f32[2,256,256]{2,1,0:T(8,128)S(1)} %copy-done.2, f32[2,6,768,128]{3,2,1,0:T(8,128)S(1)} %get-tuple-element.12.grad, f32[2,4,16,8,128]{4,3,2,1,0:T(8,128)S(1)} %bitcast.10), custom_call_target="tpu_custom_call" | custom-call | tf_op jit(solution)/shard_map/pallas_call | solution.py:571
  113.4 1.3 %copy.11 = f32[2,512,512]{2,1,0:T(8,128)} copy(f32[2,512,512]{2,1,0:T(8,128)S(1)} %get-tuple-element.16) | data formatting | bytes 4194304
  114.7 0.8 copy.12
Async XLA Ops:
  2.1 1.6 %copy-start = (f32[2,512,512]{2,1,0:T(8,128)S(1)}, f32[2,512,512]{2,1,0:T(8,128)}, u32[]{:S(2)}) copy-start(f32[2,512,512]{2,1,0:T(8,128)} %spec.1) | copy-start | bytes 6291460
  3.7 1.0 copy-start.2
  4.7 1.2 %copy-start.3 = (bf16[2,2,2,256,256]{4,3,2,1,0:T(8,128)(2,1)S(1)}, bf16[2,2,2,256,256]{4,3,2,1,0:T(8,128)(2,1)}, u32[]{:S(2)}) copy-start(bf16[2,2,2,256,256]{4,3,2,1,0:T(8,128)(2,1)} %constant.14.clone.mats) | copy-start | bytes 3145732
  6.0 2.2 %copy-start.4 = (f32[1,1,16,256,256]{4,3,2,1,0:T(8,128)S(1)}, f32[1,1,16,256,256]{4,3,2,1,0:T(8,128)}, u32[]{:S(2)}) copy-start(f32[1,1,16,256,256]{4,3,2,1,0:T(8,128)} %param.10) | copy-start | bytes 12582916
  53.9 4.6 %copy-start.1 = (f32[2,512,512]{2,1,0:T(8,128)S(1)}, f32[2,512,512]{2,1,0:T(8,128)}, u32[]{:S(2)}) copy-start(f32[2,512,512]{2,1,0:T(8,128)} %spec.1) | copy-start | bytes 6291460

commit v8 on v7

--- a/solution.py
+++ b/solution.py
@@ -313,19 +313,21 @@
                 cor_send.at[i, j], cor_recv.at[i, j], ids[way])
     outer = jnp.logical_or((b // 2) % 4 == 0, (b // 2) % 4 == 3)
 
-    def start_rows(mine):
-        for t in (0, 3, 1, 2):
+    inner = jnp.logical_not(outer)
+
+    def start_rows(mine, tiles):
+        for t in tiles:
             for way in ("down", "up"):
                 pl.when(jnp.logical_and(has[way], mine))(rows[way, t].start)
 
     for way in ("right", "left"):
         pl.when(has[way])(cols[way].start)
-    start_rows(jnp.logical_not(outer))
+    start_rows(inner, (0, 3))
     near_term[...] = jnp.zeros_like(near_term)
     for side in ("right", "left"):
         pl.when(has[side])(cols[side].wait_send)
         pl.when(has[OPPOSITE[side]])(cols[side].wait_recv)
-    start_rows(outer)
+    start_rows(outer, (0, 3))
     for copy in own:
         copy.wait()
     centre = pltpu.make_async_copy(mid, ext.at[:, :, pl.ds(128, 512), :], mid_sem)
@@ -355,8 +357,19 @@
 
     @pl.loop(0, NEAR // 2)
     def _(k):
+        def sent_edges(mine):
+            for way in ("down", "up"):
+                for t in (0, 3):
+                    pl.when(jnp.logical_and(has[way], mine))(rows[way, t].wait_send)
+
+        @pl.when(k == 1)
+        def _():
+            sent_edges(inner)
+            start_rows(inner, (1, 2))
+
         @pl.when(k == 2)
         def _():
+            sent_edges(outer)
             for j, way in enumerate(("down", "up")):
                 @pl.when(has[OPPOSITE[way]])
                 def _(way=way):
@@ -364,6 +377,7 @@
                     rows[way, 3].wait_recv()
                 for side in ("right", "left"):
                     pl.when(jnp.logical_and(has[side], has[OPPOSITE[way]]))(corners[side, j].start)
+            start_rows(outer, (1, 2))
 
         taken = []
         for i in range(2):
@@ -385,7 +399,6 @@
     for way in ("down", "up"):
         for t in (1, 2):
             pl.when(has[OPPOSITE[way]])(rows[way, t].wait_recv)
-        for t in range(4):
             pl.when(has[way])(rows[way, t].wait_send)
     for side in ("right", "left"):
         for j, way in enumerate(("down", "up")):

time: 116 us -> 113 us (0.974)
  the two profiles are of different devices: /device:TPU:32 before, /device:TPU:47 now
where the time goes in v8:
time: 113 us
  Pallas kernels  103 us (91%)
  local copies, waits for them, and re-layouts  8.16 us (7%)
  between operations  1.33 us (1%)
    pallas_call x1, Pallas kernels, finish(): pl.pallas_call(finish_kernel, out_shape=(jax.ShapeDtypeStruct((2, 512, 51...  66.1 us
    pallas_call x1, Pallas kernels, halo(): pl.pallas_call(halo_kernel, out_shape=(jax.ShapeDtypeStruct((2, 6, 768, 1...  26.5 us
    pallas_call x1, Pallas kernels, windows(): pl.pallas_call(window_kernel, out_shape=(jax.ShapeDtypeStruct((2, 6, 768,...  9.97 us
    unnamed x12, local copies, waits for them, and re-layouts  8.16 us

profile of v8, /device:TPU:47, one launch (start us, length us, event | category | flops | bytes accessed | tf_op | source)
XLA Modules:
  0.0 112.9 jit_solution(3142432671116309726)
XLA Ops:
  1.3 0.1 add_add_fusion
  1.4 0.7 bitcast_subtract_fusion.offs
  2.1 0.0 copy-start
  2.1 1.6 %copy-done = f32[2,512,512]{2,1,0:T(8,128)S(1)} copy-done((f32[2,512,512]{2,1,0:T(8,128)S(1)}, f32[2,512,512]{2,1,0:T(8,128)}, u32[]{:S(2)}) %copy-start) | copy-done | bytes 2097176
  3.7 0.0 copy-start.2
  3.7 1.0 copy-done.2
  4.7 0.0 copy-start.3
  4.7 1.2 %copy-done.3 = bf16[2,2,2,256,256]{4,3,2,1,0:T(8,128)(2,1)S(1)} copy-done((bf16[2,2,2,256,256]{4,3,2,1,0:T(8,128)(2,1)S(1)}, bf16[2,2,2,256,256]{4,3,2,1,0:T(8,128)(2,1)}, u32[]{:S(2)}) %copy-start.3) | copy-done | bytes 1048600
  6.0 0.0 copy-start.4
  6.0 2.2 %copy-done.4 = f32[1,1,16,256,256]{4,3,2,1,0:T(8,128)S(1)} copy-done((f32[1,1,16,256,256]{4,3,2,1,0:T(8,128)S(1)}, f32[1,1,16,256,256]{4,3,2,1,0:T(8,128)}, u32[]{:S(2)}) %copy-start.4) | copy-done | bytes 4194328
  8.2 26.5 %shard_map.77 = (f32[2,6,768,128]{3,2,1,0:T(8,128)S(1)}, f32[16,256,256]{2,1,0:T(8,128)S(1)}, f32[10,2,2,256,128]{4,3,2,1,0:T(8,128)S(1)}, f32[2,2,256,128]{3,2,1,0:T(8,128)S(1)}) custom-call(s32[2,16]{1,0:T(2,128)S(1)} %bitcast_subtract_fusion.offs, s32[1]{0:T(128)} %bitcast.7.count, f32[2,512,512]{2,1,0:T(8,128)S(1)} %copy-done, ...), custom_call_target="tpu_custom_call" | custom-call | tf_op jit(solution)/shard_map/pallas_call | solution.py:415
  34.7 0.0 copy-start.1
  34.7 10.0 %shard_map.78 = (f32[2,6,768,128]{3,2,1,0:T(8,128)S(1)}, f32[2,2,256,128]{3,2,1,0:T(8,128)S(1)}) custom-call(s32[2,16]{1,0:T(2,128)S(1)} %bitcast_subtract_fusion.offs, s32[1]{0:T(128)} %bitcast.8.count, f32[2,6,768,128]{3,2,1,0:T(8,128)S(1)} %get-tuple-element.8.ext, f32[2,256,256]{2,1,0:T(8,128)S(1)} %copy-done.2, ...), custom_call_target="tpu_custom_call" | custom-call | tf_op jit(solution)/shard_map/pallas_call | solution.py:237
  44.7 0.0 copy-done.1
  44.7 66.1 %shard_map.79 = (f32[2,512,512]{2,1,0:T(8,128)S(1)}, f32[2,256,256]{2,1,0:T(8,128)S(1)}) custom-call(f32[2,512,512]{2,1,0:T(8,128)S(1)} %copy-done.1, f32[2,256,256]{2,1,0:T(8,128)S(1)} %copy-done.2, f32[2,6,768,128]{3,2,1,0:T(8,128)S(1)} %get-tuple-element.12.grad, f32[2,4,16,8,128]{4,3,2,1,0:T(8,128)S(1)} %bitcast.10), custom_call_target="tpu_custom_call" | custom-call | tf_op jit(solution)/shard_map/pallas_call | solution.py:584
  110.8 1.3 %copy.11 = f32[2,512,512]{2,1,0:T(8,128)} copy(f32[2,512,512]{2,1,0:T(8,128)S(1)} %get-tuple-element.16) | data formatting | bytes 4194304
  112.1 0.8 copy.12
Async XLA Ops:
  2.1 1.6 %copy-start = (f32[2,512,512]{2,1,0:T(8,128)S(1)}, f32[2,512,512]{2,1,0:T(8,128)}, u32[]{:S(2)}) copy-start(f32[2,512,512]{2,1,0:T(8,128)} %spec.1) | copy-start | bytes 6291460
  3.7 1.0 copy-start.2
  4.7 1.2 %copy-start.3 = (bf16[2,2,2,256,256]{4,3,2,1,0:T(8,128)(2,1)S(1)}, bf16[2,2,2,256,256]{4,3,2,1,0:T(8,128)(2,1)}, u32[]{:S(2)}) copy-start(bf16[2,2,2,256,256]{4,3,2,1,0:T(8,128)(2,1)} %constant.14.clone.mats) | copy-start | bytes 3145732
  6.0 2.2 %copy-start.4 = (f32[1,1,16,256,256]{4,3,2,1,0:T(8,128)S(1)}, f32[1,1,16,256,256]{4,3,2,1,0:T(8,128)}, u32[]{:S(2)}) copy-start(f32[1,1,16,256,256]{4,3,2,1,0:T(8,128)} %param.10) | copy-start | bytes 12582916
  34.7 10.0 %copy-start.1 = (f32[2,512,512]{2,1,0:T(8,128)S(1)}, f32[2,512,512]{2,1,0:T(8,128)}, u32[]{:S(2)}) copy-start(f32[2,512,512]{2,1,0:T(8,128)} %spec.1) | copy-start | bytes 6291460

commit v9 on v8

--- a/solution.py
+++ b/solution.py
@@ -377,6 +377,9 @@
                     rows[way, 3].wait_recv()
                 for side in ("right", "left"):
                     pl.when(jnp.logical_and(has[side], has[OPPOSITE[way]]))(corners[side, j].start)
+
+        @pl.when(k == 3)
+        def _():
             start_rows(outer, (1, 2))
 
         taken = []
@@ -419,6 +422,7 @@
         in_specs=[S, S, A, A, V, V], out_specs=(V, V, V, V),
         scratch_shapes=[pltpu.VMEM((2, 6, 512, 128), F32), pltpu.VMEM((16, 2, 256, 128), F32), D((16, 2)),
                         D((4,)), D, D((2, 4)), D((2, 4)), D((2,)), D((2,)), D((2, 2)), D((2, 2))] + buffers() * 2,
+        cost_estimate=pl.CostEstimate(flops=2 * 10**10, bytes_accessed=2 * 10**7, transcendentals=0),
         compiler_params=pltpu.CompilerParams(collective_id=1, has_side_effects=True, vmem_limit_bytes=26 * 2**20),
     )(offs, count, tile, meas, ill, mats)
 

time: 113 us -> 111 us (0.982)
  the two profiles are of different devices: /device:TPU:47 before, /device:TPU:1 now
where the time goes in v9:
time: 111 us
  Pallas kernels  101 us (91%)
  local copies, waits for them, and re-layouts  8.16 us (7%)
  between operations  1.33 us (1%)
    pallas_call x1, Pallas kernels, finish(): pl.pallas_call(finish_kernel, out_shape=(jax.ShapeDtypeStruct((2, 512, 51...  59.1 us
    pallas_call x1, Pallas kernels, halo(): pl.pallas_call(halo_kernel, out_shape=(jax.ShapeDtypeStruct((2, 6, 768, 1...  36.9 us
    unnamed x12, local copies, waits for them, and re-layouts  8.16 us
    pallas_call x1, Pallas kernels, windows(): pl.pallas_call(window_kernel, out_shape=(jax.ShapeDtypeStruct((2, 6, 768,...  4.74 us

profile of v9, /device:TPU:1, one launch (start us, length us, event | category | flops | bytes accessed | tf_op | source)
XLA Modules:
  0.0 111.0 jit_solution(17712665413420030155)
XLA Ops:
  1.3 0.1 add_add_fusion
  1.4 0.7 bitcast_subtract_fusion.offs
  2.1 0.0 copy-start
  2.1 1.6 %copy-done = f32[2,512,512]{2,1,0:T(8,128)S(1)} copy-done((f32[2,512,512]{2,1,0:T(8,128)S(1)}, f32[2,512,512]{2,1,0:T(8,128)}, u32[]{:S(2)}) %copy-start) | copy-done | bytes 2097176
  3.7 0.0 copy-start.2
  3.7 1.0 copy-done.2
  4.7 0.0 copy-start.3
  4.7 1.2 %copy-done.3 = bf16[2,2,2,256,256]{4,3,2,1,0:T(8,128)(2,1)S(1)} copy-done((bf16[2,2,2,256,256]{4,3,2,1,0:T(8,128)(2,1)S(1)}, bf16[2,2,2,256,256]{4,3,2,1,0:T(8,128)(2,1)}, u32[]{:S(2)}) %copy-start.3) | copy-done | bytes 1048600
  6.0 0.0 copy-start.4
  6.0 2.2 %copy-done.4 = f32[1,1,16,256,256]{4,3,2,1,0:T(8,128)S(1)} copy-done((f32[1,1,16,256,256]{4,3,2,1,0:T(8,128)S(1)}, f32[1,1,16,256,256]{4,3,2,1,0:T(8,128)}, u32[]{:S(2)}) %copy-start.4) | copy-done | bytes 4194328
  8.2 36.9 %shard_map.77 = (f32[2,6,768,128]{3,2,1,0:T(8,128)S(1)}, f32[16,256,256]{2,1,0:T(8,128)S(1)}, f32[10,2,2,256,128]{4,3,2,1,0:T(8,128)S(1)}, f32[2,2,256,128]{3,2,1,0:T(8,128)S(1)}) custom-call(s32[2,16]{1,0:T(2,128)S(1)} %bitcast_subtract_fusion.offs, s32[1]{0:T(128)} %bitcast.7.count, f32[2,512,512]{2,1,0:T(8,128)S(1)} %copy-done, ...), custom_call_target="tpu_custom_call" | custom-call | flops 20000000000 | bytes 20000000 | tf_op jit(solution)/shard_map/pallas_call | solution.py:418
  45.0 0.0 copy-start.1
  45.0 4.7 %shard_map.78 = (f32[2,6,768,128]{3,2,1,0:T(8,128)S(1)}, f32[2,2,256,128]{3,2,1,0:T(8,128)S(1)}) custom-call(s32[2,16]{1,0:T(2,128)S(1)} %bitcast_subtract_fusion.offs, s32[1]{0:T(128)} %bitcast.8.count, f32[2,6,768,128]{3,2,1,0:T(8,128)S(1)} %get-tuple-element.8.ext, f32[2,256,256]{2,1,0:T(8,128)S(1)} %copy-done.2, ...), custom_call_target="tpu_custom_call" | custom-call | tf_op jit(solution)/shard_map/pallas_call | solution.py:237
  49.8 0.0 copy-done.1
  49.8 59.1 %shard_map.79 = (f32[2,512,512]{2,1,0:T(8,128)S(1)}, f32[2,256,256]{2,1,0:T(8,128)S(1)}) custom-call(f32[2,512,512]{2,1,0:T(8,128)S(1)} %copy-done.1, f32[2,256,256]{2,1,0:T(8,128)S(1)} %copy-done.2, f32[2,6,768,128]{3,2,1,0:T(8,128)S(1)} %get-tuple-element.12.grad, f32[2,4,16,8,128]{4,3,2,1,0:T(8,128)S(1)} %bitcast.9), custom_call_target="tpu_custom_call" | custom-call | tf_op jit(solution)/shard_map/pallas_call | solution.py:588
  108.9 1.3 %copy.11 = f32[2,512,512]{2,1,0:T(8,128)} copy(f32[2,512,512]{2,1,0:T(8,128)S(1)} %get-tuple-element.16) | data formatting | bytes 4194304
  110.2 0.8 copy.12
Async XLA Ops:
  2.1 1.6 %copy-start = (f32[2,512,512]{2,1,0:T(8,128)S(1)}, f32[2,512,512]{2,1,0:T(8,128)}, u32[]{:S(2)}) copy-start(f32[2,512,512]{2,1,0:T(8,128)} %spec.1) | copy-start | bytes 6291460
  3.7 1.0 copy-start.2
  4.7 1.2 %copy-start.3 = (bf16[2,2,2,256,256]{4,3,2,1,0:T(8,128)(2,1)S(1)}, bf16[2,2,2,256,256]{4,3,2,1,0:T(8,128)(2,1)}, u32[]{:S(2)}) copy-start(bf16[2,2,2,256,256]{4,3,2,1,0:T(8,128)(2,1)} %constant.14.clone.mats) | copy-start | bytes 3145732
  6.0 2.2 %copy-start.4 = (f32[1,1,16,256,256]{4,3,2,1,0:T(8,128)S(1)}, f32[1,1,16,256,256]{4,3,2,1,0:T(8,128)}, u32[]{:S(2)}) copy-start(f32[1,1,16,256,256]{4,3,2,1,0:T(8,128)} %param.10) | copy-start | bytes 12582916
  45.0 4.8 %copy-start.1 = (f32[2,512,512]{2,1,0:T(8,128)S(1)}, f32[2,512,512]{2,1,0:T(8,128)}, u32[]{:S(2)}) copy-start(f32[2,512,512]{2,1,0:T(8,128)} %spec.1) | copy-start | bytes 6291460

commit v10 on v9

--- a/solution.py
+++ b/solution.py
@@ -324,14 +324,18 @@
         pl.when(has[way])(cols[way].start)
     start_rows(inner, (0, 3))
     near_term[...] = jnp.zeros_like(near_term)
-    for side in ("right", "left"):
-        pl.when(has[side])(cols[side].wait_send)
-        pl.when(has[OPPOSITE[side]])(cols[side].wait_recv)
+    crossing = {"right": b == 7, "left": b == 8}
+
+    def settle(late):
+        for side in ("right", "left"):
+            sends, lands = crossing[side], crossing[OPPOSITE[side]]
+            if not late:
+                sends, lands = jnp.logical_not(sends), jnp.logical_not(lands)
+            pl.when(jnp.logical_and(has[side], sends))(cols[side].wait_send)
+            pl.when(jnp.logical_and(has[OPPOSITE[side]], lands))(cols[side].wait_recv)
+
+    settle(False)
     start_rows(outer, (0, 3))
-    for copy in own:
-        copy.wait()
-    centre = pltpu.make_async_copy(mid, ext.at[:, :, pl.ds(128, 512), :], mid_sem)
-    centre.start()
     to = lax.broadcasted_iota(jnp.int32, (256, 256), 1)
     source = 2 * (to % 128) + to // 128
     perm = jnp.where(lax.broadcasted_iota(jnp.int32, (256, 256), 0) == source, 1.0, 0.0).astype(BF)
@@ -345,6 +349,11 @@
             high, low = split(picked)
             moduli[s, pl.ds(128 * q, 128), :] = dot(high, perm) + dot(low, perm)
 
+    settle(True)
+    for copy in own:
+        copy.wait()
+    centre = pltpu.make_async_copy(mid, ext.at[:, :, pl.ds(128, 512), :], mid_sem)
+    centre.start()
     n = count[0]
     row_of, col_of = places(offs)
     inside, rank, total = [], [], jnp.int32(0)

time: 111 us -> 110 us (level)
  Pallas kernels: 101 us -> 99.6 us
    pallas_call x1, Pallas kernels: 4.74 us -> 8.22 us  [windows(): pl.pallas_call(window_kernel, out_shape=(jax.ShapeDtypeStruct((2, 6, 768,...]
    pallas_call x1, Pallas kernels: 36.9 us -> 34.5 us  [halo(): pl.pallas_call(halo_kernel, out_shape=(jax.ShapeDtypeStruct((2, 6, 768, 1...]
    pallas_call x1, Pallas kernels: 59.1 us -> 56.9 us  [finish(): pl.pallas_call(finish_kernel, out_shape=(jax.ShapeDtypeStruct((2, 512, 51...]
where the time goes in v10:
time: 110 us
  Pallas kernels  99.6 us (91%)
  local copies, waits for them, and re-layouts  8.16 us (7%)
  between operations  1.33 us (1%)
    pallas_call x1, Pallas kernels, finish(): pl.pallas_call(finish_kernel, out_shape=(jax.ShapeDtypeStruct((2, 512, 51...  56.9 us
    pallas_call x1, Pallas kernels, halo(): pl.pallas_call(halo_kernel, out_shape=(jax.ShapeDtypeStruct((2, 6, 768, 1...  34.5 us
    pallas_call x1, Pallas kernels, windows(): pl.pallas_call(window_kernel, out_shape=(jax.ShapeDtypeStruct((2, 6, 768,...  8.22 us
    unnamed x12, local copies, waits for them, and re-layouts  8.16 us

profile of v10, /device:TPU:1, one launch (start us, length us, event | category | flops | bytes accessed | tf_op | source)
XLA Modules:
  0.0 109.9 jit_solution(1333242451582437714)
XLA Ops:
  1.3 0.1 add_add_fusion
  1.4 0.7 bitcast_subtract_fusion.offs
  2.1 0.0 copy-start
  2.1 1.6 %copy-done = f32[2,512,512]{2,1,0:T(8,128)S(1)} copy-done((f32[2,512,512]{2,1,0:T(8,128)S(1)}, f32[2,512,512]{2,1,0:T(8,128)}, u32[]{:S(2)}) %copy-start) | copy-done | bytes 2097176
  3.7 0.0 copy-start.2
  3.7 1.0 copy-done.2
  4.7 0.0 copy-start.3
  4.7 1.2 %copy-done.3 = bf16[2,2,2,256,256]{4,3,2,1,0:T(8,128)(2,1)S(1)} copy-done((bf16[2,2,2,256,256]{4,3,2,1,0:T(8,128)(2,1)S(1)}, bf16[2,2,2,256,256]{4,3,2,1,0:T(8,128)(2,1)}, u32[]{:S(2)}) %copy-start.3) | copy-done | bytes 1048600
  6.0 0.0 copy-start.4
  6.0 2.2 %copy-done.4 = f32[1,1,16,256,256]{4,3,2,1,0:T(8,128)S(1)} copy-done((f32[1,1,16,256,256]{4,3,2,1,0:T(8,128)S(1)}, f32[1,1,16,256,256]{4,3,2,1,0:T(8,128)}, u32[]{:S(2)}) %copy-start.4) | copy-done | bytes 4194328
  8.2 34.5 %shard_map.77 = (f32[2,6,768,128]{3,2,1,0:T(8,128)S(1)}, f32[16,256,256]{2,1,0:T(8,128)S(1)}, f32[10,2,2,256,128]{4,3,2,1,0:T(8,128)S(1)}, f32[2,2,256,128]{3,2,1,0:T(8,128)S(1)}) custom-call(s32[2,16]{1,0:T(2,128)S(1)} %bitcast_subtract_fusion.offs, s32[1]{0:T(128)} %bitcast.7.count, f32[2,512,512]{2,1,0:T(8,128)S(1)} %copy-done, ...), custom_call_target="tpu_custom_call" | custom-call | flops 20000000000 | bytes 20000000 | tf_op jit(solution)/shard_map/pallas_call | solution.py:427
  42.6 0.0 copy-start.1
  42.6 8.2 %shard_map.78 = (f32[2,6,768,128]{3,2,1,0:T(8,128)S(1)}, f32[2,2,256,128]{3,2,1,0:T(8,128)S(1)}) custom-call(s32[2,16]{1,0:T(2,128)S(1)} %bitcast_subtract_fusion.offs, s32[1]{0:T(128)} %bitcast.8.count, f32[2,6,768,128]{3,2,1,0:T(8,128)S(1)} %get-tuple-element.8.ext, f32[2,256,256]{2,1,0:T(8,128)S(1)} %copy-done.2, ...), custom_call_target="tpu_custom_call" | custom-call | tf_op jit(solution)/shard_map/pallas_call | solution.py:237
  50.9 0.0 copy-done.1
  50.9 56.9 %shard_map.79 = (f32[2,512,512]{2,1,0:T(8,128)S(1)}, f32[2,256,256]{2,1,0:T(8,128)S(1)}) custom-call(f32[2,512,512]{2,1,0:T(8,128)S(1)} %copy-done.1, f32[2,256,256]{2,1,0:T(8,128)S(1)} %copy-done.2, f32[2,6,768,128]{3,2,1,0:T(8,128)S(1)} %get-tuple-element.12.grad, f32[2,4,16,8,128]{4,3,2,1,0:T(8,128)S(1)} %bitcast.9), custom_call_target="tpu_custom_call" | custom-call | tf_op jit(solution)/shard_map/pallas_call | solution.py:597
  107.8 1.3 %copy.11 = f32[2,512,512]{2,1,0:T(8,128)} copy(f32[2,512,512]{2,1,0:T(8,128)S(1)} %get-tuple-element.16) | data formatting | bytes 4194304
  109.1 0.8 copy.12
Async XLA Ops:
  2.1 1.6 %copy-start = (f32[2,512,512]{2,1,0:T(8,128)S(1)}, f32[2,512,512]{2,1,0:T(8,128)}, u32[]{:S(2)}) copy-start(f32[2,512,512]{2,1,0:T(8,128)} %spec.1) | copy-start | bytes 6291460
  3.7 1.0 copy-start.2
  4.7 1.2 %copy-start.3 = (bf16[2,2,2,256,256]{4,3,2,1,0:T(8,128)(2,1)S(1)}, bf16[2,2,2,256,256]{4,3,2,1,0:T(8,128)(2,1)}, u32[]{:S(2)}) copy-start(bf16[2,2,2,256,256]{4,3,2,1,0:T(8,128)(2,1)} %constant.14.clone.mats) | copy-start | bytes 3145732
  6.0 2.2 %copy-start.4 = (f32[1,1,16,256,256]{4,3,2,1,0:T(8,128)S(1)}, f32[1,1,16,256,256]{4,3,2,1,0:T(8,128)}, u32[]{:S(2)}) copy-start(f32[1,1,16,256,256]{4,3,2,1,0:T(8,128)} %param.10) | copy-start | bytes 12582916
  42.6 8.2 %copy-start.1 = (f32[2,512,512]{2,1,0:T(8,128)S(1)}, f32[2,512,512]{2,1,0:T(8,128)}, u32[]{:S(2)}) copy-start(f32[2,512,512]{2,1,0:T(8,128)} %spec.1) | copy-start | bytes 6291460

commit v11 on v10

--- a/solution.py
+++ b/solution.py
@@ -10,7 +10,7 @@
 F32 = jnp.float32
 BF = jnp.bfloat16
 MESH = pl.DeviceIdType.MESH
-NEAR = 10
+NEAR = 8
 
 
 def consts():

time: 110 us -> 111 us (level); the launches traced: 110 us -> 110 us
    pallas_call x1, Pallas kernels: 8.22 us -> 4.78 us  [windows(): pl.pallas_call(window_kernel, out_shape=(jax.ShapeDtypeStruct((2, 6, 768,...]
    pallas_call x1, Pallas kernels: 56.9 us -> 60.1 us  [finish(): pl.pallas_call(finish_kernel, out_shape=(jax.ShapeDtypeStruct((2, 512, 51...]
where the time goes in v11:
time: 111 us; the launch traced here: 110 us
  Pallas kernels  99.3 us (89%)
  local copies, waits for them, and re-layouts  8.16 us (7%)
  between operations  1.33 us (1%)
    pallas_call x1, Pallas kernels, finish(): pl.pallas_call(finish_kernel, out_shape=(jax.ShapeDtypeStruct((2, 512, 51...  60.1 us
    pallas_call x1, Pallas kernels, halo(): pl.pallas_call(halo_kernel, out_shape=(jax.ShapeDtypeStruct((2, 6, 768, 1...  34.4 us
    unnamed x12, local copies, waits for them, and re-layouts  8.16 us
    pallas_call x1, Pallas kernels, windows(): pl.pallas_call(window_kernel, out_shape=(jax.ShapeDtypeStruct((2, 6, 768,...  4.78 us

profile of v11, /device:TPU:1, one launch (start us, length us, event | category | flops | bytes accessed | tf_op | source)
XLA Modules:
  0.0 109.6 jit_solution(7637674270183898069)
XLA Ops:
  1.3 0.1 add_add_fusion
  1.4 0.7 bitcast_subtract_fusion.offs
  2.1 0.0 copy-start
  2.1 1.6 %copy-done = f32[2,512,512]{2,1,0:T(8,128)S(1)} copy-done((f32[2,512,512]{2,1,0:T(8,128)S(1)}, f32[2,512,512]{2,1,0:T(8,128)}, u32[]{:S(2)}) %copy-start) | copy-done | bytes 2097176
  3.7 0.0 copy-start.2
  3.7 1.0 copy-done.2
  4.7 0.0 copy-start.3
  4.7 1.2 %copy-done.3 = bf16[2,2,2,256,256]{4,3,2,1,0:T(8,128)(2,1)S(1)} copy-done((bf16[2,2,2,256,256]{4,3,2,1,0:T(8,128)(2,1)S(1)}, bf16[2,2,2,256,256]{4,3,2,1,0:T(8,128)(2,1)}, u32[]{:S(2)}) %copy-start.3) | copy-done | bytes 1048600
  6.0 0.0 copy-start.4
  6.0 2.2 %copy-done.4 = f32[1,1,16,256,256]{4,3,2,1,0:T(8,128)S(1)} copy-done((f32[1,1,16,256,256]{4,3,2,1,0:T(8,128)S(1)}, f32[1,1,16,256,256]{4,3,2,1,0:T(8,128)}, u32[]{:S(2)}) %copy-start.4) | copy-done | bytes 4194328
  8.2 34.4 %shard_map.77 = (f32[2,6,768,128]{3,2,1,0:T(8,128)S(1)}, f32[16,256,256]{2,1,0:T(8,128)S(1)}, f32[8,2,2,256,128]{4,3,2,1,0:T(8,128)S(1)}, f32[2,2,256,128]{3,2,1,0:T(8,128)S(1)}) custom-call(s32[2,16]{1,0:T(2,128)S(1)} %bitcast_subtract_fusion.offs, s32[1]{0:T(128)} %bitcast.7.count, f32[2,512,512]{2,1,0:T(8,128)S(1)} %copy-done, ...), custom_call_target="tpu_custom_call" | custom-call | flops 20000000000 | bytes 20000000 | tf_op jit(solution)/shard_map/pallas_call | solution.py:427
  42.6 0.0 copy-start.1
  42.6 4.8 %shard_map.78 = (f32[2,6,768,128]{3,2,1,0:T(8,128)S(1)}, f32[2,2,256,128]{3,2,1,0:T(8,128)S(1)}) custom-call(s32[2,16]{1,0:T(2,128)S(1)} %bitcast_subtract_fusion.offs, s32[1]{0:T(128)} %bitcast.8.count, f32[2,6,768,128]{3,2,1,0:T(8,128)S(1)} %get-tuple-element.8.ext, f32[2,256,256]{2,1,0:T(8,128)S(1)} %copy-done.2, ...), custom_call_target="tpu_custom_call" | custom-call | tf_op jit(solution)/shard_map/pallas_call | solution.py:237
  47.4 0.0 copy-done.1
  47.4 60.1 %shard_map.79 = (f32[2,512,512]{2,1,0:T(8,128)S(1)}, f32[2,256,256]{2,1,0:T(8,128)S(1)}) custom-call(f32[2,512,512]{2,1,0:T(8,128)S(1)} %copy-done.1, f32[2,256,256]{2,1,0:T(8,128)S(1)} %copy-done.2, f32[2,6,768,128]{3,2,1,0:T(8,128)S(1)} %get-tuple-element.12.grad, f32[2,4,16,8,128]{4,3,2,1,0:T(8,128)S(1)} %bitcast.9), custom_call_target="tpu_custom_call" | custom-call | tf_op jit(solution)/shard_map/pallas_call | solution.py:597
  107.5 1.3 %copy.11 = f32[2,512,512]{2,1,0:T(8,128)} copy(f32[2,512,512]{2,1,0:T(8,128)S(1)} %get-tuple-element.16) | data formatting | bytes 4194304
  108.8 0.8 copy.12
Async XLA Ops:
  2.1 1.6 %copy-start = (f32[2,512,512]{2,1,0:T(8,128)S(1)}, f32[2,512,512]{2,1,0:T(8,128)}, u32[]{:S(2)}) copy-start(f32[2,512,512]{2,1,0:T(8,128)} %spec.1) | copy-start | bytes 6291460
  3.7 1.0 copy-start.2
  4.7 1.2 %copy-start.3 = (bf16[2,2,2,256,256]{4,3,2,1,0:T(8,128)(2,1)S(1)}, bf16[2,2,2,256,256]{4,3,2,1,0:T(8,128)(2,1)}, u32[]{:S(2)}) copy-start(bf16[2,2,2,256,256]{4,3,2,1,0:T(8,128)(2,1)} %constant.14.clone.mats) | copy-start | bytes 3145732
  6.0 2.2 %copy-start.4 = (f32[1,1,16,256,256]{4,3,2,1,0:T(8,128)S(1)}, f32[1,1,16,256,256]{4,3,2,1,0:T(8,128)}, u32[]{:S(2)}) copy-start(f32[1,1,16,256,256]{4,3,2,1,0:T(8,128)} %param.10) | copy-start | bytes 12582916
  42.6 4.8 %copy-start.1 = (f32[2,512,512]{2,1,0:T(8,128)S(1)}, f32[2,512,512]{2,1,0:T(8,128)}, u32[]{:S(2)}) copy-start(f32[2,512,512]{2,1,0:T(8,128)} %spec.1) | copy-start | bytes 6291460
